TPU v7x, 32 devices: a whole 2x2x4 slice. The times are simulated.
32 devices in a mesh: gz: 8 (over y, x, core), xy: 4 (over z).
Axes of the slice: x: 2, y: 2, z: 4, core: 2. Of those that a mesh axis runs over, the one named last changes fastest.
Arguments:
- prior_estimate: float32 [384, 128, 128], P('gz', 'xy'), may hold values from 0.5 to 2
- views_upright: float32 [3, 384, 128, 128], P(None, 'gz', 'xy'), may hold values from 0.2 to 5
- views_turned: float32 [3, 384, 128, 128], P(None, 'gz', 'xy'), may hold values from 0.2 to 5
- kernel_depth: float32 [6, 61], replicated, may hold values from 0.005 to 1.55, as said below
- kernel_rows: float32 [6, 31], replicated, may hold values from 0.005 to 1.55, as said below
- kernel_columns: float32 [6, 31], replicated, may hold values from 0.005 to 1.55, as said below
- lateral_offsets: int32 [6], replicated, may hold values from -8 to 8, as said below
- block_views: int32 [32, 3], replicated, may hold values from 0 to 5, all different within a row
Outputs:
- estimate: float32 [384, 128, 128], P('gz', 'xy')
Inputs may be any that keep to these rules, and one draw needn't show every extreme that they name: `block_views`: row r holds 3 different views and belongs to the block at position r // 4 along gz and r % 4 along xy. `lateral_offsets`: one view has offset 8 and another -8. `kernel_depth`: positive taps. `kernel_rows`: positive taps. `kernel_columns`: positive taps.
All inputs are finite; a program needn't handle non-finite values.
Results may differ from a plain program's by a relative error of at most 0.00005.
Values sent between devices are 32-bit elements; how exact they have to be, the bound alone decides.
No kernel may reach another device: no remote copies, remote signals or barrier semaphores. Data moves between devices by JAX's collectives and lax.ppermute only.
A program may use at most 128 MiB of HBM per device.

v0:
```python
import jax
import jax.numpy as jnp
from jax import lax
from jax.sharding import PartitionSpec as P

ITERS = 2


exact_mode = lax.Precision.HIGHEST


def padded(cells, sides, width):
    for axis, dim in sides:
        count = lax.axis_size(axis)
        ends = count - 1
        head = lax.slice_in_dim(cells, 0, width, axis=dim)
        tail = lax.slice_in_dim(cells, cells.shape[dim] - width, cells.shape[dim], axis=dim)
        cells = jnp.concatenate(
            [
                lax.ppermute(tail, axis, [(i, (i + 1) % count) for i in range(ends)]),
                cells,
                lax.ppermute(head, axis, [((i + 1) % count, i) for i in range(ends)]),
            ],
            axis=dim,
        )
    return cells


def passed_along(value, axis, steps):
    count = lax.axis_size(axis)
    leading, last = (max(0, -steps), min(count, count - steps))
    return lax.ppermute(value, axis, [(source, source + steps) for source in range(leading, last)])


def band_matrix(kernel, length):
    extent = kernel.shape[0]
    row_index = jnp.arange(length, dtype=jnp.int32)[:, None]
    col_index = jnp.arange(length + extent - 1, dtype=jnp.int32)[None, :]
    offset = col_index - row_index
    choose = (offset[:, :, None] == jnp.arange(extent, dtype=jnp.int32)[None, None, :]).astype(
        jnp.float32
    )
    return jnp.sum(choose * kernel[None, None, :], axis=2)


def lateral_matrix(kernel, displacement, length):
    extent = kernel.shape[0]
    radius = (extent - 1) // 2
    row_index = jnp.arange(length, dtype=jnp.int32)[:, None]
    col_index = jnp.arange(length, dtype=jnp.int32)[None, :]
    offset = col_index - row_index + radius + displacement
    choose = (offset[:, :, None] == jnp.arange(extent, dtype=jnp.int32)[None, None, :]).astype(
        jnp.float32
    )
    return jnp.sum(choose * kernel[None, None, :], axis=2)


def normalize(kernel):
    return kernel / jnp.sum(kernel, axis=-1, keepdims=True)


def blur_forward(haloed, band_depth, band_rows, lateral):
    section = jnp.einsum("zj,jyx->zyx", band_depth, haloed, precision=exact_mode)
    section = jnp.einsum("yj,zjx->zyx", band_rows, section, precision=exact_mode)
    return jnp.einsum("zyj,xj->zyx", section, lateral, precision=exact_mode)


def region_onehot(length, reach, inner):
    places = jnp.arange(length, dtype=jnp.int32)
    region = (places >= reach).astype(jnp.int32) + (places >= reach + inner).astype(jnp.int32)
    return (region[:, None] == jnp.arange(3, dtype=jnp.int32)[None, :]).astype(jnp.float32)


def local(
    prior_estimate,
    views_upright,
    views_turned,
    kernel_depth,
    kernel_rows,
    kernel_columns,
    lateral_offsets,
    block_views,
):
    depth, rows, columns = prior_estimate.shape
    count_views = kernel_depth.shape[0]
    count_blocks = block_views.shape[0]
    count_active = block_views.shape[1]
    reach_depth = (kernel_depth.shape[1] - 1) // 2
    reach_rows = (kernel_rows.shape[1] - 1) // 2
    turned = jnp.transpose(
        lax.all_to_all(views_turned, "xy", split_axis=3, concat_axis=2, tiled=True), (0, 1, 3, 2)
    )
    observed = jnp.concatenate([views_upright, turned], axis=0)
    taps_depth = normalize(kernel_depth)
    taps_rows = normalize(kernel_rows)
    taps_columns = normalize(kernel_columns)
    forward_depth = [band_matrix(taps_depth[number], depth) for number in range(count_views)]
    forward_rows = [band_matrix(taps_rows[number], rows) for number in range(count_views)]
    laterals = [
        lateral_matrix(taps_columns[number], lateral_offsets[number], columns)
        for number in range(count_views)
    ]
    member = (
        jnp.sum(
            (
                block_views[:, :, None] == jnp.arange(count_views, dtype=jnp.int32)[None, None, :]
            ).astype(jnp.float32),
            axis=1,
        )
        / count_active
    )
    side_count = lax.axis_size("xy")
    depth_count = lax.axis_size("gz")
    here_depth = lax.axis_index("gz")
    here_rows = lax.axis_index("xy")
    block_list = jnp.arange(count_blocks, dtype=jnp.int32)
    neighbours = jnp.arange(3, dtype=jnp.int32) - 1
    near_depth = jnp.clip(here_depth + neighbours, 0, depth_count - 1)
    near_rows = jnp.clip(here_rows + neighbours, 0, side_count - 1)
    near_ids = near_depth[:, None] * side_count + near_rows[None, :]
    picker = (near_ids[:, :, None] == block_list[None, None, :]).astype(jnp.float32)
    near_weights = jnp.einsum("abn,nv->abv", picker, member, precision=exact_mode)
    onehot_depth = region_onehot(depth + 2 * reach_depth, reach_depth, depth)
    onehot_rows = region_onehot(rows + 2 * reach_rows, reach_rows, rows)
    weight_fields = jnp.einsum(
        "za,abv,yb->vzy", onehot_depth, near_weights, onehot_rows, precision=exact_mode
    )
    estimate = prior_estimate
    for iteration in range(ITERS):
        haloed = padded(estimate, (("xy", 1),), reach_rows)
        haloed = padded(haloed, (("gz", 0),), reach_depth)
        accumulated = jnp.zeros(
            (depth + 2 * reach_depth, rows + 2 * reach_rows, columns), jnp.float32
        )
        for number in range(count_views):
            blurred = blur_forward(
                haloed, forward_depth[number], forward_rows[number], laterals[number]
            )
            quotient = observed[number] / blurred
            spread = jnp.einsum("zyj,jx->zyx", quotient, laterals[number], precision=exact_mode)
            spread = jnp.einsum("je,zjx->zex", forward_rows[number], spread, precision=exact_mode)
            spread = jnp.einsum("je,jyx->eyx", forward_depth[number], spread, precision=exact_mode)
            accumulated = accumulated + weight_fields[number][:, :, None] * spread
        lower = accumulated[:reach_depth]
        upper = accumulated[reach_depth + depth :]
        middle = accumulated[reach_depth : reach_depth + depth]
        from_below = passed_along(upper, "gz", 1)
        from_above = passed_along(lower, "gz", -1)
        middle = middle + jnp.pad(from_below, ((0, depth - reach_depth), (0, 0), (0, 0)))
        middle = middle + jnp.pad(from_above, ((depth - reach_depth, 0), (0, 0), (0, 0)))
        left_rim = middle[:, :reach_rows]
        right_rim = middle[:, reach_rows + rows :]
        centre = middle[:, reach_rows : reach_rows + rows]
        from_left = passed_along(right_rim, "xy", 1)
        from_right = passed_along(left_rim, "xy", -1)
        centre = centre + jnp.pad(from_left, ((0, 0), (0, rows - reach_rows), (0, 0)))
        correction = centre + jnp.pad(from_right, ((0, 0), (rows - reach_rows, 0), (0, 0)))
        estimate = estimate * correction
    return estimate


def solution(mesh):
    in_specs = (
        P("gz", "xy", None),
        P(None, "gz", "xy", None),
        P(None, "gz", "xy", None),
        P(),
        P(),
        P(),
        P(),
        P(),
    )
    out_specs = P("gz", "xy", None)
    return jax.shard_map(local, mesh=mesh, in_specs=in_specs, out_specs=out_specs, check_vma=False)
```

profile of v0, /device:TPU:1, one launch (start us, length us, event | category | flops | bytes accessed | tf_op | source)
XLA Modules:
  0.0 371.8 jit_solution(13855618108526861795)
XLA Ops:
  1.5 4.8 %collective-permute-start = (f32[48,15,128]{2,0,1:T(8,128)S(1)}, f32[48,15,128]{2,0,1:T(8,128)}, u32[]{:S(2)}, u32[]{:S(2)}) collective-permute-start(f32[48,15,128]{2,0,1:T(8,128)S(1)} %copy.240), channel_id=1, source_target_pairs={{0,1},{1,2},{2,3},{4,5},{5,6},{6,7},{8,9},{9,10},{10,11},{12,13},{... | collective-permute-start | bytes 1105928 | tf_op jit(solution)/shard_map/ppermute | solution.py:20
  7.7 6.2 %copy.129 = f32[3,48,32,128]{1,2,0,3:T(8,128)} copy(f32[3,48,32,128]{3,2,1,0:T(8,128)S(1)} %copy-done.4) | data formatting | bytes 4718592 | tf_op args[2]
  13.9 8.3 %reshape.196 = f32[4,1,147456]{2,1,0:T(1,128)} reshape(f32[128,3,32,48]{3,2,1,0:T(8,128)} %bitcast.349) | data formatting | bytes 4718592
  22.2 4.8 %all-to-all-start = ((f32[4,1,147456]{2,1,0:T(1,128)}), f32[4,1,147456]{2,1,0:T(1,128)}, u32[]{:S(2)}, u32[]{:S(2)}) async-start(f32[4,1,147456]{2,1,0:T(1,128)} %reshape.196), calls=%async_computation | async-start | bytes 4718592 | tf_op jit(solution)/shard_map/all_to_all | solution.py:91
  38.0 4.5 %collective-permute-start.2 = (f32[30,62,128]{2,1,0:T(8,128)S(1)}, f32[30,62,128]{2,1,0:T(8,128)S(1)}, u32[]{:S(2)}, u32[]{:S(2)}) collective-permute-start(f32[30,62,128]{2,1,0:T(8,128)S(1)} %copy.119), channel_id=1, source_target_pairs={{0,4},{4,8},{8,12},{12,16},{16,20},{20,24},{24,28},{1,5},{5,9},{9,... | collective-permute-start | bytes 2856968 | tf_op jit(solution)/shard_map/ppermute | solution.py:20
  43.1 2.1 collective-permute-start.3
  47.8 5.8 %collective-permute-done.2 = f32[30,62,128]{2,1,0:T(8,128)S(1)} collective-permute-done((f32[30,62,128]{2,1,0:T(8,128)S(1)}, f32[30,62,128]{2,1,0:T(8,128)S(1)}, u32[]{:S(2)}, u32[]{:S(2)}) %collective-permute-start.2) | collective-permute-done | bytes 952352 | tf_op jit(solution)/shard_map/ppermute | solution.py:20
  54.1 11.6 %collective-permute-done.3 = f32[30,62,128]{2,1,0:T(8,128)S(1)} collective-permute-done((f32[30,62,128]{2,1,0:T(8,128)S(1)}, f32[30,62,128]{2,1,0:T(8,128)S(1)}, u32[]{:S(2)}, u32[]{:S(2)}) %collective-permute-start.3) | collective-permute-done | bytes 952352 | tf_op jit(solution)/shard_map/ppermute | solution.py:22
  66.3 2.3 fusion.146
  68.6 2.3 fusion.140
  70.9 2.3 fusion.152
  76.7 2.3 fusion.158
  82.1 2.3 fusion.164
  85.9 2.3 fusion.134
  94.5 2.4 fusion.57
  96.9 2.4 fusion.60
  99.3 2.4 fusion.63
  101.8 3.8 %fusion.42 = f32[108,62,128]{2,0,1:T(8,128)S(1)} fusion(f32[48,62,128]{2,1,0:T(8,128)S(1)} %convolution_bitcast_fusion.9, f32[48,108]{1,0:T(8,128)S(1)} %get-tuple-element.8), kind=kOutput, calls=%fused_computation.61 | convolution fusion | flops 493682688 | bytes 4972800 | tf_op jit(solution)/shard_map/je,jyx->eyx/dot_general | solution.py:142
  105.6 5.4 %fusion.44 = f32[108,62,128]{2,0,1:T(8,128)} fusion(f32[48,62,128]{2,1,0:T(8,128)S(1)} %convolution_bitcast_fusion.10, f32[48,108]{1,0:T(8,128)S(1)} %get-tuple-element.9), kind=kOutput, calls=%fused_computation.63 | convolution fusion | flops 493682688 | bytes 4972800 | tf_op jit(solution)/shard_map/je,jyx->eyx/dot_general | solution.py:142
  110.9 5.4 %fusion.46 = f32[108,62,128]{2,0,1:T(8,128)} fusion(f32[48,62,128]{2,1,0:T(8,128)S(1)} %convolution_bitcast_fusion.11, f32[48,108]{1,0:T(8,128)S(1)} %get-tuple-element.10), kind=kOutput, calls=%fused_computation.65 | convolution fusion | flops 493682688 | bytes 4972800 | tf_op jit(solution)/shard_map/je,jyx->eyx/dot_general | solution.py:142
  116.9 9.7 %reduce = f32[4,147456]{1,0:T(4,128)} reduce(f32[4,1,147456]{2,1,0:T(1,128)} %all-to-all-done, f32[]{:T(128)} %broadcast.242), dimensions={1}, to_apply=%all_to_all.13.reduce_sub_computation | reduce | bytes 4718596 | tf_op jit(solution)/shard_map/all_to_all | solution.py:91
  126.6 7.2 %reshape.197 = f32[128,3,32,48]{3,2,1,0:T(8,128)} reshape(f32[4,147456]{1,0:T(4,128)} %reduce) | data formatting | bytes 4718592
  133.8 9.7 %copy.131 = f32[3,48,4,32,32]{1,4,3,2,0:T(8,128)} copy(f32[3,48,4,32,32]{1,3,0,4,2:T(8,128)} %bitcast.347) | data formatting | bytes 4718592 | tf_op jit(solution)/shard_map/all_to_all | solution.py:91
  143.5 7.3 %copy.132 = f32[3,48,128,32]{2,3,1,0:T(8,128)} copy(f32[3,48,128,32]{1,3,2,0:T(8,128)} %bitcast.348) | data formatting | bytes 4718592 | tf_op jit(solution)/shard_map/all_to_all | solution.py:91
  150.8 2.2 convolution_divide_fusion.8
  155.3 3.7 fusion.40
  162.1 3.9 %fusion.38 = f32[108,62,128]{2,0,1:T(8,128)S(1)} fusion(f32[48,62,128]{2,1,0:T(8,128)S(1)} %convolution_bitcast_fusion.7, f32[48,108]{1,0:T(8,128)S(1)} %copy-done.30), kind=kOutput, calls=%fused_computation.57 | convolution fusion | flops 493682688 | bytes 4972800 | tf_op jit(solution)/shard_map/je,jyx->eyx/dot_general | solution.py:142
  169.3 11.8 %multiply_add_fusion.1 = f32[108,62,128]{2,0,1:T(8,128)S(1)} fusion(f32[108,62,128]{2,0,1:T(8,128)S(1)} %fusion.38, f32[108,62,128]{2,0,1:T(8,128)S(1)} %fusion.40, f32[108,62,128]{2,0,1:T(8,128)S(1)} %fusion.42, f32[108,62,128]{2,0,1:T(8,128)S(1)} %copy-done, f32[108,62,128]{2,0,1:T(8,128)S(1)} %copy-done.1, f32[108,62]{0,1:T(8,128)S(1)} %copy-done.42, ...), kind=kOutput, calls=%fused_computation.3 | convolution fusion | flops 503110656 | bytes 22275264 | tf_op jit(solution)/shard_map/je,jyx->eyx/dot_general | solution.py:142
  181.9 1.9 collective-permute-start.4
  184.4 2.5 collective-permute-start.5
  186.9 8.0 %collective-permute-done.4 = f32[30,62,128]{2,1,0:T(8,128)S(1)} collective-permute-done((f32[30,62,128]{2,1,0:T(8,128)S(1)}, f32[30,62,128]{2,1,0:T(8,128)S(1)}, u32[]{:S(2)}, u32[]{:S(2)}) %collective-permute-start.4) | collective-permute-done | bytes 952352 | tf_op jit(solution)/shard_map/ppermute | solution.py:32
  195.4 11.6 %collective-permute-done.5 = f32[30,62,128]{2,1,0:T(8,128)S(1)} collective-permute-done((f32[30,62,128]{2,1,0:T(8,128)S(1)}, f32[30,62,128]{2,1,0:T(8,128)S(1)}, u32[]{:S(2)}, u32[]{:S(2)}) %collective-permute-start.5) | collective-permute-done | bytes 952352 | tf_op jit(solution)/shard_map/ppermute | solution.py:32
  208.0 4.1 %collective-permute-start.6 = (f32[48,15,128]{2,0,1:T(8,128)S(1)}, f32[48,15,128]{2,0,1:T(8,128)S(1)}, u32[]{:S(2)}, u32[]{:S(2)}) collective-permute-start(f32[48,15,128]{2,0,1:T(8,128)S(1)} %get-tuple-element.25), channel_id=1, source_target_pairs={{0,1},{1,2},{2,3},{4,5},{5,6},{6,7},{8,9},{9,10},{10,11},{12,13},{... | collective-permute-start | bytes 1105928 | tf_op jit(solution)/shard_map/ppermute | solution.py:32
  213.3 3.3 collective-permute-done.6
  216.6 4.1 %collective-permute-done.7 = f32[48,15,128]{2,0,1:T(8,128)S(1)} collective-permute-done((f32[48,15,128]{2,0,1:T(8,128)S(1)}, f32[48,15,128]{2,0,1:T(8,128)S(1)}, u32[]{:S(2)}, u32[]{:S(2)}) %collective-permute-start.7) | collective-permute-done | bytes 368672 | tf_op jit(solution)/shard_map/ppermute | solution.py:32
  221.3 2.7 collective-permute-start.8
  225.3 3.1 collective-permute-done.8
  228.4 3.8 %collective-permute-done.9 = f32[48,15,128]{2,0,1:T(8,128)S(1)} collective-permute-done((f32[48,15,128]{2,0,1:T(8,128)S(1)}, f32[48,15,128]{2,0,1:T(8,128)S(1)}, u32[]{:S(2)}, u32[]{:S(2)}) %collective-permute-start.9) | collective-permute-done | bytes 368672 | tf_op jit(solution)/shard_map/ppermute | solution.py:22
  233.2 5.8 %collective-permute-start.10 = (f32[30,62,128]{2,1,0:T(8,128)S(1)}, f32[30,62,128]{2,1,0:T(8,128)S(1)}, u32[]{:S(2)}, u32[]{:S(2)}) collective-permute-start(f32[30,62,128]{2,1,0:T(8,128)S(1)} %copy.144), channel_id=1, source_target_pairs={{0,4},{4,8},{8,12},{12,16},{16,20},{20,24},{24,28},{1,5},{5,9},{9,... | collective-permute-start | bytes 2856968 | tf_op jit(solution)/shard_map/ppermute | solution.py:20
  239.6 2.1 collective-permute-start.11
  241.8 8.3 %collective-permute-done.10 = f32[30,62,128]{2,1,0:T(8,128)S(1)} collective-permute-done((f32[30,62,128]{2,1,0:T(8,128)S(1)}, f32[30,62,128]{2,1,0:T(8,128)S(1)}, u32[]{:S(2)}, u32[]{:S(2)}) %collective-permute-start.10) | collective-permute-done | bytes 952352 | tf_op jit(solution)/shard_map/ppermute | solution.py:20
  250.7 10.2 %collective-permute-done.11 = f32[30,62,128]{2,1,0:T(8,128)S(1)} collective-permute-done((f32[30,62,128]{2,1,0:T(8,128)S(1)}, f32[30,62,128]{2,1,0:T(8,128)S(1)}, u32[]{:S(2)}, u32[]{:S(2)}) %collective-permute-start.11) | collective-permute-done | bytes 952352 | tf_op jit(solution)/shard_map/ppermute | solution.py:22
  261.4 2.3 fusion.131
  263.7 1.5 fusion.81
  268.3 2.3 fusion.161
  275.6 3.7 fusion.35
  279.3 2.3 fusion.155
  281.6 1.5 fusion.69
  286.2 3.9 %fusion.33 = f32[108,62,128]{2,0,1:T(8,128)S(1)} fusion(f32[48,62,128]{2,1,0:T(8,128)S(1)} %convolution_bitcast_fusion.4, f32[48,108]{1,0:T(8,128)S(1)} %copy-done.36), kind=kOutput, calls=%fused_computation.52 | convolution fusion | flops 493682688 | bytes 4972800 | tf_op jit(solution)/shard_map/je,jyx->eyx/dot_general | solution.py:142
  290.1 2.3 fusion.149
  296.9 4.1 %fusion.31 = f32[108,62,128]{2,0,1:T(8,128)S(1)} fusion(f32[48,62,128]{2,1,0:T(8,128)S(1)} %convolution_bitcast_fusion.3, f32[48,108]{1,0:T(8,128)S(1)} %copy-done.34), kind=kOutput, calls=%fused_computation.50 | convolution fusion | flops 493682688 | bytes 4972800 | tf_op jit(solution)/shard_map/je,jyx->eyx/dot_general | solution.py:142
  301.1 2.3 fusion.143
  303.3 1.5 fusion.75
  307.9 3.7 fusion.29
  311.6 2.4 fusion.137
  318.6 3.7 fusion.27
  322.3 11.9 %multiply_add_fusion = f32[108,62,128]{2,0,1:T(8,128)S(1)} fusion(f32[108,62,128]{2,0,1:T(8,128)S(1)} %fusion.27, f32[108,62,128]{2,0,1:T(8,128)S(1)} %fusion.29, f32[108,62,128]{2,0,1:T(8,128)S(1)} %fusion.31, f32[108,62,128]{2,0,1:T(8,128)S(1)} %fusion.33, f32[108,62,128]{2,0,1:T(8,128)S(1)} %fusion.35, f32[108,62]{0,1:T(8,128)S(1)} %copy-done.42, ...), kind=kOutput, calls=%fused_computation.2 | convolution fusion | flops 503110656 | bytes 22275264 | tf_op jit(solution)/shard_map/je,jyx->eyx/dot_general | solution.py:142
  335.1 1.9 collective-permute-start.12
  337.6 2.5 collective-permute-start.13
  340.0 8.0 %collective-permute-done.12 = f32[30,62,128]{2,1,0:T(8,128)S(1)} collective-permute-done((f32[30,62,128]{2,1,0:T(8,128)S(1)}, f32[30,62,128]{2,1,0:T(8,128)S(1)}, u32[]{:S(2)}, u32[]{:S(2)}) %collective-permute-start.12) | collective-permute-done | bytes 952352 | tf_op jit(solution)/shard_map/ppermute | solution.py:32
  348.6 9.2 %collective-permute-done.13 = f32[30,62,128]{2,1,0:T(8,128)S(1)} collective-permute-done((f32[30,62,128]{2,1,0:T(8,128)S(1)}, f32[30,62,128]{2,1,0:T(8,128)S(1)}, u32[]{:S(2)}, u32[]{:S(2)}) %collective-permute-start.13) | collective-permute-done | bytes 952352 | tf_op jit(solution)/shard_map/ppermute | solution.py:32
  358.7 3.4 collective-permute-start.14
  363.4 3.1 collective-permute-done.14
  366.5 3.8 %collective-permute-done.15 = f32[48,15,128]{2,0,1:T(8,128)S(1)} collective-permute-done((f32[48,15,128]{2,0,1:T(8,128)S(1)}, f32[48,15,128]{2,0,1:T(8,128)S(1)}, u32[]{:S(2)}, u32[]{:S(2)}) %collective-permute-start.15) | collective-permute-done | bytes 368672 | tf_op jit(solution)/shard_map/ppermute | solution.py:32
  (225 shorter events, 78.1 us)
Async XLA Ops:
  0.0 7.7 %copy-start.4 = (f32[3,48,32,128]{3,2,1,0:T(8,128)S(1)}, f32[3,48,32,128]{3,2,1,0:T(8,128)}, u32[]{:S(2)}) copy-start(f32[3,48,32,128]{3,2,1,0:T(8,128)} %param.10) | copy-start | bytes 7077892
  1.5 34.1 %collective-permute-start = (f32[48,15,128]{2,0,1:T(8,128)S(1)}, f32[48,15,128]{2,0,1:T(8,128)}, u32[]{:S(2)}, u32[]{:S(2)}) collective-permute-start(f32[48,15,128]{2,0,1:T(8,128)S(1)} %copy.240), channel_id=1, source_target_pairs={{0,1},{1,2},{2,3},{4,5},{5,6},{6,7},{8,9},{9,10},{10,11},{12,13},{... | collective-permute-start | bytes 1105928 | tf_op jit(solution)/shard_map/ppermute | solution.py:20
  6.4 30.7 %collective-permute-start.1 = (f32[48,15,128]{2,0,1:T(8,128)S(1)}, f32[48,15,128]{2,0,1:T(8,128)S(1)}, u32[]{:S(2)}, u32[]{:S(2)}) collective-permute-start(f32[48,15,128]{2,0,1:T(8,128)S(1)} %copy.241), channel_id=1, source_target_pairs={{1,0},{2,1},{3,2},{5,4},{6,5},{7,6},{9,8},{10,9},{11,10},{13,12},{... | collective-permute-start | bytes 1105928 | tf_op jit(solution)/shard_map/ppermute | solution.py:22
  22.2 4.9 %copy-start.48 = (f32[6,61]{1,0:T(8,128)S(1)}, f32[6,61]{1,0:T(8,128)}, u32[]{:S(2)}) copy-start(f32[6,61]{1,0:T(8,128)} %param.11) | copy-start | bytes 4396
  22.2 5.1 %copy-start.49 = (f32[6,31]{1,0:T(8,128)S(1)}, f32[6,31]{1,0:T(8,128)}, u32[]{:S(2)}) copy-start(f32[6,31]{1,0:T(8,128)} %param.12) | copy-start | bytes 2236
  22.2 5.3 %copy-start.47 = (s32[6]{0:T(128)S(1)}, s32[6]{0:T(128)}, u32[]{:S(2)}) copy-start(s32[6]{0:T(128)} %param.14) | copy-start | bytes 76
  22.2 7.4 %copy-start.50 = (f32[6,31]{1,0:T(8,128)S(1)}, f32[6,31]{1,0:T(8,128)}, u32[]{:S(2)}) copy-start(f32[6,31]{1,0:T(8,128)} %param.13) | copy-start | bytes 2236
  22.2 10.1 %copy-start.51 = (s32[32,3]{0,1:T(4,128)S(1)}, s32[32,3]{0,1:T(4,128)}, u32[]{:S(2)}) copy-start(s32[32,3]{0,1:T(4,128)} %param.15) | copy-start | bytes 1156
  22.2 94.1 %all-to-all-start = ((f32[4,1,147456]{2,1,0:T(1,128)}), f32[4,1,147456]{2,1,0:T(1,128)}, u32[]{:S(2)}, u32[]{:S(2)}) async-start(f32[4,1,147456]{2,1,0:T(1,128)} %reshape.196), calls=%async_computation | async-start | bytes 4718592 | tf_op jit(solution)/shard_map/all_to_all | solution.py:91
  27.0 9.6 %copy-start.2 = (f32[48,32,128]{2,1,0:T(8,128)S(1)}, f32[48,32,128]{2,1,0:T(8,128)}, u32[]{:S(2)}) copy-start(f32[48,32,128]{2,1,0:T(8,128)} %param.8) | copy-start | bytes 2359300
  33.9 41.8 %copy-start.10 = (f32[128,128]{1,0:T(8,128)}, f32[128,128]{1,0:T(8,128)S(1)}, u32[]{:S(2)}) copy-start(f32[128,128]{1,0:T(8,128)S(1)} %get-tuple-element.66) | copy-start | bytes 196612
  35.4 54.8 %copy-start.21 = (f32[32,62]{1,0:T(8,128)}, f32[32,62]{1,0:T(8,128)S(1)}, u32[]{:S(2)}) copy-start(f32[32,62]{1,0:T(8,128)S(1)} %get-tuple-element.14) | copy-start | bytes 23812
  35.4 56.2 %copy-start.23 = (f32[32,62]{1,0:T(8,128)}, f32[32,62]{1,0:T(8,128)S(1)}, u32[]{:S(2)}) copy-start(f32[32,62]{1,0:T(8,128)S(1)} %get-tuple-element.15) | copy-start | bytes 23812
  35.4 57.7 %copy-start.25 = (f32[32,62]{1,0:T(8,128)}, f32[32,62]{1,0:T(8,128)S(1)}, u32[]{:S(2)}) copy-start(f32[32,62]{1,0:T(8,128)S(1)} %get-tuple-element.16) | copy-start | bytes 23812
  35.4 59.1 %copy-start.19 = (f32[32,62]{1,0:T(8,128)}, f32[32,62]{1,0:T(8,128)S(1)}, u32[]{:S(2)}) copy-start(f32[32,62]{1,0:T(8,128)S(1)} %get-tuple-element.13) | copy-start | bytes 23812
  35.4 61.5 %copy-start.17 = (f32[32,62]{1,0:T(8,128)}, f32[32,62]{1,0:T(8,128)S(1)}, u32[]{:S(2)}) copy-start(f32[32,62]{1,0:T(8,128)S(1)} %get-tuple-element.12) | copy-start | bytes 23812
  35.4 63.9 %copy-start.27 = (f32[32,62]{1,0:T(8,128)}, f32[32,62]{1,0:T(8,128)S(1)}, u32[]{:S(2)}) copy-start(f32[32,62]{1,0:T(8,128)S(1)} %get-tuple-element.11) | copy-start | bytes 23812
  38.0 15.5 %collective-permute-start.2 = (f32[30,62,128]{2,1,0:T(8,128)S(1)}, f32[30,62,128]{2,1,0:T(8,128)S(1)}, u32[]{:S(2)}, u32[]{:S(2)}) collective-permute-start(f32[30,62,128]{2,1,0:T(8,128)S(1)} %copy.119), channel_id=1, source_target_pairs={{0,4},{4,8},{8,12},{12,16},{16,20},{20,24},{24,28},{1,5},{5,9},{9,... | collective-permute-start | bytes 2856968 | tf_op jit(solution)/shard_map/ppermute | solution.py:20
  43.1 22.6 %collective-permute-start.3 = (f32[30,62,128]{2,1,0:T(8,128)S(1)}, f32[30,62,128]{2,1,0:T(8,128)S(1)}, u32[]{:S(2)}, u32[]{:S(2)}) collective-permute-start(f32[30,62,128]{2,1,0:T(8,128)S(1)} %copy.120), channel_id=1, source_target_pairs={{4,0},{8,4},{12,8},{16,12},{20,16},{24,20},{28,24},{5,1},{9,5},{13... | collective-permute-start | bytes 2856968 | tf_op jit(solution)/shard_map/ppermute | solution.py:22
  45.6 35.6 %copy-start.13 = (f32[128,128]{1,0:T(8,128)}, f32[128,128]{1,0:T(8,128)S(1)}, u32[]{:S(2)}) copy-start(f32[128,128]{1,0:T(8,128)S(1)} %get-tuple-element.67) | copy-start | bytes 196612
  45.6 43.3 %copy-start.15 = (f32[128,128]{1,0:T(8,128)}, f32[128,128]{1,0:T(8,128)S(1)}, u32[]{:S(2)}) copy-start(f32[128,128]{1,0:T(8,128)S(1)} %get-tuple-element.68) | copy-start | bytes 196612
  47.7 20.9 %copy-start.31 = (f32[48,108]{1,0:T(8,128)}, f32[48,108]{1,0:T(8,128)S(1)}, u32[]{:S(2)}) copy-start(f32[48,108]{1,0:T(8,128)S(1)} %get-tuple-element.7) | copy-start | bytes 62212
  47.7 20.9 %copy-start.29 = (f32[48,108]{1,0:T(8,128)}, f32[48,108]{1,0:T(8,128)S(1)}, u32[]{:S(2)}) copy-start(f32[48,108]{1,0:T(8,128)S(1)} %get-tuple-element.6) | copy-start | bytes 62212
  47.7 38.2 %copy-start.39 = (f32[48,108]{1,0:T(8,128)}, f32[48,108]{1,0:T(8,128)S(1)}, u32[]{:S(2)}) copy-start(f32[48,108]{1,0:T(8,128)S(1)} %get-tuple-element.5) | copy-start | bytes 62212
  47.7 54.0 %copy-start.33 = (f32[48,108]{1,0:T(8,128)}, f32[48,108]{1,0:T(8,128)S(1)}, u32[]{:S(2)}) copy-start(f32[48,108]{1,0:T(8,128)S(1)} %get-tuple-element.8) | copy-start | bytes 62212
  47.7 57.8 %copy-start.35 = (f32[48,108]{1,0:T(8,128)}, f32[48,108]{1,0:T(8,128)S(1)}, u32[]{:S(2)}) copy-start(f32[48,108]{1,0:T(8,128)S(1)} %get-tuple-element.9) | copy-start | bytes 62212
  47.7 63.2 %copy-start.37 = (f32[48,108]{1,0:T(8,128)}, f32[48,108]{1,0:T(8,128)S(1)}, u32[]{:S(2)}) copy-start(f32[48,108]{1,0:T(8,128)S(1)} %get-tuple-element.10) | copy-start | bytes 62212
  150.8 2.3 copy-start.9
  150.8 3.0 copy-start.20
  153.1 2.2 copy-start.32
  155.3 3.7 %copy-start.5 = (f32[3,48,128,32]{2,3,1,0:T(8,128)S(1)}, f32[3,48,128,32]{2,3,1,0:T(8,128)}, u32[]{:S(2)}) copy-start(f32[3,48,128,32]{2,3,1,0:T(8,128)} %copy.132) | copy-start | bytes 7077892
  155.3 3.7 %copy-start.7 = (f32[48,32,128]{2,1,0:T(8,128)S(1)}, f32[48,32,128]{2,1,0:T(8,128)}, u32[]{:S(2)}) copy-start(f32[48,32,128]{2,1,0:T(8,128)} %fusion.60) | copy-start | bytes 2359300
  155.3 3.7 %copy-start.8 = (f32[128,128]{1,0:T(8,128)S(1)}, f32[128,128]{1,0:T(8,128)}, u32[]{:S(2)}) copy-start(f32[128,128]{1,0:T(8,128)} %get-tuple-element.64) | copy-start | bytes 196612
  159.9 2.2 copy-start.30
  162.1 3.9 %copy-start.6 = (f32[48,32,128]{2,1,0:T(8,128)S(1)}, f32[48,32,128]{2,1,0:T(8,128)}, u32[]{:S(2)}) copy-start(f32[48,32,128]{2,1,0:T(8,128)} %fusion.63) | copy-start | bytes 2359300
  162.1 3.9 %copy-start.12 = (f32[128,128]{1,0:T(8,128)S(1)}, f32[128,128]{1,0:T(8,128)}, u32[]{:S(2)}) copy-start(f32[128,128]{1,0:T(8,128)} %get-tuple-element.63) | copy-start | bytes 196612
  162.1 7.0 %copy-start.1 = (f32[108,62,128]{2,0,1:T(8,128)S(1)}, f32[108,62,128]{2,0,1:T(8,128)}, u32[]{:S(2)}) copy-start(f32[108,62,128]{2,0,1:T(8,128)} %fusion.46) | copy-start | bytes 10285060
  166.9 2.3 copy-start
  166.9 2.3 copy-start.40
  166.9 2.3 copy-start.41
  166.9 2.3 copy-start.42
  166.9 2.3 copy-start.43
  166.9 2.3 copy-start.44
  166.9 2.3 copy-start.45
  166.9 2.3 copy-start.46
  181.9 12.9 %collective-permute-start.4 = (f32[30,62,128]{2,1,0:T(8,128)S(1)}, f32[30,62,128]{2,1,0:T(8,128)S(1)}, u32[]{:S(2)}, u32[]{:S(2)}) collective-permute-start(f32[30,62,128]{2,1,0:T(8,128)S(1)} %copy.139), channel_id=1, source_target_pairs={{0,4},{4,8},{8,12},{12,16},{16,20},{20,24},{24,28},{1,5},{5,9},{9,... | collective-permute-start | bytes 2856968 | tf_op jit(solution)/shard_map/ppermute | solution.py:32
  184.4 22.7 %collective-permute-start.5 = (f32[30,62,128]{2,1,0:T(8,128)S(1)}, f32[30,62,128]{2,1,0:T(8,128)S(1)}, u32[]{:S(2)}, u32[]{:S(2)}) collective-permute-start(f32[30,62,128]{2,1,0:T(8,128)S(1)} %copy.141), channel_id=1, source_target_pairs={{4,0},{8,4},{12,8},{16,12},{20,16},{24,20},{28,24},{5,1},{9,5},{13... | collective-permute-start | bytes 2856968 | tf_op jit(solution)/shard_map/ppermute | solution.py:32
  207.6 13.1 %copy-start.3 = (f32[48,32,128]{2,1,0:T(8,128)S(1)}, f32[48,32,128]{2,1,0:T(8,128)}, u32[]{:S(2)}) copy-start(f32[48,32,128]{2,1,0:T(8,128)} %param.8) | copy-start | bytes 2359300
  208.0 8.6 %collective-permute-start.6 = (f32[48,15,128]{2,0,1:T(8,128)S(1)}, f32[48,15,128]{2,0,1:T(8,128)S(1)}, u32[]{:S(2)}, u32[]{:S(2)}) collective-permute-start(f32[48,15,128]{2,0,1:T(8,128)S(1)} %get-tuple-element.25), channel_id=1, source_target_pairs={{0,1},{1,2},{2,3},{4,5},{5,6},{6,7},{8,9},{9,10},{10,11},{12,13},{... | collective-permute-start | bytes 1105928 | tf_op jit(solution)/shard_map/ppermute | solution.py:32
  212.0 8.7 %collective-permute-start.7 = (f32[48,15,128]{2,0,1:T(8,128)S(1)}, f32[48,15,128]{2,0,1:T(8,128)S(1)}, u32[]{:S(2)}, u32[]{:S(2)}) collective-permute-start(f32[48,15,128]{2,0,1:T(8,128)S(1)} %get-tuple-element.26), channel_id=1, source_target_pairs={{1,0},{2,1},{3,2},{5,4},{6,5},{7,6},{9,8},{10,9},{11,10},{13,12},{... | collective-permute-start | bytes 1105928 | tf_op jit(solution)/shard_map/ppermute | solution.py:32
  221.3 7.1 %collective-permute-start.8 = (f32[48,15,128]{2,0,1:T(8,128)S(1)}, f32[48,15,128]{2,0,1:T(8,128)S(1)}, u32[]{:S(2)}, u32[]{:S(2)}) collective-permute-start(f32[48,15,128]{2,0,1:T(8,128)S(1)} %get-tuple-element.29), channel_id=1, source_target_pairs={{0,1},{1,2},{2,3},{4,5},{5,6},{6,7},{8,9},{9,10},{10,11},{12,13},{... | collective-permute-start | bytes 1105928 | tf_op jit(solution)/shard_map/ppermute | solution.py:20
  224.0 8.3 %collective-permute-start.9 = (f32[48,15,128]{2,0,1:T(8,128)S(1)}, f32[48,15,128]{2,0,1:T(8,128)S(1)}, u32[]{:S(2)}, u32[]{:S(2)}) collective-permute-start(f32[48,15,128]{2,0,1:T(8,128)S(1)} %get-tuple-element.30), channel_id=1, source_target_pairs={{1,0},{2,1},{3,2},{5,4},{6,5},{7,6},{9,8},{10,9},{11,10},{13,12},{... | collective-permute-start | bytes 1105928 | tf_op jit(solution)/shard_map/ppermute | solution.py:22
  233.2 16.9 %collective-permute-start.10 = (f32[30,62,128]{2,1,0:T(8,128)S(1)}, f32[30,62,128]{2,1,0:T(8,128)S(1)}, u32[]{:S(2)}, u32[]{:S(2)}) collective-permute-start(f32[30,62,128]{2,1,0:T(8,128)S(1)} %copy.144), channel_id=1, source_target_pairs={{0,4},{4,8},{8,12},{12,16},{16,20},{20,24},{24,28},{1,5},{5,9},{9,... | collective-permute-start | bytes 2856968 | tf_op jit(solution)/shard_map/ppermute | solution.py:20
  239.6 21.2 %collective-permute-start.11 = (f32[30,62,128]{2,1,0:T(8,128)S(1)}, f32[30,62,128]{2,1,0:T(8,128)S(1)}, u32[]{:S(2)}, u32[]{:S(2)}) collective-permute-start(f32[30,62,128]{2,1,0:T(8,128)S(1)} %copy.145), channel_id=1, source_target_pairs={{4,0},{8,4},{12,8},{16,12},{20,16},{24,20},{28,24},{5,1},{9,5},{13... | collective-permute-start | bytes 2856968 | tf_op jit(solution)/shard_map/ppermute | solution.py:22
  268.3 2.3 copy-start.26
  268.3 3.8 %copy-start.53 = (f32[3,48,32,128]{3,2,1,0:T(8,128)S(1)}, f32[3,48,32,128]{3,2,1,0:T(8,128)}, u32[]{:S(2)}) copy-start(f32[3,48,32,128]{3,2,1,0:T(8,128)} %param.9) | copy-start | bytes 7077892
  275.6 3.7 copy-start.36
  279.3 2.3 copy-start.24
  286.2 3.9 %copy-start.34 = (f32[48,108]{1,0:T(8,128)S(1)}, f32[48,108]{1,0:T(8,128)}, u32[]{:S(2)}) copy-start(f32[48,108]{1,0:T(8,128)} %copy-done.33) | copy-start | bytes 62212
  290.1 2.3 copy-start.22
  335.1 12.9 %collective-permute-start.12 = (f32[30,62,128]{2,1,0:T(8,128)S(1)}, f32[30,62,128]{2,1,0:T(8,128)S(1)}, u32[]{:S(2)}, u32[]{:S(2)}) collective-permute-start(f32[30,62,128]{2,1,0:T(8,128)S(1)} %copy.160), channel_id=1, source_target_pairs={{0,4},{4,8},{8,12},{12,16},{16,20},{20,24},{24,28},{1,5},{5,9},{9,... | collective-permute-start | bytes 2856968 | tf_op jit(solution)/shard_map/ppermute | solution.py:32
  337.6 20.2 %collective-permute-start.13 = (f32[30,62,128]{2,1,0:T(8,128)S(1)}, f32[30,62,128]{2,1,0:T(8,128)S(1)}, u32[]{:S(2)}, u32[]{:S(2)}) collective-permute-start(f32[30,62,128]{2,1,0:T(8,128)S(1)} %copy.162), channel_id=1, source_target_pairs={{4,0},{8,4},{12,8},{16,12},{20,16},{24,20},{28,24},{5,1},{9,5},{13... | collective-permute-start | bytes 2856968 | tf_op jit(solution)/shard_map/ppermute | solution.py:32
  358.7 7.8 %collective-permute-start.14 = (f32[48,15,128]{2,0,1:T(8,128)S(1)}, f32[48,15,128]{2,0,1:T(8,128)S(1)}, u32[]{:S(2)}, u32[]{:S(2)}) collective-permute-start(f32[48,15,128]{2,0,1:T(8,128)S(1)} %get-tuple-element.21), channel_id=1, source_target_pairs={{0,1},{1,2},{2,3},{4,5},{5,6},{6,7},{8,9},{9,10},{10,11},{12,13},{... | collective-permute-start | bytes 1105928 | tf_op jit(solution)/shard_map/ppermute | solution.py:32
  362.1 8.3 %collective-permute-start.15 = (f32[48,15,128]{2,0,1:T(8,128)S(1)}, f32[48,15,128]{2,0,1:T(8,128)S(1)}, u32[]{:S(2)}, u32[]{:S(2)}) collective-permute-start(f32[48,15,128]{2,0,1:T(8,128)S(1)} %get-tuple-element.22), channel_id=1, source_target_pairs={{1,0},{2,1},{3,2},{5,4},{6,5},{7,6},{9,8},{10,9},{11,10},{13,12},{... | collective-permute-start | bytes 1105928 | tf_op jit(solution)/shard_map/ppermute | solution.py:32
  (7 other events, 11.8 us)
where the time goes:
time: 378 us; the launch traced here: 372 us
  matrix products  152 us (40%)
  waiting for transfers between devices  94 us (25%)
  local copies, waits for them, and re-layouts  55.5 us (15%)
  starting transfers between devices  48.3 us (13%)
  other arithmetic  19.7 us (5%)
    dot_general x12, matrix products, local(): jnp.einsum('je,jyx->eyx', forward_depth[number], spread, precision=exact_...  64.8 us
    ppermute x8, waiting for transfers between devices, passed_along(): lax.ppermute(value, axis, [(source, source + steps) for source in range(l...  51.1 us
    dot_general x12, matrix products, blur_forward(): jnp.einsum('zj,jyx->zyx', band_depth, haloed, precision=exact_mode)  27.5 us
    ppermute x4, waiting for transfers between devices, padded(): lax.ppermute(head, axis, [((i + 1) % count, i) for i in range(ends)])  25.7 us
    unnamed x115, local copies, waits for them, and re-layouts  23.8 us
    dot_general x12, matrix products, blur_forward(): jnp.einsum('yj,zjx->zyx', band_rows, section, precision=exact_mode)  20.9 us
    ppermute x8, starting transfers between devices, passed_along(): lax.ppermute(value, axis, [(source, source + steps) for source in range(l...  18.8 us
    ppermute x4, starting transfers between devices, padded(): lax.ppermute(tail, axis, [(i, (i + 1) % count) for i in range(ends)])  17.9 us
  transfers between devices with their start and end apart: 17, of which 14 were waited for; matrix products, arithmetic and copies ran while one was open for 22% of the time, Pallas kernels for 0%

commit v1 on v0

v1 whole, which is shorter than its diff:
```python
import functools

import jax
import jax.numpy as jnp
from jax import lax
from jax.experimental import pallas as pl
from jax.experimental.pallas import tpu as pltpu
from jax.sharding import PartitionSpec as P

ITERS = 2
F32 = jnp.float32
BF16 = jnp.bfloat16
VMEM_LIMIT = 60 * 1024 * 1024


def round_up(value, unit):
    return -(-value // unit) * unit


def shifted(value, axis, step):
    count = lax.axis_size(axis)
    if step > 0:
        pairs = [(i, i + 1) for i in range(count - 1)]
    else:
        pairs = [(i + 1, i) for i in range(count - 1)]
    return lax.ppermute(value, axis, pairs)


def top_part(value):
    return lax.reduce_precision(value, 8, 7)


def split_cols(matrix):
    high = top_part(matrix)
    low = matrix - high
    return jnp.concatenate([high, high, low], axis=-1).astype(BF16)


def split_square(matrix):
    high = top_part(matrix)
    low = matrix - high
    upper = jnp.concatenate([high, low], axis=-1)
    lower = jnp.concatenate([high, jnp.zeros_like(low)], axis=-1)
    return jnp.concatenate([upper, lower], axis=-2).astype(BF16)


def halves(value):
    high = value.astype(BF16)
    low = (value - high.astype(F32)).astype(BF16)
    return high, low


def banded(taps, index):
    extent = taps.shape[-1]
    pick = index[..., None] == jnp.arange(extent, dtype=jnp.int32)
    return jnp.sum(jnp.where(pick, taps[:, None, None, :], 0.0), axis=-1)


def forward_kernel(sizes, c, clo, chi, s, slo, shi, wz, wy, wx, out, mid):
    depth, rows, reach, zpad, views = sizes
    width = c.shape[-1]
    side = s.shape[0] // depth
    total = rows + side
    step = pl.program_id(0)

    @pl.when(step == 0)
    def _():
        fill = jnp.zeros((zpad - reach, width), F32)

        def column(low, centre, high, y, n):
            return jnp.concatenate(
                [
                    low[pl.ds(y, reach, stride=n), :],
                    fill,
                    centre[pl.ds(y, depth, stride=n), :],
                    high[pl.ds(y, reach, stride=n), :],
                    fill,
                ],
                axis=0,
            )

        def run(low, centre, high, n, base):
            def body(i, carry):
                both = jnp.concatenate(
                    [column(low, centre, high, 2 * i + j, n) for j in range(2)], axis=1
                )
                top, rest = halves(both)
                data = jnp.concatenate([top, rest, top], axis=0)
                result = jnp.dot(wz[...], data, preferred_element_type=F32)
                for j in range(2):
                    mid[pl.ds(base + 2 * i + j, views * depth, stride=total), :] = result[
                        :, j * width : (j + 1) * width
                    ]
                return carry

            lax.fori_loop(0, n // 2, body, 0)

        run(clo, c, chi, rows, 0)
        run(slo, s, shi, side, rows)

    @pl.when(step > 0)
    def _():
        view = step - 1
        group = 8

        def body(i, carry):
            start = (view * depth + i * group) * total
            lines = []
            for j in range(group // 2):
                at = pl.multiple_of(start + 2 * j * total, total)
                both = jnp.concatenate(
                    [mid[pl.ds(at, total), :], mid[pl.ds(at + total, total), :]], axis=1
                )
                top, rest = halves(both)
                data = jnp.concatenate([top, rest, top], axis=0)
                result = jnp.dot(wy[0], data, preferred_element_type=F32)
                lines += [result[:, :width], result[:, width:]]
            flat = jnp.concatenate(lines, axis=0)
            top, rest = halves(flat)
            result = jnp.dot(
                jnp.concatenate([top, rest], axis=1), wx[0], preferred_element_type=F32
            )
            at = pl.multiple_of(i * (group * rows), group * rows)
            out[0, pl.ds(at, group * rows), :] = result[:, :width] + result[:, width:]
            return carry

        lax.fori_loop(0, depth // group, body, 0)


def forward(sizes, c, clo, chi, s, slo, shi, wz, wy, wx):
    depth, rows, reach, zpad, views = sizes
    width = c.shape[-1]
    side = s.shape[0] // depth
    total = rows + side
    whole = lambda a: pl.BlockSpec(a.shape, lambda i: (0,) * a.ndim)
    per_view = lambda a: pl.BlockSpec(
        (1,) + a.shape[1:], lambda i: (jnp.maximum(i - 1, 0),) + (0,) * (a.ndim - 1)
    )
    result = jax.ShapeDtypeStruct((views, depth * rows, width), F32)
    return pl.pallas_call(
        functools.partial(forward_kernel, sizes),
        out_shape=result,
        grid=(views + 1,),
        in_specs=[whole(a) for a in (c, clo, chi, s, slo, shi, wz)] + [per_view(wy), per_view(wx)],
        out_specs=per_view(result),
        scratch_shapes=[pltpu.VMEM((views * depth * total, width), F32)],
        compiler_params=pltpu.CompilerParams(vmem_limit_bytes=VMEM_LIMIT),
        cost_estimate=pl.CostEstimate(
            flops=6 * 10**9, bytes_accessed=12 * 10**6, transcendentals=0
        ),
        name="forward",
    )(c, clo, chi, s, slo, shi, wz, wy, wx)


def backward_kernel(sizes, side, obs, blur, wx, wy, wzc, wzs, cc, clo, chi, sc, slo, shi, mid):
    depth, rows, reach, zpad, views = sizes
    width = obs.shape[-1]
    total = rows + side
    lines = views * depth
    step = pl.program_id(0)

    @pl.when(step < views)
    def _():
        group = 8

        def body(i, carry):
            at = pl.multiple_of(i * (group * rows), group * rows)
            ratio = obs[0, pl.ds(at, group * rows), :] / blur[0, pl.ds(at, group * rows), :]
            top, rest = halves(ratio)
            flat = jnp.dot(jnp.concatenate([top, rest], axis=1), wx[0], preferred_element_type=F32)
            flat = flat[:, :width] + flat[:, width:]
            for j in range(group // 2):
                both = jnp.concatenate(
                    [
                        flat[2 * j * rows : (2 * j + 1) * rows],
                        flat[(2 * j + 1) * rows : (2 * j + 2) * rows],
                    ],
                    axis=1,
                )
                top, rest = halves(both)
                data = jnp.concatenate([top, rest, top], axis=0)
                result = jnp.dot(wy[0], data, preferred_element_type=F32)
                for k in range(2):
                    line = step * depth + i * group + 2 * j + k
                    mid[pl.ds(line, total, stride=lines), :] = result[
                        :, k * width : (k + 1) * width
                    ]
            return carry

        lax.fori_loop(0, depth // group, body, 0)

    @pl.when(step == views)
    def _():
        def run(weights, low, centre, high, n, base, first, last):
            def body(i, carry):
                at = pl.multiple_of((base + 2 * i) * lines, lines)
                both = jnp.concatenate(
                    [mid[pl.ds(at, lines), :], mid[pl.ds(at + lines, lines), :]], axis=1
                )
                top, rest = halves(both)
                data = jnp.concatenate([top, rest, top], axis=0)
                result = jnp.dot(weights, data, preferred_element_type=F32)
                for j in range(2):
                    part = result[:, j * width : (j + 1) * width]
                    y = 2 * i + j
                    low[pl.ds(y, reach, stride=n), :] = part[:reach]
                    centre[pl.ds(y, depth, stride=n), :] = part[zpad : zpad + depth]
                    high[pl.ds(y, reach, stride=n), :] = part[zpad + depth : zpad + depth + reach]
                return carry

            lax.fori_loop(first, last, body, 0)

        run(wzc[...], clo, cc, chi, rows, 0, 0, rows // 2)
        run(wzs[0], slo, sc, shi, side, rows, 0, side // 4)
        run(wzs[1], slo, sc, shi, side, rows, side // 4, side // 2)


def backward(sizes, side, obs, blur, wx, wy, wzc, wzs):
    depth, rows, reach, zpad, views = sizes
    width = obs.shape[-1]
    total = rows + side
    whole = lambda a: pl.BlockSpec(a.shape, lambda i: (0,) * len(a.shape))
    per_view = lambda a: pl.BlockSpec(
        (1,) + a.shape[1:], lambda i: (jnp.minimum(i, views - 1),) + (0,) * (a.ndim - 1)
    )
    shapes = [
        jax.ShapeDtypeStruct((count * n, width), F32)
        for n in (rows, side)
        for count in (depth, reach, reach)
    ]
    return pl.pallas_call(
        functools.partial(backward_kernel, sizes, side),
        out_shape=shapes,
        grid=(views + 1,),
        in_specs=[per_view(a) for a in (obs, blur, wx, wy)] + [whole(wzc), whole(wzs)],
        out_specs=[whole(a) for a in shapes],
        scratch_shapes=[pltpu.VMEM((total * views * depth, width), F32)],
        compiler_params=pltpu.CompilerParams(vmem_limit_bytes=VMEM_LIMIT),
        cost_estimate=pl.CostEstimate(
            flops=6 * 10**9, bytes_accessed=12 * 10**6, transcendentals=0
        ),
        name="backward",
    )(obs, blur, wx, wy, wzc, wzs)


def pack_kernel(count, per, x, out):
    rows = x.shape[-1] // count
    for g in range(x.shape[0] // per):
        for d in range(count):
            out[d, g] = jnp.concatenate(
                [x[g * per + j, :, d * rows : (d + 1) * rows] for j in range(per)], axis=1
            )


def pack(turned, count, per):
    planes, xl, yf = turned.shape
    block = 48 if planes % 48 == 0 else per
    return pl.pallas_call(
        functools.partial(pack_kernel, count, per),
        out_shape=jax.ShapeDtypeStruct((count, planes // per, xl, per * (yf // count)), F32),
        grid=(planes // block,),
        in_specs=[pl.BlockSpec((block, xl, yf), lambda i: (i, 0, 0))],
        out_specs=pl.BlockSpec(
            (count, block // per, xl, per * (yf // count)), lambda i: (0, i, 0, 0)
        ),
        compiler_params=pltpu.CompilerParams(vmem_limit_bytes=VMEM_LIMIT),
        name="pack",
    )(turned)


def unpack_kernel(x, out):
    for g in range(x.shape[1]):
        stacked = jnp.concatenate([x[k, g] for k in range(x.shape[0])], axis=0)
        out[g] = stacked.T


def unpack(received):
    count, groups, xl, lanes = received.shape
    block = 12 if groups % 12 == 0 else 1
    return pl.pallas_call(
        unpack_kernel,
        out_shape=jax.ShapeDtypeStruct((groups, lanes, count * xl), F32),
        grid=(groups // block,),
        in_specs=[pl.BlockSpec((count, block, xl, lanes), lambda i: (0, i, 0, 0))],
        out_specs=pl.BlockSpec((block, lanes, count * xl), lambda i: (i, 0, 0)),
        compiler_params=pltpu.CompilerParams(vmem_limit_bytes=VMEM_LIMIT),
        name="unpack",
    )(received)


def normalize(kernel):
    return kernel / jnp.sum(kernel, axis=-1, keepdims=True)


def local(
    prior_estimate,
    views_upright,
    views_turned,
    kernel_depth,
    kernel_rows,
    kernel_columns,
    lateral_offsets,
    block_views,
):
    depth, rows, width = prior_estimate.shape
    views = kernel_depth.shape[0]
    reach = (kernel_depth.shape[1] - 1) // 2
    reach_y = (kernel_rows.shape[1] - 1) // 2
    reach_x = (kernel_columns.shape[1] - 1) // 2
    zpad = round_up(reach, 16)
    ypad = round_up(reach_y, 8)
    side = 2 * ypad
    sizes = (depth, rows, reach, zpad, views)
    n_xy = lax.axis_size("xy")
    n_gz = lax.axis_size("gz")

    half = views_turned.shape[0]
    per = width // rows
    packed = pack(
        views_turned.reshape(half * depth, views_turned.shape[2], views_turned.shape[3]), n_xy, per
    )
    received = lax.all_to_all(packed, "xy", split_axis=0, concat_axis=0, tiled=True)
    turned = unpack(received).reshape(half, depth * rows, width)
    observed = jnp.concatenate(
        [views_upright.reshape(views - half, depth * rows, width), turned], axis=0
    )

    taps_z = normalize(kernel_depth)
    taps_y = normalize(kernel_rows)
    taps_x = normalize(kernel_columns)
    z_in = jnp.arange(depth, dtype=jnp.int32)
    low = jnp.arange(zpad, dtype=jnp.int32)
    far = jnp.int32(1 << 20)
    z_ext = jnp.concatenate(
        [
            jnp.where(low < reach, low - reach, far),
            z_in,
            jnp.where(low < reach, low + depth, far),
        ]
    )
    y_in = jnp.arange(rows, dtype=jnp.int32)
    rim = jnp.arange(ypad, dtype=jnp.int32)
    y_ext = jnp.concatenate([y_in, rim - ypad, rim + rows])
    x_in = jnp.arange(width, dtype=jnp.int32)
    band_z = banded(taps_z, (z_ext[None, :] - z_in[:, None] + reach)[None])
    band_y = banded(taps_y, (y_ext[None, :] - y_in[:, None] + reach_y)[None])
    band_x = banded(
        taps_x,
        (x_in[None, :] - x_in[:, None] + reach_x)[None] + lateral_offsets[:, None, None],
    )
    wz_f = split_cols(band_z.reshape(views * depth, z_ext.shape[0]))
    wy_f = split_cols(band_y)
    wx_f = split_square(jnp.swapaxes(band_x, 1, 2))
    wx_b = split_square(band_x)
    wy_b = split_cols(jnp.swapaxes(band_y, 1, 2))

    member = jnp.sum(
        (block_views[:, :, None] == jnp.arange(views, dtype=jnp.int32)).astype(F32), axis=1
    ) / block_views.shape[1]
    member = member.reshape(n_gz, n_xy, views)
    near = jnp.arange(3, dtype=jnp.int32) - 1
    near_z = jnp.clip(lax.axis_index("gz") + near, 0, n_gz - 1)
    near_y = jnp.clip(lax.axis_index("xy") + near, 0, n_xy - 1)
    pick_z = (near_z[:, None] == jnp.arange(n_gz, dtype=jnp.int32)).astype(F32)
    pick_y = (near_y[:, None] == jnp.arange(n_xy, dtype=jnp.int32)).astype(F32)
    around = jnp.sum(pick_z[:, :, None, None] * member, axis=1)
    around = jnp.sum(pick_y[None, :, :, None] * around[:, None], axis=2)
    by_row = jnp.concatenate(
        [
            jnp.broadcast_to(around[i][None], (n,) + around.shape[1:])
            for i, n in enumerate((zpad, depth, zpad))
        ]
    )
    spread = jnp.transpose(band_z, (2, 0, 1))
    wz_b = [
        split_cols((spread * by_row[:, b, :, None]).reshape(z_ext.shape[0], views * depth))
        for b in range(3)
    ]
    wz_centre = wz_b[1]
    wz_side = jnp.stack([wz_b[0], wz_b[2]])

    estimate = prior_estimate
    for iteration in range(ITERS):
        from_left = shifted(estimate[:, rows - ypad :], "xy", 1)
        from_right = shifted(estimate[:, :ypad], "xy", -1)
        below = shifted(estimate[depth - reach :], "gz", 1)
        above = shifted(estimate[:reach], "gz", -1)
        sides = jnp.concatenate([from_left, from_right], axis=1)
        side_below = shifted(sides[depth - reach :], "gz", 1)
        side_above = shifted(sides[:reach], "gz", -1)
        flat = lambda a: a.reshape(-1, width)
        blurred = forward(
            sizes,
            *(flat(a) for a in (estimate, below, above, sides, side_below, side_above)),
            wz_f,
            wy_f,
            wx_f,
        )
        cc, clo, chi, sc, slo, shi = backward(
            sizes, side, observed, blurred, wx_b, wy_b, wz_centre, wz_side
        )
        cube = lambda a, n: a.reshape(-1, n, width)
        cc, clo, chi = (cube(a, rows) for a in (cc, clo, chi))
        sc, slo, shi = (cube(a, side) for a in (sc, slo, shi))
        s_low = shifted(shi, "gz", 1)
        s_high = shifted(slo, "gz", -1)
        c_low = shifted(chi, "gz", 1)
        c_high = shifted(clo, "gz", -1)
        head = ((0, depth - reach), (0, 0), (0, 0))
        tail = ((depth - reach, 0), (0, 0), (0, 0))
        sc = sc + jnp.pad(s_low, head) + jnp.pad(s_high, tail)
        from_left = shifted(sc[:, ypad:], "xy", 1)
        from_right = shifted(sc[:, :ypad], "xy", -1)
        cc = cc + jnp.pad(c_low, head) + jnp.pad(c_high, tail)
        cc = cc + jnp.pad(from_left, ((0, 0), (0, rows - ypad), (0, 0)))
        cc = cc + jnp.pad(from_right, ((0, 0), (rows - ypad, 0), (0, 0)))
        estimate = estimate * cc
    return estimate


def solution(mesh):
    in_specs = (
        P("gz", "xy", None),
        P(None, "gz", "xy", None),
        P(None, "gz", "xy", None),
        P(),
        P(),
        P(),
        P(),
        P(),
    )
    out_specs = P("gz", "xy", None)
    return jax.shard_map(local, mesh=mesh, in_specs=in_specs, out_specs=out_specs, check_vma=False)
```

time: 378 us -> 291 us (0.77)
  matrix products: 152 us -> 0 us
  Pallas kernels: 0 us -> 126 us
  waiting for transfers between devices: 94 us -> 43.3 us
  local copies, waits for them, and re-layouts: 55.5 us -> 12.3 us
  starting transfers between devices: 48.3 us -> 79.1 us
  other arithmetic: 19.7 us -> 24.6 us
    dot_general x75 -> x0, matrix products: 152 us -> none  [the longest x12 64.8 us: local(): jnp.einsum('je,jyx->eyx', forward_depth[number], spread, precision=exact_...]
    pallas_call x0 -> x6, Pallas kernels: none -> 126 us  [the longest x2 60.1 us: backward(): pl.pallas_call(functools.partial(backward_kernel, sizes, side), out_shape...]
    ppermute x16 -> x24, waiting for transfers between devices: 94 us -> 43.3 us  [shifted(): return lax.ppermute(value, axis, pairs)]
    ppermute x16 -> x24, starting transfers between devices: 43.5 us -> 75.3 us  [shifted(): return lax.ppermute(value, axis, pairs)]
    unnamed x115 -> x46, local copies, waits for them, and re-layouts: 23.8 us -> 4.53 us
    all_to_all x3 -> x0, local copies, waits for them, and re-layouts: 17.6 us -> none  [local(): lax.all_to_all(views_turned, 'xy', split_axis=3, concat_axis=2, tiled=True)]
    concatenate x1 -> x10, other arithmetic: 0.1 us -> 11.1 us  [the longest x1 4.79 us: local(): jnp.concatenate([views_upright.reshape(views - half, depth * rows, width)...]
    all_to_all x1 -> x0, other arithmetic: 9.65 us -> none  [local(): lax.all_to_all(views_turned, 'xy', split_axis=3, concat_axis=2, tiled=True)]
  transfers between devices with their start and end apart: 17 -> 25, of which waited for: 14 -> 11; matrix products, arithmetic and copies ran while one was open for 22% -> 9% of each run, Pallas kernels for 0% -> 12%
where the time goes in v1:
time: 291 us; the launch traced here: 286 us
  Pallas kernels  126 us (43%)
  starting transfers between devices  79.1 us (27%)
  waiting for transfers between devices  43.3 us (15%)
  other arithmetic  24.6 us (8%)
  local copies, waits for them, and re-layouts  12.3 us (4%)
    ppermute x24, starting transfers between devices, shifted(): return lax.ppermute(value, axis, pairs)  75.3 us
    pallas_call x2, Pallas kernels, backward(): pl.pallas_call(functools.partial(backward_kernel, sizes, side), out_shape...  60.1 us
    pallas_call x2, Pallas kernels, forward(): pl.pallas_call(functools.partial(forward_kernel, sizes), out_shape=result...  57.1 us
    ppermute x24, waiting for transfers between devices, shifted(): return lax.ppermute(value, axis, pairs)  43.3 us
  transfers between devices with their start and end apart: 25, of which 11 were waited for; matrix products, arithmetic and copies ran while one was open for 9% of the time, Pallas kernels for 12%

profile of v1, /device:TPU:1, one launch (start us, length us, event | category | flops | bytes accessed | tf_op | source)
XLA Modules:
  0.0 286.3 jit_solution(2000229867417992777)
XLA Ops:
  0.0 2.1 fusion.23
  2.1 1.3 collective-permute-start.3
  3.3 5.4 %collective-permute-start.2 = (f32[48,16,128]{2,1,0:T(8,128)}, f32[48,16,128]{2,1,0:T(8,128)}, u32[]{:S(2)}, u32[]{:S(2)}) collective-permute-start(f32[48,16,128]{2,1,0:T(8,128)} %get-tuple-element.42), channel_id=1, source_target_pairs={{0,1},{1,2},{2,3},{4,5},{5,6},{6,7},{8,9},{9,10},{10,11},{12,13},{... | collective-permute-start | bytes 1179656 | tf_op jit(solution)/shard_map/ppermute | solution.py:26
  8.8 2.2 fusion.24
  11.0 2.9 collective-permute-start.1
  13.8 3.5 %collective-permute-start = (f32[30,32,128]{2,1,0:T(8,128)}, f32[30,32,128]{2,1,0:T(8,128)}, u32[]{:S(2)}, u32[]{:S(2)}) collective-permute-start(f32[30,32,128]{2,1,0:T(8,128)} %get-tuple-element.44), channel_id=1, source_target_pairs={{0,4},{4,8},{8,12},{12,16},{16,20},{20,24},{24,28},{1,5},{5,9},{9,... | collective-permute-start | bytes 1474568 | tf_op jit(solution)/shard_map/ppermute | solution.py:26
  17.3 4.8 %pack.1 = f32[4,36,32,128]{3,2,1,0:T(8,128)} custom-call(f32[144,32,128]{2,1,0:T(8,128)} %bitcast.71), custom_call_target="tpu_custom_call" | custom-call | tf_op jit(solution)/shard_map/pack/pallas_call | solution.py:258
  22.1 3.8 %all-to-all-start = ((f32[4,36,32,128]{3,2,1,0:T(8,128)}), f32[4,36,32,128]{3,2,1,0:T(8,128)S(1)}, u32[]{:S(2)}, u32[]{:S(2)}) async-start(f32[4,36,32,128]{3,2,1,0:T(8,128)} %pack.1), calls=%async_computation | async-start | bytes 4718592 | tf_op jit(solution)/shard_map/all_to_all | solution.py:322
  28.4 1.0 select_reduce_fusion.1
  30.4 0.7 fusion.13
  31.3 0.8 copy.63
  32.2 1.8 select_reduce_fusion
  34.3 1.0 fusion.2.wx
  35.3 2.0 maximum_maximum_fusion.wzs
  38.5 0.9 pad_maximum_fusion.1.wz
  39.4 0.8 pad_maximum_fusion.2.wzc
  40.4 1.0 constant_dynamic-update-slice_fusion.1
  41.4 1.0 constant_dynamic-update-slice_fusion
  42.6 2.3 collective-permute-start.5
  44.9 3.3 %collective-permute-start.4 = (f32[30,32,128]{2,1,0:T(8,128)S(1)}, f32[30,32,128]{2,1,0:T(8,128)S(1)}, u32[]{:S(2)}, u32[]{:S(2)}) collective-permute-start(f32[30,32,128]{2,1,0:T(8,128)S(1)} %get-tuple-element.40), channel_id=1, source_target_pairs={{0,4},{4,8},{8,12},{12,16},{16,20},{20,24},{24,28},{1,5},{5,9},{9,... | collective-permute-start | bytes 1474568 | tf_op jit(solution)/shard_map/ppermute | solution.py:26
  48.2 1.6 pad_maximum_fusion.3.wy
  49.8 0.8 pad_maximum_fusion.4.wy
  50.6 1.0 fusion.3.wx
  51.6 2.5 collective-permute-done.5
  54.1 0.8 copy-done.19
  55.0 28.5 %forward.2.blur = f32[6,1536,128]{2,1,0:T(8,128)} custom-call(f32[1536,128]{1,0:T(8,128)} %bitcast.68, f32[960,128]{1,0:T(8,128)} %bitcast.4.clo, f32[960,128]{1,0:T(8,128)} %bitcast.5.chi, f32[1536,128]{1,0:T(8,128)} %bitcast.69, f32[960,128]{1,0:T(8,128)} %bitcast.87, f32[960,128]{1,0:T(8,128)} %bitcast.86, bf16[288,336]{1,0:T(8,128)(2,1)} %pad_maximum_fusion.1.wz, ...), custom_call_target="tpu_custom_call" | custom-call | flops 6000000000 | bytes 12000000 | tf_op jit(solution)/shard_map/forward/pallas_call | solution.py:140
  83.6 1.5 copy-done.2
  85.0 4.3 %unpack.1 = f32[36,128,128]{2,1,0:T(8,128)} custom-call(f32[4,36,32,128]{3,2,1,0:T(8,128)} %copy-done.2), custom_call_target="tpu_custom_call" | custom-call | tf_op jit(solution)/shard_map/unpack/pallas_call | solution.py:280
  89.3 4.8 %pad_maximum_fusion.obs = f32[6,1536,128]{2,1,0:T(8,128)} fusion(f32[3,1536,128]{2,1,0:T(8,128)} %bitcast.67, f32[3,1536,128]{2,1,0:T(8,128)} %bitcast.72), kind=kLoop, calls=%fused_computation.3 | loop fusion | flops 1179648 | bytes 9437184 | tf_op jit(solution)/shard_map/concatenate | solution.py:324
  94.1 30.1 %backward.2 = (f32[1536,128]{1,0:T(8,128)}, f32[960,128]{1,0:T(8,128)}, f32[960,128]{1,0:T(8,128)}, f32[1536,128]{1,0:T(8,128)}, f32[960,128]{1,0:T(8,128)}, /*index=5*/f32[960,128]{1,0:T(8,128)}) custom-call(f32[6,1536,128]{2,1,0:T(8,128)} %pad_maximum_fusion.obs, f32[6,1536,128]{2,1,0:T(8,128)} %forward.2.blur, bf16[6,256,256]{2,1,0:T(8,128)(2,1)} %fusion.3.wx, ...), custom_call_target="tpu_custom_call" | custom-call | flops 6000000000 | bytes 12000000 | tf_op jit(solution)/shard_map/backward/pallas_call | solution.py:231
  124.2 4.2 %collective-permute-start.8 = (f32[30,32,128]{2,1,0:T(8,128)}, f32[30,32,128]{2,1,0:T(8,128)S(1)}, u32[]{:S(2)}, u32[]{:S(2)}) collective-permute-start(f32[30,32,128]{2,1,0:T(8,128)} %bitcast.93), channel_id=1, source_target_pairs={{0,4},{4,8},{8,12},{12,16},{16,20},{20,24},{24,28},{1,5},{5,9},{9,... | collective-permute-start | bytes 1474568 | tf_op jit(solution)/shard_map/ppermute | solution.py:26
  128.4 1.9 collective-permute-start.9
  130.3 5.1 %collective-permute-start.6 = (f32[30,32,128]{2,1,0:T(8,128)}, f32[30,32,128]{2,1,0:T(8,128)S(1)}, u32[]{:S(2)}, u32[]{:S(2)}) collective-permute-start(f32[30,32,128]{2,1,0:T(8,128)} %bitcast.85), channel_id=1, source_target_pairs={{0,4},{4,8},{8,12},{12,16},{16,20},{20,24},{24,28},{1,5},{5,9},{9,... | collective-permute-start | bytes 1474568 | tf_op jit(solution)/shard_map/ppermute | solution.py:26
  135.4 1.9 collective-permute-start.7
  137.3 8.4 %collective-permute-done.9 = f32[30,32,128]{2,1,0:T(8,128)S(1)} collective-permute-done((f32[30,32,128]{2,1,0:T(8,128)}, f32[30,32,128]{2,1,0:T(8,128)S(1)}, u32[]{:S(2)}, u32[]{:S(2)}) %collective-permute-start.9) | collective-permute-done | bytes 491552 | tf_op jit(solution)/shard_map/ppermute | solution.py:26
  145.7 1.3 pad_add_fusion.1
  147.1 3.3 %collective-permute-start.10 = (f32[48,16,128]{2,1,0:T(8,128)S(1)}, f32[48,16,128]{2,1,0:T(8,128)S(1)}, u32[]{:S(2)}, u32[]{:S(2)}) collective-permute-start(f32[48,16,128]{2,1,0:T(8,128)S(1)} %get-tuple-element.37), channel_id=1, source_target_pairs={{0,1},{1,2},{2,3},{4,5},{5,6},{6,7},{8,9},{9,10},{10,11},{12,13},{... | collective-permute-start | bytes 1179656 | tf_op jit(solution)/shard_map/ppermute | solution.py:26
  150.3 1.3 collective-permute-start.11
  151.7 3.5 %collective-permute-done.7 = f32[30,32,128]{2,1,0:T(8,128)S(1)} collective-permute-done((f32[30,32,128]{2,1,0:T(8,128)}, f32[30,32,128]{2,1,0:T(8,128)S(1)}, u32[]{:S(2)}, u32[]{:S(2)}) %collective-permute-start.7) | collective-permute-done | bytes 491552 | tf_op jit(solution)/shard_map/ppermute | solution.py:26
  155.2 1.6 collective-permute-done.10
  156.7 3.9 %collective-permute-done.11 = f32[48,16,128]{2,1,0:T(8,128)S(1)} collective-permute-done((f32[48,16,128]{2,1,0:T(8,128)S(1)}, f32[48,16,128]{2,1,0:T(8,128)S(1)}, u32[]{:S(2)}, u32[]{:S(2)}) %collective-permute-start.11) | collective-permute-done | bytes 393248 | tf_op jit(solution)/shard_map/ppermute | solution.py:26
  161.0 3.1 %collective-permute-start.14 = (f32[48,16,128]{2,1,0:T(8,128)S(1)}, f32[48,16,128]{2,1,0:T(8,128)S(1)}, u32[]{:S(2)}, u32[]{:S(2)}) collective-permute-start(f32[48,16,128]{2,1,0:T(8,128)S(1)} %get-tuple-element.34), channel_id=1, source_target_pairs={{0,1},{1,2},{2,3},{4,5},{5,6},{6,7},{8,9},{9,10},{10,11},{12,13},{... | collective-permute-start | bytes 1179656 | tf_op jit(solution)/shard_map/ppermute | solution.py:26
  164.1 1.3 collective-permute-start.15
  165.5 1.9 collective-permute-start.13
  167.5 3.6 %collective-permute-start.12 = (f32[30,32,128]{2,1,0:T(8,128)S(1)}, f32[30,32,128]{2,1,0:T(8,128)S(1)}, u32[]{:S(2)}, u32[]{:S(2)}) collective-permute-start(f32[30,32,128]{2,1,0:T(8,128)S(1)} %get-tuple-element.36), channel_id=1, source_target_pairs={{0,4},{4,8},{8,12},{12,16},{16,20},{20,24},{24,28},{1,5},{5,9},{9,... | collective-permute-start | bytes 1474568 | tf_op jit(solution)/shard_map/ppermute | solution.py:26
  171.2 1.5 collective-permute-done.15
  172.8 1.9 collective-permute-start.17
  174.8 5.7 %collective-permute-start.16 = (f32[30,32,128]{2,1,0:T(8,128)S(1)}, f32[30,32,128]{2,1,0:T(8,128)S(1)}, u32[]{:S(2)}, u32[]{:S(2)}) collective-permute-start(f32[30,32,128]{2,1,0:T(8,128)S(1)} %get-tuple-element.32), channel_id=1, source_target_pairs={{0,4},{4,8},{8,12},{12,16},{16,20},{20,24},{24,28},{1,5},{5,9},{9,... | collective-permute-start | bytes 1474568 | tf_op jit(solution)/shard_map/ppermute | solution.py:26
  180.5 6.6 %collective-permute-done.17 = f32[30,32,128]{2,1,0:T(8,128)S(1)} collective-permute-done((f32[30,32,128]{2,1,0:T(8,128)S(1)}, f32[30,32,128]{2,1,0:T(8,128)S(1)}, u32[]{:S(2)}, u32[]{:S(2)}) %collective-permute-start.17) | collective-permute-done | bytes 491552 | tf_op jit(solution)/shard_map/ppermute | solution.py:26
  187.2 0.8 copy-done.21
  188.2 28.6 %forward.3.blur = f32[6,1536,128]{2,1,0:T(8,128)} custom-call(f32[1536,128]{1,0:T(8,128)} %bitcast.66, f32[960,128]{1,0:T(8,128)} %bitcast.84, f32[960,128]{1,0:T(8,128)} %bitcast.81, f32[1536,128]{1,0:T(8,128)} %bitcast.70, f32[960,128]{1,0:T(8,128)} %bitcast.92, f32[960,128]{1,0:T(8,128)} %bitcast.89, bf16[288,336]{1,0:T(8,128)(2,1)} %pad_maximum_fusion.1.wz, ...), custom_call_target="tpu_custom_call" | custom-call | flops 6000000000 | bytes 12000000 | tf_op jit(solution)/shard_map/forward/pallas_call | solution.py:140
  216.7 30.1 %backward.3 = (f32[1536,128]{1,0:T(8,128)}, f32[960,128]{1,0:T(8,128)}, f32[960,128]{1,0:T(8,128)}, f32[1536,128]{1,0:T(8,128)}, f32[960,128]{1,0:T(8,128)}, /*index=5*/f32[960,128]{1,0:T(8,128)}) custom-call(f32[6,1536,128]{2,1,0:T(8,128)} %pad_maximum_fusion.obs, f32[6,1536,128]{2,1,0:T(8,128)} %forward.3.blur, bf16[6,256,256]{2,1,0:T(8,128)(2,1)} %fusion.3.wx, ...), custom_call_target="tpu_custom_call" | custom-call | flops 6000000000 | bytes 12000000 | tf_op jit(solution)/shard_map/backward/pallas_call | solution.py:231
  246.8 3.3 %collective-permute-start.20 = (f32[30,32,128]{2,1,0:T(8,128)}, f32[30,32,128]{2,1,0:T(8,128)S(1)}, u32[]{:S(2)}, u32[]{:S(2)}) collective-permute-start(f32[30,32,128]{2,1,0:T(8,128)} %bitcast.90), channel_id=1, source_target_pairs={{0,4},{4,8},{8,12},{12,16},{16,20},{20,24},{24,28},{1,5},{5,9},{9,... | collective-permute-start | bytes 1474568 | tf_op jit(solution)/shard_map/ppermute | solution.py:26
  250.1 1.9 collective-permute-start.21
  252.0 9.2 %collective-permute-start.18 = (f32[30,32,128]{2,1,0:T(8,128)}, f32[30,32,128]{2,1,0:T(8,128)S(1)}, u32[]{:S(2)}, u32[]{:S(2)}) collective-permute-start(f32[30,32,128]{2,1,0:T(8,128)} %bitcast.82), channel_id=1, source_target_pairs={{0,4},{4,8},{8,12},{12,16},{16,20},{20,24},{24,28},{1,5},{5,9},{9,... | collective-permute-start | bytes 1474568 | tf_op jit(solution)/shard_map/ppermute | solution.py:26
  261.2 1.9 collective-permute-start.19
  263.2 8.2 %collective-permute-done.21 = f32[30,32,128]{2,1,0:T(8,128)S(1)} collective-permute-done((f32[30,32,128]{2,1,0:T(8,128)}, f32[30,32,128]{2,1,0:T(8,128)S(1)}, u32[]{:S(2)}, u32[]{:S(2)}) %collective-permute-start.21) | collective-permute-done | bytes 491552 | tf_op jit(solution)/shard_map/ppermute | solution.py:26
  271.3 1.3 pad_add_fusion
  272.7 3.8 %collective-permute-start.22 = (f32[48,16,128]{2,1,0:T(8,128)S(1)}, f32[48,16,128]{2,1,0:T(8,128)S(1)}, u32[]{:S(2)}, u32[]{:S(2)}) collective-permute-start(f32[48,16,128]{2,1,0:T(8,128)S(1)} %get-tuple-element.29), channel_id=1, source_target_pairs={{0,1},{1,2},{2,3},{4,5},{5,6},{6,7},{8,9},{9,10},{10,11},{12,13},{... | collective-permute-start | bytes 1179656 | tf_op jit(solution)/shard_map/ppermute | solution.py:26
  276.5 1.3 collective-permute-start.23
  277.8 1.4 collective-permute-done.19
  279.2 2.0 collective-permute-done.22
  281.2 3.8 %collective-permute-done.23 = f32[48,16,128]{2,1,0:T(8,128)S(1)} collective-permute-done((f32[48,16,128]{2,1,0:T(8,128)S(1)}, f32[48,16,128]{2,1,0:T(8,128)S(1)}, u32[]{:S(2)}, u32[]{:S(2)}) %collective-permute-start.23) | collective-permute-done | bytes 393248 | tf_op jit(solution)/shard_map/ppermute | solution.py:26
  285.1 1.2 add_multiply_fusion
  (114 shorter events, 6.6 us)
Async XLA Ops:
  2.1 39.3 %collective-permute-start.3 = (f32[48,16,128]{2,1,0:T(8,128)}, f32[48,16,128]{2,1,0:T(8,128)}, u32[]{:S(2)}, u32[]{:S(2)}) collective-permute-start(f32[48,16,128]{2,1,0:T(8,128)} %get-tuple-element.41), channel_id=1, source_target_pairs={{1,0},{2,1},{3,2},{5,4},{6,5},{7,6},{9,8},{10,9},{11,10},{13,12},{... | collective-permute-start | bytes 1179656 | tf_op jit(solution)/shard_map/ppermute | solution.py:26
  3.3 37.0 %collective-permute-start.2 = (f32[48,16,128]{2,1,0:T(8,128)}, f32[48,16,128]{2,1,0:T(8,128)}, u32[]{:S(2)}, u32[]{:S(2)}) collective-permute-start(f32[48,16,128]{2,1,0:T(8,128)} %get-tuple-element.42), channel_id=1, source_target_pairs={{0,1},{1,2},{2,3},{4,5},{5,6},{6,7},{8,9},{9,10},{10,11},{12,13},{... | collective-permute-start | bytes 1179656 | tf_op jit(solution)/shard_map/ppermute | solution.py:26
  11.0 40.6 %collective-permute-start.1 = (f32[30,32,128]{2,1,0:T(8,128)}, f32[30,32,128]{2,1,0:T(8,128)}, u32[]{:S(2)}, u32[]{:S(2)}) collective-permute-start(f32[30,32,128]{2,1,0:T(8,128)} %get-tuple-element.43), channel_id=1, source_target_pairs={{4,0},{8,4},{12,8},{16,12},{20,16},{24,20},{28,24},{5,1},{9,5},{13... | collective-permute-start | bytes 1474568 | tf_op jit(solution)/shard_map/ppermute | solution.py:26
  13.8 37.8 %collective-permute-start = (f32[30,32,128]{2,1,0:T(8,128)}, f32[30,32,128]{2,1,0:T(8,128)}, u32[]{:S(2)}, u32[]{:S(2)}) collective-permute-start(f32[30,32,128]{2,1,0:T(8,128)} %get-tuple-element.44), channel_id=1, source_target_pairs={{0,4},{4,8},{8,12},{12,16},{16,20},{20,24},{24,28},{1,5},{5,9},{9,... | collective-permute-start | bytes 1474568 | tf_op jit(solution)/shard_map/ppermute | solution.py:26
  22.1 4.4 %copy-start.11 = (f32[6,61]{1,0:T(8,128)S(1)}, f32[6,61]{1,0:T(8,128)}, u32[]{:S(2)}) copy-start(f32[6,61]{1,0:T(8,128)} %param.11) | copy-start | bytes 4396
  22.1 4.6 %copy-start.10 = (f32[6,31]{1,0:T(8,128)S(1)}, f32[6,31]{1,0:T(8,128)}, u32[]{:S(2)}) copy-start(f32[6,31]{1,0:T(8,128)} %param.12) | copy-start | bytes 2236
  22.1 4.7 %copy-start.9 = (f32[6,31]{1,0:T(8,128)S(1)}, f32[6,31]{1,0:T(8,128)}, u32[]{:S(2)}) copy-start(f32[6,31]{1,0:T(8,128)} %param.13) | copy-start | bytes 2236
  22.1 5.2 %copy-start.12 = (s32[32,3]{0,1:T(4,128)S(1)}, s32[32,3]{0,1:T(4,128)}, u32[]{:S(2)}) copy-start(s32[32,3]{0,1:T(4,128)} %param.15) | copy-start | bytes 1156
  22.1 61.4 %all-to-all-start = ((f32[4,36,32,128]{3,2,1,0:T(8,128)}), f32[4,36,32,128]{3,2,1,0:T(8,128)S(1)}, u32[]{:S(2)}, u32[]{:S(2)}) async-start(f32[4,36,32,128]{3,2,1,0:T(8,128)} %pack.1), calls=%async_computation | async-start | bytes 4718592 | tf_op jit(solution)/shard_map/all_to_all | solution.py:322
  25.9 6.2 %copy-start.15 = (s32[6]{0:T(128)S(1)}, s32[6]{0:T(128)}, u32[]{:S(2)}) copy-start(s32[6]{0:T(128)} %param.14) | copy-start | bytes 76
  34.1 3.1 %copy-start.13 = (s32[16]{0:T(128)S(1)}, s32[16]{0:T(128)}, u32[]{:S(2)}) copy-start(s32[16]{0:T(128)} %get-tuple-element.72) | copy-start | bytes 196
  34.1 3.1 %copy-start.14 = (s32[16]{0:T(128)S(1)}, s32[16]{0:T(128)}, u32[]{:S(2)}) copy-start(s32[16]{0:T(128)} %get-tuple-element.73) | copy-start | bytes 196
  34.2 4.3 %copy-start.8 = (f32[112,288]{1,0:T(8,128)S(1)}, f32[112,288]{1,0:T(8,128)}, u32[]{:S(2)}) copy-start(f32[112,288]{1,0:T(8,128)} %copy.63) | copy-start | bytes 387076
  42.5 12.5 %copy-start.4 = (f32[48,32,128]{2,1,0:T(8,128)}, f32[48,32,128]{2,1,0:T(8,128)S(1)}, u32[]{:S(2)}) copy-start(f32[48,32,128]{2,1,0:T(8,128)S(1)} %constant_dynamic-update-slice_fusion) | copy-start | bytes 2359300
  42.6 11.5 %collective-permute-start.5 = (f32[30,32,128]{2,1,0:T(8,128)S(1)}, f32[30,32,128]{2,1,0:T(8,128)S(1)}, u32[]{:S(2)}, u32[]{:S(2)}) collective-permute-start(f32[30,32,128]{2,1,0:T(8,128)S(1)} %get-tuple-element.39), channel_id=1, source_target_pairs={{4,0},{8,4},{12,8},{16,12},{20,16},{24,20},{28,24},{5,1},{9,5},{13... | collective-permute-start | bytes 1474568 | tf_op jit(solution)/shard_map/ppermute | solution.py:26
  44.9 9.2 %collective-permute-start.4 = (f32[30,32,128]{2,1,0:T(8,128)S(1)}, f32[30,32,128]{2,1,0:T(8,128)S(1)}, u32[]{:S(2)}, u32[]{:S(2)}) collective-permute-start(f32[30,32,128]{2,1,0:T(8,128)S(1)} %get-tuple-element.40), channel_id=1, source_target_pairs={{0,4},{4,8},{8,12},{12,16},{16,20},{20,24},{24,28},{1,5},{5,9},{9,... | collective-permute-start | bytes 1474568 | tf_op jit(solution)/shard_map/ppermute | solution.py:26
  54.1 1.0 copy-start.18
  54.1 0.8 copy-start.19
  83.6 1.5 copy-start.2
  124.2 36.4 %copy-start.3 = (f32[48,32,128]{2,1,0:T(8,128)S(1)}, f32[48,32,128]{2,1,0:T(8,128)}, u32[]{:S(2)}) copy-start(f32[48,32,128]{2,1,0:T(8,128)} %param.8) | copy-start | bytes 2359300
  124.2 36.4 %copy-start.7 = (f32[1536,128]{1,0:T(8,128)S(1)}, f32[1536,128]{1,0:T(8,128)}, u32[]{:S(2)}) copy-start(f32[1536,128]{1,0:T(8,128)} %get-tuple-element.17) | copy-start | bytes 2359300
  124.2 13.1 %collective-permute-start.8 = (f32[30,32,128]{2,1,0:T(8,128)}, f32[30,32,128]{2,1,0:T(8,128)S(1)}, u32[]{:S(2)}, u32[]{:S(2)}) collective-permute-start(f32[30,32,128]{2,1,0:T(8,128)} %bitcast.93), channel_id=1, source_target_pairs={{0,4},{4,8},{8,12},{12,16},{16,20},{20,24},{24,28},{1,5},{5,9},{9,... | collective-permute-start | bytes 1474568 | tf_op jit(solution)/shard_map/ppermute | solution.py:26
  128.4 17.3 %collective-permute-start.9 = (f32[30,32,128]{2,1,0:T(8,128)}, f32[30,32,128]{2,1,0:T(8,128)S(1)}, u32[]{:S(2)}, u32[]{:S(2)}) collective-permute-start(f32[30,32,128]{2,1,0:T(8,128)} %bitcast.91), channel_id=1, source_target_pairs={{4,0},{8,4},{12,8},{16,12},{20,16},{24,20},{28,24},{5,1},{9,5},{13... | collective-permute-start | bytes 1474568 | tf_op jit(solution)/shard_map/ppermute | solution.py:26
  130.3 21.3 %collective-permute-start.6 = (f32[30,32,128]{2,1,0:T(8,128)}, f32[30,32,128]{2,1,0:T(8,128)S(1)}, u32[]{:S(2)}, u32[]{:S(2)}) collective-permute-start(f32[30,32,128]{2,1,0:T(8,128)} %bitcast.85), channel_id=1, source_target_pairs={{0,4},{4,8},{8,12},{12,16},{16,20},{20,24},{24,28},{1,5},{5,9},{9,... | collective-permute-start | bytes 1474568 | tf_op jit(solution)/shard_map/ppermute | solution.py:26
  135.4 19.8 %collective-permute-start.7 = (f32[30,32,128]{2,1,0:T(8,128)}, f32[30,32,128]{2,1,0:T(8,128)S(1)}, u32[]{:S(2)}, u32[]{:S(2)}) collective-permute-start(f32[30,32,128]{2,1,0:T(8,128)} %bitcast.83), channel_id=1, source_target_pairs={{4,0},{8,4},{12,8},{16,12},{20,16},{24,20},{28,24},{5,1},{9,5},{13... | collective-permute-start | bytes 1474568 | tf_op jit(solution)/shard_map/ppermute | solution.py:26
  147.1 9.6 %collective-permute-start.10 = (f32[48,16,128]{2,1,0:T(8,128)S(1)}, f32[48,16,128]{2,1,0:T(8,128)S(1)}, u32[]{:S(2)}, u32[]{:S(2)}) collective-permute-start(f32[48,16,128]{2,1,0:T(8,128)S(1)} %get-tuple-element.37), channel_id=1, source_target_pairs={{0,1},{1,2},{2,3},{4,5},{5,6},{6,7},{8,9},{9,10},{10,11},{12,13},{... | collective-permute-start | bytes 1179656 | tf_op jit(solution)/shard_map/ppermute | solution.py:26
  150.3 10.2 %collective-permute-start.11 = (f32[48,16,128]{2,1,0:T(8,128)S(1)}, f32[48,16,128]{2,1,0:T(8,128)S(1)}, u32[]{:S(2)}, u32[]{:S(2)}) collective-permute-start(f32[48,16,128]{2,1,0:T(8,128)S(1)} %get-tuple-element.38), channel_id=1, source_target_pairs={{1,0},{2,1},{3,2},{5,4},{6,5},{7,6},{9,8},{10,9},{11,10},{13,12},{... | collective-permute-start | bytes 1179656 | tf_op jit(solution)/shard_map/ppermute | solution.py:26
  161.0 11.8 %copy-start = (f32[48,32,128]{2,1,0:T(8,128)}, f32[48,32,128]{2,1,0:T(8,128)S(1)}, u32[]{:S(2)}) copy-start(f32[48,32,128]{2,1,0:T(8,128)S(1)} %add_multiply_fusion.1) | copy-start | bytes 2359300
  161.0 10.1 %collective-permute-start.14 = (f32[48,16,128]{2,1,0:T(8,128)S(1)}, f32[48,16,128]{2,1,0:T(8,128)S(1)}, u32[]{:S(2)}, u32[]{:S(2)}) collective-permute-start(f32[48,16,128]{2,1,0:T(8,128)S(1)} %get-tuple-element.34), channel_id=1, source_target_pairs={{0,1},{1,2},{2,3},{4,5},{5,6},{6,7},{8,9},{9,10},{10,11},{12,13},{... | collective-permute-start | bytes 1179656 | tf_op jit(solution)/shard_map/ppermute | solution.py:26
  164.1 8.5 %collective-permute-start.15 = (f32[48,16,128]{2,1,0:T(8,128)S(1)}, f32[48,16,128]{2,1,0:T(8,128)S(1)}, u32[]{:S(2)}, u32[]{:S(2)}) collective-permute-start(f32[48,16,128]{2,1,0:T(8,128)S(1)} %get-tuple-element.33), channel_id=1, source_target_pairs={{1,0},{2,1},{3,2},{5,4},{6,5},{7,6},{9,8},{10,9},{11,10},{13,12},{... | collective-permute-start | bytes 1179656 | tf_op jit(solution)/shard_map/ppermute | solution.py:26
  165.5 15.0 %collective-permute-start.13 = (f32[30,32,128]{2,1,0:T(8,128)S(1)}, f32[30,32,128]{2,1,0:T(8,128)S(1)}, u32[]{:S(2)}, u32[]{:S(2)}) collective-permute-start(f32[30,32,128]{2,1,0:T(8,128)S(1)} %get-tuple-element.35), channel_id=1, source_target_pairs={{4,0},{8,4},{12,8},{16,12},{20,16},{24,20},{28,24},{5,1},{9,5},{13... | collective-permute-start | bytes 1474568 | tf_op jit(solution)/shard_map/ppermute | solution.py:26
  167.5 13.1 %collective-permute-start.12 = (f32[30,32,128]{2,1,0:T(8,128)S(1)}, f32[30,32,128]{2,1,0:T(8,128)S(1)}, u32[]{:S(2)}, u32[]{:S(2)}) collective-permute-start(f32[30,32,128]{2,1,0:T(8,128)S(1)} %get-tuple-element.36), channel_id=1, source_target_pairs={{0,4},{4,8},{8,12},{12,16},{16,20},{20,24},{24,28},{1,5},{5,9},{9,... | collective-permute-start | bytes 1474568 | tf_op jit(solution)/shard_map/ppermute | solution.py:26
  172.7 15.3 %copy-start.5 = (f32[48,32,128]{2,1,0:T(8,128)}, f32[48,32,128]{2,1,0:T(8,128)S(1)}, u32[]{:S(2)}) copy-start(f32[48,32,128]{2,1,0:T(8,128)S(1)} %constant_dynamic-update-slice_fusion.2) | copy-start | bytes 2359300
  172.8 14.3 %collective-permute-start.17 = (f32[30,32,128]{2,1,0:T(8,128)S(1)}, f32[30,32,128]{2,1,0:T(8,128)S(1)}, u32[]{:S(2)}, u32[]{:S(2)}) collective-permute-start(f32[30,32,128]{2,1,0:T(8,128)S(1)} %get-tuple-element.31), channel_id=1, source_target_pairs={{4,0},{8,4},{12,8},{16,12},{20,16},{24,20},{28,24},{5,1},{9,5},{13... | collective-permute-start | bytes 1474568 | tf_op jit(solution)/shard_map/ppermute | solution.py:26
  174.8 12.4 %collective-permute-start.16 = (f32[30,32,128]{2,1,0:T(8,128)S(1)}, f32[30,32,128]{2,1,0:T(8,128)S(1)}, u32[]{:S(2)}, u32[]{:S(2)}) collective-permute-start(f32[30,32,128]{2,1,0:T(8,128)S(1)} %get-tuple-element.32), channel_id=1, source_target_pairs={{0,4},{4,8},{8,12},{12,16},{16,20},{20,24},{24,28},{1,5},{5,9},{9,... | collective-permute-start | bytes 1474568 | tf_op jit(solution)/shard_map/ppermute | solution.py:26
  180.5 7.5 %copy-start.16 = (f32[30,32,128]{2,1,0:T(8,128)}, f32[30,32,128]{2,1,0:T(8,128)S(1)}, u32[]{:S(2)}) copy-start(f32[30,32,128]{2,1,0:T(8,128)S(1)} %collective-permute-done.13) | copy-start | bytes 1474564
  180.5 7.5 %copy-start.17 = (f32[30,32,128]{2,1,0:T(8,128)}, f32[30,32,128]{2,1,0:T(8,128)S(1)}, u32[]{:S(2)}) copy-start(f32[30,32,128]{2,1,0:T(8,128)S(1)} %collective-permute-done.12) | copy-start | bytes 1474564
  187.2 1.0 copy-start.20
  187.2 0.8 copy-start.21
  246.8 38.3 %copy-start.1 = (f32[48,32,128]{2,1,0:T(8,128)S(1)}, f32[48,32,128]{2,1,0:T(8,128)}, u32[]{:S(2)}) copy-start(f32[48,32,128]{2,1,0:T(8,128)} %copy-done) | copy-start | bytes 2359300
  246.8 38.3 %copy-start.6 = (f32[1536,128]{1,0:T(8,128)S(1)}, f32[1536,128]{1,0:T(8,128)}, u32[]{:S(2)}) copy-start(f32[1536,128]{1,0:T(8,128)} %get-tuple-element.23) | copy-start | bytes 2359300
  246.8 16.4 %collective-permute-start.20 = (f32[30,32,128]{2,1,0:T(8,128)}, f32[30,32,128]{2,1,0:T(8,128)S(1)}, u32[]{:S(2)}, u32[]{:S(2)}) collective-permute-start(f32[30,32,128]{2,1,0:T(8,128)} %bitcast.90), channel_id=1, source_target_pairs={{0,4},{4,8},{8,12},{12,16},{16,20},{20,24},{24,28},{1,5},{5,9},{9,... | collective-permute-start | bytes 1474568 | tf_op jit(solution)/shard_map/ppermute | solution.py:26
  250.1 21.3 %collective-permute-start.21 = (f32[30,32,128]{2,1,0:T(8,128)}, f32[30,32,128]{2,1,0:T(8,128)S(1)}, u32[]{:S(2)}, u32[]{:S(2)}) collective-permute-start(f32[30,32,128]{2,1,0:T(8,128)} %bitcast.88), channel_id=1, source_target_pairs={{4,0},{8,4},{12,8},{16,12},{20,16},{24,20},{28,24},{5,1},{9,5},{13... | collective-permute-start | bytes 1474568 | tf_op jit(solution)/shard_map/ppermute | solution.py:26
  252.0 25.8 %collective-permute-start.18 = (f32[30,32,128]{2,1,0:T(8,128)}, f32[30,32,128]{2,1,0:T(8,128)S(1)}, u32[]{:S(2)}, u32[]{:S(2)}) collective-permute-start(f32[30,32,128]{2,1,0:T(8,128)} %bitcast.82), channel_id=1, source_target_pairs={{0,4},{4,8},{8,12},{12,16},{16,20},{20,24},{24,28},{1,5},{5,9},{9,... | collective-permute-start | bytes 1474568 | tf_op jit(solution)/shard_map/ppermute | solution.py:26
  261.2 18.0 %collective-permute-start.19 = (f32[30,32,128]{2,1,0:T(8,128)}, f32[30,32,128]{2,1,0:T(8,128)S(1)}, u32[]{:S(2)}, u32[]{:S(2)}) collective-permute-start(f32[30,32,128]{2,1,0:T(8,128)} %bitcast.80), channel_id=1, source_target_pairs={{4,0},{8,4},{12,8},{16,12},{20,16},{24,20},{28,24},{5,1},{9,5},{13... | collective-permute-start | bytes 1474568 | tf_op jit(solution)/shard_map/ppermute | solution.py:26
  272.7 8.5 %collective-permute-start.22 = (f32[48,16,128]{2,1,0:T(8,128)S(1)}, f32[48,16,128]{2,1,0:T(8,128)S(1)}, u32[]{:S(2)}, u32[]{:S(2)}) collective-permute-start(f32[48,16,128]{2,1,0:T(8,128)S(1)} %get-tuple-element.29), channel_id=1, source_target_pairs={{0,1},{1,2},{2,3},{4,5},{5,6},{6,7},{8,9},{9,10},{10,11},{12,13},{... | collective-permute-start | bytes 1179656 | tf_op jit(solution)/shard_map/ppermute | solution.py:26
  276.5 8.5 %collective-permute-start.23 = (f32[48,16,128]{2,1,0:T(8,128)S(1)}, f32[48,16,128]{2,1,0:T(8,128)S(1)}, u32[]{:S(2)}, u32[]{:S(2)}) collective-permute-start(f32[48,16,128]{2,1,0:T(8,128)S(1)} %get-tuple-element.30), channel_id=1, source_target_pairs={{1,0},{2,1},{3,2},{5,4},{6,5},{7,6},{9,8},{10,9},{11,10},{13,12},{... | collective-permute-start | bytes 1179656 | tf_op jit(solution)/shard_map/ppermute | solution.py:26

commit v2 on v0

v2 whole, which is shorter than its diff:
```python
import functools

import jax
import jax.numpy as jnp
from jax import lax
from jax.experimental import pallas as pl
from jax.experimental.pallas import tpu as pltpu
from jax.sharding import PartitionSpec as P

ITERS = 2
F32 = jnp.float32
BF16 = jnp.bfloat16
VMEM_LIMIT = 36 * 1024 * 1024


def round_up(value, unit):
    return -(-value // unit) * unit


def exchange(low, high, axis):
    count = lax.axis_size(axis)
    even = lax.axis_index(axis) % 2 == 0
    rounds = [
        [pair for i in range(begin, count - 1, 2) for pair in ((i, i + 1), (i + 1, i))]
        for begin in (0, 1)
    ]
    a = lax.ppermute(jnp.where(even, high, low), axis, rounds[0])
    b = lax.ppermute(jnp.where(even, low, high), axis, rounds[1])
    return jnp.where(even, b, a), jnp.where(even, a, b)


def halves(value):
    high = value.astype(BF16)
    low = (value - high.astype(F32)).astype(BF16)
    return high, low


def stack(value):
    top, rest = halves(value)
    return jnp.concatenate([top, rest, top], axis=0)


def update_kernel(plan, *refs):
    refs = list(refs)
    take = lambda n: [refs.pop(0) for _ in range(n)]
    depth, rows, side, reach, zpad = plan.depth, plan.rows, plan.side, plan.reach, plan.zpad
    width = plan.width
    total = rows + side
    pitch_y = total + 2
    if plan.forward:
        c, clo, chi, s, slo, shi, wzf, wyf, wxf = take(9)
    if plan.upright_back:
        obs_u, wzb_u = take(2)
    if plan.turned_back:
        obs_t, wzb_t = take(2)
        if not plan.forward:
            (blur_in,) = take(1)
            acc = take(6)
    wxb, wyb = take(2)
    if plan.turned_back:
        outs = take(6)
    else:
        outs = take(6)
        (blur_out,) = take(1)
    if plan.forward:
        (mid,) = take(1)
    (back,) = take(1)
    copies = []
    if plan.turned_back and not plan.forward:
        held = take(6)
        (arrived,) = take(1)
        copies = [
            pltpu.make_async_copy(x, y, arrived.at[i]) for i, (x, y) in enumerate(zip(acc, held))
        ]
        acc = held

        @pl.when(pl.program_id(0) == 0)
        def _():
            for copy in copies:
                copy.start()

    step = pl.program_id(0)
    first = 1 if plan.forward else 0
    n_up = plan.upright if (plan.forward) else 0
    n_all = n_up + plan.turned
    lines = plan.lines
    pitch_z = lines + 8
    group = plan.group

    if plan.forward:

        @pl.when(step == 0)
        def _():
            fill = jnp.zeros((zpad - reach, width), F32)

            def column(low, centre, high, y, n):
                return jnp.concatenate(
                    [
                        low[pl.ds(y, reach, stride=n), :],
                        fill,
                        centre[pl.ds(y, depth, stride=n), :],
                        high[pl.ds(y, reach, stride=n), :],
                        fill,
                    ],
                    axis=0,
                )

            def run(low, centre, high, n, base):
                def body(i, carry):
                    both = jnp.concatenate(
                        [column(low, centre, high, 2 * i + j, n) for j in range(2)], axis=1
                    )
                    result = jnp.dot(wzf[...], stack(both), preferred_element_type=F32)
                    for j in range(2):
                        mid[pl.ds(base + 2 * i + j, n_all * depth, stride=pitch_y), :] = result[
                            :, j * width : (j + 1) * width
                        ]
                    return carry

                lax.fori_loop(0, n // 2, body, 0, unroll=8)

            run(clo, c, chi, rows, 0)
            run(slo, s, shi, side, rows)

    def blur_lines(view, i):
        start = (view * depth + i * group) * pitch_y
        pieces = []
        for j in range(group // 2):
            at = start + 2 * j * pitch_y
            both = jnp.concatenate(
                [mid[pl.ds(at, total), :], mid[pl.ds(at + pitch_y, total), :]], axis=1
            )
            top, rest = halves(both)
            result = jnp.dot(
                wyf[0], jnp.concatenate([top, rest], axis=0), preferred_element_type=F32
            )
            result = result[:rows] + result[rows:]
            pieces += [result[:, :width], result[:, width:]]
        top, rest = halves(jnp.concatenate(pieces, axis=0))
        result = jnp.dot(
            jnp.concatenate([top, rest], axis=1), wxf[0], preferred_element_type=F32
        )
        return result[:, :width] + result[:, width:]

    def spread_lines(slot, i, ratio):
        top, rest = halves(ratio)
        flat = jnp.dot(jnp.concatenate([top, rest], axis=1), wxb[0], preferred_element_type=F32)
        flat = flat[:, :width] + flat[:, width:]
        for j in range(group // 2):
            both = jnp.concatenate(
                [flat[(2 * j + k) * rows : (2 * j + k + 1) * rows] for k in range(2)], axis=1
            )
            result = jnp.dot(wyb[0], stack(both), preferred_element_type=F32)
            for k in range(2):
                line = slot * depth + i * group + 2 * j + k
                back[pl.ds(line, total, stride=pitch_z), :] = result[
                    :, k * width : (k + 1) * width
                ]

    def turned_lines(i):
        per = plan.per
        blocks = []
        for g in range(group // per):
            at = i * (group // per) + g
            blocks.append(jnp.concatenate([obs_t[k, at] for k in range(plan.count)], axis=0).T)
        return jnp.concatenate(blocks, axis=0)

    size = group * rows
    window = lambda i: pl.ds(pl.multiple_of(i * size, size), size)

    def loop(body):
        def wrapped(i, carry):
            body(i)
            return carry

        lax.fori_loop(0, depth // group, wrapped, 0, unroll=plan.unroll)

    if plan.upright_back:

        @pl.when((step >= first) & (step < first + n_up))
        def _():
            view = step - first

            def body(i):
                spread_lines(view, i, obs_u[0, window(i), :] / blur_lines(view, i))

            loop(body)

    @pl.when((step >= first + n_up) & (step < first + n_all))
    def _():
        view = step - first

        def body(i):
            blurred = blur_lines(view, i) if plan.forward else blur_in[0, window(i), :]
            if plan.turned_back:
                spread_lines(view, i, turned_lines(i) / blurred)
            else:
                blur_out[0, window(i), :] = blurred

        loop(body)

    @pl.when(step == first + n_all)
    def _():
        for copy in copies:
            copy.wait()
        banks = []
        if plan.upright_back:
            banks.append((wzb_u, 0, plan.upright * depth))
        if plan.turned_back:
            banks.append((wzb_t, n_up * depth, plan.turned * depth))

        def run(region, targets, adds, n, base, begin, end):
            def body(i, carry):
                at = (base + 2 * i) * pitch_z
                result = None
                for weights, offset, count in banks:
                    both = jnp.concatenate(
                        [back[pl.ds(at + j * pitch_z + offset, count), :] for j in range(2)],
                        axis=1,
                    )
                    term = jnp.dot(weights[region], stack(both), preferred_element_type=F32)
                    result = term if result is None else result + term
                for j in range(2):
                    part = result[:, j * width : (j + 1) * width]
                    for target, add, low, count in zip(
                        targets, adds, (zpad, 0, zpad + depth), (depth, reach, reach)
                    ):
                        spot = (pl.ds(2 * i + j, count, stride=n), slice(None))
                        piece = part[low : low + count]
                        if add is not None:
                            piece = piece + add[spot]
                        target[spot] = piece
                return carry

            lax.fori_loop(begin, end, body, 0, unroll=4)

        adds = acc if (plan.turned_back and not plan.forward) else [None] * 6
        run(0, outs[3:], adds[3:], side, rows, 0, side // 4)
        run(2, outs[3:], adds[3:], side, rows, side // 4, side // 2)
        run(1, outs[:3], adds[:3], rows, 0, 0, rows // 2)


class Plan:
    def __init__(self, **fields):
        self.__dict__.update(fields)


def update(plan, **a):
    first = 1 if plan.forward else 0
    n_up = plan.upright if plan.forward else 0
    n_all = n_up + plan.turned
    used = (plan.upright if plan.upright_back else 0) + (plan.turned if plan.turned_back else 0)
    plan.lines = used * plan.depth
    total = plan.rows + plan.side
    shift = plan.upright - n_up
    once = pl.Buffered(1)

    def whole(x):
        return pl.BlockSpec(x.shape, lambda i: (0,) * len(x.shape), pipeline_mode=once)

    def per_view(x, start, count, offset=0):
        return pl.BlockSpec(
            (1,) + x.shape[1:],
            lambda i: (jnp.clip(i - start, 0, count - 1) + offset,) + (0,) * (len(x.shape) - 1),
        )

    args, specs = [], []

    def give(x, spec):
        args.append(x)
        specs.append(spec)

    if plan.forward:
        for x in a["volumes"]:
            give(x, whole(x))
        give(a["wzf"], whole(a["wzf"]))
        give(a["wyf"], per_view(a["wyf"], first, n_all))
        give(a["wxf"], per_view(a["wxf"], first, n_all))
    if plan.upright_back:
        give(a["obs_u"], per_view(a["obs_u"], first, plan.upright))
        give(a["wzb_u"], whole(a["wzb_u"]))
    if plan.turned_back:
        x = a["obs_t"]
        begin = first + n_up
        give(
            x,
            pl.BlockSpec(
                (x.shape[0], x.shape[1] // plan.turned) + x.shape[2:],
                lambda i: (0, jnp.clip(i - begin, 0, plan.turned - 1), 0, 0),
            ),
        )
        give(a["wzb_t"], whole(a["wzb_t"]))
        if not plan.forward:
            give(a["blurred"], per_view(a["blurred"], begin, plan.turned))
            for x in a["acc"]:
                give(x, pl.BlockSpec(memory_space=pl.ANY))
    backs = plan.upright if not plan.turned_back else n_all
    give(a["wxb"], per_view(a["wxb"], first, backs, shift))
    give(a["wyb"], per_view(a["wyb"], first, backs, shift))

    shapes = [
        jax.ShapeDtypeStruct((count * n, plan.width), F32)
        for n in (plan.rows, plan.side)
        for count in (plan.depth, plan.reach, plan.reach)
    ]
    out_specs = [whole(x) for x in shapes]
    if not plan.turned_back:
        x = jax.ShapeDtypeStruct((plan.turned, plan.depth * plan.rows, plan.width), F32)
        shapes.append(x)
        out_specs.append(per_view(x, first + n_up, plan.turned))
    scratch = []
    if plan.forward:
        scratch.append(pltpu.VMEM((n_all * plan.depth * (total + 2), plan.width), F32))
    scratch.append(pltpu.VMEM((total * (plan.lines + 8), plan.width), F32))
    if plan.turned_back and not plan.forward:
        scratch += [pltpu.VMEM(x.shape, F32) for x in a["acc"]]
        scratch.append(pltpu.SemaphoreType.DMA((len(a["acc"]),)))
    return pl.pallas_call(
        functools.partial(update_kernel, plan),
        out_shape=shapes,
        grid=(first + n_all + 1,),
        in_specs=specs,
        out_specs=out_specs,
        scratch_shapes=scratch,
        compiler_params=pltpu.CompilerParams(vmem_limit_bytes=plan.vmem),
        cost_estimate=pl.CostEstimate(
            flops=10**10, bytes_accessed=12 * 10**6, transcendentals=0
        ),
        name=plan.name,
    )(*args)


def pack_kernel(count, per, x, out):
    rows = x.shape[-1] // count
    for g in range(x.shape[0] // per):
        for d in range(count):
            out[d, g] = jnp.concatenate(
                [x[g * per + j, :, d * rows : (d + 1) * rows] for j in range(per)], axis=1
            )


def pack(turned, count, per):
    planes, xl, yf = turned.shape
    block = 48 if planes % 48 == 0 else per
    return pl.pallas_call(
        functools.partial(pack_kernel, count, per),
        out_shape=jax.ShapeDtypeStruct((count, planes // per, xl, per * (yf // count)), F32),
        grid=(planes // block,),
        in_specs=[pl.BlockSpec((block, xl, yf), lambda i: (i, 0, 0))],
        out_specs=pl.BlockSpec(
            (count, block // per, xl, per * (yf // count)), lambda i: (0, i, 0, 0)
        ),
        compiler_params=pltpu.CompilerParams(vmem_limit_bytes=VMEM_LIMIT),
        name="pack",
    )(turned)


def bands_kernel(plan, place, views_of, shift_x, kd, kr, kc, wzf, wyf, wxf, wxb, wyb, wzu, wzt):
    depth, rows, side, reach, zpad = plan.depth, plan.rows, plan.side, plan.reach, plan.zpad
    width = plan.width
    ypad = side // 2
    gap = zpad - reach
    active = views_of.shape[1]

    def taps(ref, v):
        row = ref[v : v + 1, :]
        row = row / jnp.sum(row, axis=1, keepdims=True)
        return jnp.concatenate([row, jnp.zeros((1, width - row.shape[1]), F32)], axis=1)

    def slide(row, height, amount):
        base = jnp.broadcast_to(row, (height, width))
        return pltpu.roll(base, amount, 1, stride=1, stride_axis=0)

    def parts(matrix):
        high = matrix.astype(BF16).astype(F32)
        return high, matrix - high

    def turn(matrix):
        rows_in, cols_in = matrix.shape
        square = jnp.concatenate([matrix, jnp.zeros((width - rows_in, cols_in), F32)], axis=0)
        square = jnp.concatenate([square, jnp.zeros((width, width - cols_in), F32)], axis=1)
        return square.T[:cols_in, :rows_in]

    def share(i, j, v):
        z = jnp.clip(place[0] + i - 1, 0, plan.n_gz - 1)
        y = jnp.clip(place[1] + j - 1, 0, plan.count - 1)
        found = jnp.int32(0)
        for k in range(active):
            found = found + (views_of[z * plan.count + y, k] == v).astype(jnp.int32)
        return found.astype(F32) / active

    place_z = lax.broadcasted_iota(jnp.int32, (depth + 2 * zpad, depth), 0)
    kept = []
    for v in range(plan.upright + plan.turned):
        wide = slide(taps(kd, v), depth, 0)
        zeros = jnp.zeros((depth, gap), F32)
        band = jnp.concatenate(
            [
                wide[:, :reach],
                zeros,
                wide[:, reach : reach + depth],
                wide[:, reach + depth : 2 * reach + depth],
                zeros,
            ],
            axis=1,
        )
        high, low = parts(band)
        wzf[v * depth : (v + 1) * depth, :] = jnp.concatenate([high, high, low], axis=1).astype(
            BF16
        )
        kept.append(turn(band))

        wide = slide(taps(kr, v), rows, ypad - plan.reach_y)
        band = jnp.concatenate(
            [wide[:, ypad : ypad + rows], wide[:, :ypad], wide[:, ypad + rows : 2 * ypad + rows]],
            axis=1,
        )
        high, low = parts(band)
        wyf[v] = jnp.concatenate(
            [
                jnp.concatenate([high, high], axis=1),
                jnp.concatenate([low, jnp.zeros_like(low)], axis=1),
            ],
            axis=0,
        ).astype(BF16)
        high, low = parts(turn(band))
        wyb[v] = jnp.concatenate([high, high, low], axis=1).astype(BF16)

        offset = plan.reach_x + shift_x[v]
        index = (
            lax.broadcasted_iota(jnp.int32, (width, width), 1)
            - lax.broadcasted_iota(jnp.int32, (width, width), 0)
            + offset
        )
        wide = pltpu.roll(slide(taps(kc, v), width, 0), width - offset, 1)
        band = jnp.where((index >= 0) & (index < kc.shape[1]), wide, 0.0)
        for out, matrix in ((wxb, band), (wxf, band.T)):
            high, low = parts(matrix)
            out[v, :width, :width] = high.astype(BF16)
            out[v, :width, width:] = low.astype(BF16)
            out[v, width:, :width] = high.astype(BF16)
            out[v, width:, width:] = jnp.zeros_like(low).astype(BF16)

    for out, begin, count in ((wzu, 0, plan.upright), (wzt, plan.upright, plan.turned)):
        for j in range(3):
            pieces = []
            for v in range(begin, begin + count):
                scale = jnp.where(
                    place_z < zpad,
                    share(0, j, v),
                    jnp.where(place_z < zpad + depth, share(1, j, v), share(2, j, v)),
                )
                pieces.append(kept[v] * scale)
            high, low = parts(jnp.concatenate(pieces, axis=1))
            out[j] = jnp.concatenate([high, high, low], axis=1).astype(BF16)


def bands(plan, place, views_of, shift_x, kd, kr, kc):
    views = plan.upright + plan.turned
    tall = plan.depth + 2 * plan.zpad
    total = plan.rows + plan.side
    shapes = [
        (views * plan.depth, 3 * tall),
        (views, 2 * plan.rows, 2 * total),
        (views, 2 * plan.width, 2 * plan.width),
        (views, 2 * plan.width, 2 * plan.width),
        (views, total, 3 * plan.rows),
        (3, tall, 3 * plan.upright * plan.depth),
        (3, tall, 3 * plan.turned * plan.depth),
    ]
    smem = pl.BlockSpec(memory_space=pltpu.SMEM)
    vmem = pl.BlockSpec(memory_space=pltpu.VMEM)
    return pl.pallas_call(
        functools.partial(bands_kernel, plan),
        out_shape=[jax.ShapeDtypeStruct(x, BF16) for x in shapes],
        in_specs=[smem] * 3 + [vmem] * 3,
        out_specs=[vmem] * len(shapes),
        compiler_params=pltpu.CompilerParams(vmem_limit_bytes=plan.vmem),
        name=plan.name,
    )(place, views_of, shift_x, kd, kr, kc)


def local(
    prior_estimate,
    views_upright,
    views_turned,
    kernel_depth,
    kernel_rows,
    kernel_columns,
    lateral_offsets,
    block_views,
):
    depth, rows, width = prior_estimate.shape
    views = kernel_depth.shape[0]
    reach = (kernel_depth.shape[1] - 1) // 2
    reach_y = (kernel_rows.shape[1] - 1) // 2
    reach_x = (kernel_columns.shape[1] - 1) // 2
    zpad = round_up(reach, 16)
    ypad = round_up(reach_y, 8)
    side = 2 * ypad
    n_xy = lax.axis_size("xy")
    n_gz = lax.axis_size("gz")

    half = views_turned.shape[0]
    per = width // rows
    packed = pack(
        views_turned.reshape(half * depth, views_turned.shape[2], views_turned.shape[3]), n_xy, per
    )
    upright = views_upright.reshape(views - half, depth * rows, width)

    n_up = views - half
    common = dict(
        depth=depth,
        rows=rows,
        side=side,
        reach=reach,
        zpad=zpad,
        width=width,
        upright=n_up,
        turned=half,
        per=per,
        count=n_xy,
        group=8,
        unroll=depth // 8,
    )
    plan = Plan(
        name="bands", vmem=56 << 20, n_gz=n_gz, reach_y=reach_y, reach_x=reach_x, **common
    )
    place = jnp.stack([lax.axis_index("gz"), lax.axis_index("xy")]).astype(jnp.int32)
    wz_f, wy_f, wx_f, wx_b, wy_b, wzb_u, wzb_t = bands(
        plan, place, block_views, lateral_offsets, kernel_depth, kernel_rows, kernel_columns
    )
    flat = lambda x: x.reshape(-1, width)
    cube = lambda x, n: x.reshape(-1, n, width)
    head = ((0, depth - reach), (0, 0), (0, 0))
    tail = ((depth - reach, 0), (0, 0), (0, 0))
    back = dict(wxb=wx_b, wyb=wy_b)
    ahead = dict(wzf=wz_f, wyf=wy_f, wxf=wx_f)
    estimate = prior_estimate
    for iteration in range(ITERS):
        from_left, from_right = exchange(
            estimate[:, :ypad], estimate[:, rows - ypad :], "xy"
        )
        source = estimate
        if iteration == 0:
            packed, source, from_left, from_right = lax.optimization_barrier(
                (packed, estimate, from_left, from_right)
            )
            received = lax.all_to_all(packed, "xy", split_axis=0, concat_axis=0, tiled=True)
        below, above = exchange(source[:reach], source[depth - reach :], "gz")
        sides = jnp.concatenate([from_left, from_right], axis=1)
        side_below, side_above = exchange(sides[:reach], sides[depth - reach :], "gz")
        volumes = [flat(x) for x in (estimate, below, above, sides, side_below, side_above)]
        if iteration == 0:
            *acc, blurred = update(
                Plan(
                    name="first", vmem=56 << 20, forward=True, upright_back=True, turned_back=False, **common
                ),
                volumes=volumes,
                obs_u=upright,
                wzb_u=wzb_u,
                **ahead,
                **back,
            )
            parts = update(
                Plan(
                    name="second", vmem=56 << 20, forward=False, upright_back=False, turned_back=True, **common
                ),
                obs_t=received,
                wzb_t=wzb_t,
                blurred=blurred,
                acc=acc,
                **back,
            )
        else:
            parts = update(
                Plan(name="both", vmem=36 << 20, forward=True, upright_back=True, turned_back=True, **common),
                volumes=volumes,
                obs_u=upright,
                obs_t=received,
                wzb_u=wzb_u,
                wzb_t=wzb_t,
                **ahead,
                **back,
            )
        cc, clo, chi = (cube(x, rows) for x in parts[:3])
        sc, slo, shi = (cube(x, side) for x in parts[3:])
        s_low, s_high = exchange(slo, shi, "gz")
        c_low, c_high = exchange(clo, chi, "gz")
        sc = sc + jnp.pad(s_low, head) + jnp.pad(s_high, tail)
        from_left, from_right = exchange(sc[:, :ypad], sc[:, ypad:], "xy")
        cc = cc + jnp.pad(c_low, head) + jnp.pad(c_high, tail)
        cc = cc + jnp.pad(from_left, ((0, 0), (0, rows - ypad), (0, 0)))
        cc = cc + jnp.pad(from_right, ((0, 0), (rows - ypad, 0), (0, 0)))
        estimate = estimate * cc
    return estimate


def solution(mesh):
    in_specs = (
        P("gz", "xy", None),
        P(None, "gz", "xy", None),
        P(None, "gz", "xy", None),
        P(),
        P(),
        P(),
        P(),
        P(),
    )
    out_specs = P("gz", "xy", None)
    return jax.shard_map(local, mesh=mesh, in_specs=in_specs, out_specs=out_specs, check_vma=False)
```

time: 378 us -> 206 us (0.54)
  matrix products: 152 us -> 0 us
  Pallas kernels: 0 us -> 73.8 us
  local copies, waits for them, and re-layouts: 55.5 us -> 4.97 us
  waiting for transfers between devices: 94 us -> 50.6 us
  starting transfers between devices: 48.3 us -> 59.3 us
  other arithmetic: 19.7 us -> 14 us
    dot_general x75 -> x0, matrix products: 152 us -> none  [the longest x12 64.8 us: local(): jnp.einsum('je,jyx->eyx', forward_depth[number], spread, precision=exact_...]
    pallas_call x0 -> x5, Pallas kernels: none -> 73.8 us  [the longest x3 63.7 us: update(): pl.pallas_call(functools.partial(update_kernel, plan), out_shape=shapes,...]
    ppermute x16 -> x24, waiting for transfers between devices: 94 us -> 50.6 us  [the longest x12 44.4 us: exchange(): b = lax.ppermute(jnp.where(even, low, high), axis, rounds[1])]
    unnamed x115 -> x36, local copies, waits for them, and re-layouts: 23.8 us -> 4.93 us
    all_to_all x3 -> x0, local copies, waits for them, and re-layouts: 17.6 us -> none  [local(): lax.all_to_all(views_turned, 'xy', split_axis=3, concat_axis=2, tiled=True)]
    select_n x0 -> x23, other arithmetic: none -> 11.4 us  [the longest x12 4.86 us: exchange(): return (jnp.where(even, b, a), jnp.where(even, a, b))]
    all_to_all x1 -> x0, other arithmetic: 9.65 us -> none  [local(): lax.all_to_all(views_turned, 'xy', split_axis=3, concat_axis=2, tiled=True)]
    ppermute x16 -> x24, starting transfers between devices: 43.5 us -> 53.1 us  [the longest x12 38.1 us: exchange(): b = lax.ppermute(jnp.where(even, low, high), axis, rounds[1])]
  transfers between devices with their start and end apart: 17 -> 25, of which waited for: 14 -> 9; matrix products, arithmetic and copies ran while one was open for 22% -> 5% of each run, Pallas kernels for 0% -> 17%
where the time goes in v2:
time: 206 us; the launch traced here: 203 us
  Pallas kernels  73.8 us (36%)
  starting transfers between devices  59.3 us (29%)
  waiting for transfers between devices  50.6 us (25%)
  other arithmetic  14 us (7%)
  local copies, waits for them, and re-layouts  4.97 us (2%)
    pallas_call x3, Pallas kernels, update(): pl.pallas_call(functools.partial(update_kernel, plan), out_shape=shapes,...  63.7 us
    ppermute x12, waiting for transfers between devices, exchange(): b = lax.ppermute(jnp.where(even, low, high), axis, rounds[1])  44.4 us
    ppermute x12, starting transfers between devices, exchange(): b = lax.ppermute(jnp.where(even, low, high), axis, rounds[1])  38.1 us
    ppermute x12, starting transfers between devices, exchange(): a = lax.ppermute(jnp.where(even, high, low), axis, rounds[0])  15 us
    pallas_call x1, Pallas kernels, bands(): pl.pallas_call(functools.partial(bands_kernel, plan), out_shape=[jax.Shap...  7.04 us
    all_to_all x1, starting transfers between devices, local(): lax.all_to_all(packed, 'xy', split_axis=0, concat_axis=0, tiled=True)  6.28 us
    ppermute x12, waiting for transfers between devices, exchange(): a = lax.ppermute(jnp.where(even, high, low), axis, rounds[0])  6.25 us
    unnamed x36, local copies, waits for them, and re-layouts  4.93 us
  transfers between devices with their start and end apart: 25, of which 9 were waited for; matrix products, arithmetic and copies ran while one was open for 5% of the time, Pallas kernels for 17%

profile of v2, /device:TPU:1, one launch (start us, length us, event | category | flops | bytes accessed | tf_op | source)
XLA Modules:
  0.0 203.5 jit_solution(5293546729517415545)
XLA Ops:
  0.0 1.2 slice_select_fusion.12
  1.2 2.2 %collective-permute-start.1 = (f32[48,16,128]{2,1,0:T(8,128)S(1)}, f32[48,16,128]{2,1,0:T(8,128)S(1)}, u32[]{:S(2)}, u32[]{:S(2)}) collective-permute-start(f32[48,16,128]{2,1,0:T(8,128)S(1)} %get-tuple-element.111), channel_id=1, source_target_pairs={{0,1},{1,0},{2,3},{3,2},{4,5},{5,4},{6,7},{7,6},{8,9},{9,8},{10,11... | collective-permute-start | bytes 1179656 | tf_op jit(solution)/shard_map/ppermute | solution.py:27
  3.4 0.7 collective-permute-start
  4.1 1.7 copy-done
  5.7 3.1 %pack.1 = f32[4,36,32,128]{3,2,1,0:T(8,128)} custom-call(f32[144,32,128]{2,1,0:T(8,128)S(1)} %bitcast.29), custom_call_target="tpu_custom_call" | custom-call | tf_op jit(solution)/shard_map/pack/pallas_call | solution.py:345
  8.9 3.3 %collective-permute-done.1 = f32[48,16,128]{2,1,0:T(8,128)S(1)} collective-permute-done((f32[48,16,128]{2,1,0:T(8,128)S(1)}, f32[48,16,128]{2,1,0:T(8,128)S(1)}, u32[]{:S(2)}, u32[]{:S(2)}) %collective-permute-start.1) | collective-permute-done | bytes 393248 | tf_op jit(solution)/shard_map/ppermute | solution.py:27
  12.2 0.8 broadcast_select_fusion.32
  13.0 6.3 %all-to-all-start = ((f32[4,36,32,128]{3,2,1,0:T(8,128)}), f32[4,36,32,128]{3,2,1,0:T(8,128)S(1)}, u32[]{:S(2)}, u32[]{:S(2)}) async-start(f32[4,36,32,128]{3,2,1,0:T(8,128)} %pack.1), calls=%async_computation | async-start | bytes 4718592 | tf_op jit(solution)/shard_map/all_to_all | solution.py:549
  19.3 1.1 constant_dynamic-update-slice_fusion.1
  20.5 1.2 slice_select_fusion.2
  21.7 2.1 %collective-permute-start.5 = (f32[30,32,128]{2,1,0:T(8,128)}, f32[30,32,128]{2,1,0:T(8,128)}, u32[]{:S(2)}, u32[]{:S(2)}) collective-permute-start(f32[30,32,128]{2,1,0:T(8,128)} %get-tuple-element.105), channel_id=1, source_target_pairs={{0,4},{4,0},{8,12},{12,8},{16,20},{20,16},{24,28},{28,24},{1,5},{5... | collective-permute-start | bytes 1474568 | tf_op jit(solution)/shard_map/ppermute | solution.py:27
  23.8 3.0 %collective-permute-start.4 = (f32[30,32,128]{2,1,0:T(8,128)}, f32[30,32,128]{2,1,0:T(8,128)}, u32[]{:S(2)}, u32[]{:S(2)}) collective-permute-start(f32[30,32,128]{2,1,0:T(8,128)} %get-tuple-element.106), channel_id=1, source_target_pairs={{4,8},{8,4},{12,16},{16,12},{20,24},{24,20},{5,9},{9,5},{13,17},{1... | collective-permute-start | bytes 1474568 | tf_op jit(solution)/shard_map/ppermute | solution.py:28
  26.8 1.1 slice_select_fusion.4
  28.0 3.5 %collective-permute-start.2 = (f32[30,32,128]{2,1,0:T(8,128)}, f32[30,32,128]{2,1,0:T(8,128)S(1)}, u32[]{:S(2)}, u32[]{:S(2)}) collective-permute-start(f32[30,32,128]{2,1,0:T(8,128)} %get-tuple-element.108), channel_id=1, source_target_pairs={{4,8},{8,4},{12,16},{16,12},{20,24},{24,20},{5,9},{9,5},{13,17},{1... | collective-permute-start | bytes 1474568 | tf_op jit(solution)/shard_map/ppermute | solution.py:28
  31.5 0.7 copy.9.views_of
  32.2 0.7 pad_add_fusion.2.place
  32.8 7.0 %bands.1 = (bf16[288,336]{1,0:T(8,128)(2,1)}, bf16[6,64,128]{2,1,0:T(8,128)(2,1)}, bf16[6,256,256]{2,1,0:T(8,128)(2,1)}, bf16[6,256,256]{2,1,0:T(8,128)(2,1)}, b...) custom-call(s32[2]{0:T(128)} %pad_add_fusion.2.place, ...), custom_call_target="tpu_custom_call" | custom-call | tf_op jit(solution)/shard_map/bands/pallas_call | solution.py:473
  39.9 2.2 %broadcast_select_fusion.22 = (f32[30,32,128]{2,1,0:T(8,128)}, f32[30,32,128]{2,1,0:T(8,128)}) fusion(f32[30,32,128]{2,1,0:T(8,128)} %collective-permute-done.5, f32[30,32,128]{2,1,0:T(8,128)} %collective-permute-done.4, pred[]{:T(512)S(6)} %eq.30), kind=kLoop, calls=%fused_computation.47 | loop fusion | flops 245760 | bytes 1966081 | tf_op jit(solution)/shard_map/jit(_where)/select_n | solution.py:29
  42.1 7.6 %collective-permute-done.2 = f32[30,32,128]{2,1,0:T(8,128)S(1)} collective-permute-done((f32[30,32,128]{2,1,0:T(8,128)}, f32[30,32,128]{2,1,0:T(8,128)S(1)}, u32[]{:S(2)}, u32[]{:S(2)}) %collective-permute-start.2) | collective-permute-done | bytes 491552 | tf_op jit(solution)/shard_map/ppermute | solution.py:28
  49.7 1.1 broadcast_select_fusion.24
  50.8 24.6 %first.1 = (f32[1536,128]{1,0:T(8,128)}, f32[960,128]{1,0:T(8,128)}, f32[960,128]{1,0:T(8,128)}, f32[1536,128]{1,0:T(8,128)}, f32[960,128]{1,0:T(8,128)}, /*index=5*/f32[960,128]{1,0:T(8,128)}, f32[3,1536,128]{2,1,0:T(8,128)}) custom-call(f32[1536,128]{1,0:T(8,128)} %bitcast.39, f32[960,128]{1,0:T(8,128)} %bitcast.54, f32[960,128]{1,0:T(8,128)} %bitcast.53, ...), custom_call_target="tpu_custom_call" | custom-call | flops 10000000000 | bytes 12000000 | tf_op jit(solution)/shard_map/first/pallas_call | solution.py:318
  75.4 1.4 copy-done.1
  76.8 12.3 %second.1 = (f32[1536,128]{1,0:T(8,128)}, f32[960,128]{1,0:T(8,128)}, f32[960,128]{1,0:T(8,128)}, f32[1536,128]{1,0:T(8,128)}, f32[960,128]{1,0:T(8,128)}, /*index=5*/f32[960,128]{1,0:T(8,128)}) custom-call(f32[4,36,32,128]{3,2,1,0:T(8,128)} %copy-done.1, bf16[3,112,432]{2,1,0:T(8,128)(2,1)} %get-tuple-element.36.refs_1_.refs_12_, ...), custom_call_target="tpu_custom_call" | custom-call | flops 10000000000 | bytes 12000000 | tf_op jit(solution)/shard_map/second/pallas_call | solution.py:318
  89.1 1.2 broadcast_select_fusion.5
  90.4 0.1 collective-permute-start.9
  90.5 4.0 %collective-permute-start.8 = (f32[30,32,128]{2,1,0:T(8,128)S(1)}, f32[30,32,128]{2,1,0:T(8,128)S(1)}, u32[]{:S(2)}, u32[]{:S(2)}) collective-permute-start(f32[30,32,128]{2,1,0:T(8,128)S(1)} %bitcast.47), channel_id=1, source_target_pairs={{4,8},{8,4},{12,16},{16,12},{20,24},{24,20},{5,9},{9,5},{13,17},{1... | collective-permute-start | bytes 1474568 | tf_op jit(solution)/shard_map/ppermute | solution.py:28
  94.5 1.2 broadcast_select_fusion.7
  95.8 0.1 collective-permute-start.7
  95.8 3.5 %collective-permute-start.6 = (f32[30,32,128]{2,1,0:T(8,128)S(1)}, f32[30,32,128]{2,1,0:T(8,128)S(1)}, u32[]{:S(2)}, u32[]{:S(2)}) collective-permute-start(f32[30,32,128]{2,1,0:T(8,128)S(1)} %bitcast.45), channel_id=1, source_target_pairs={{4,8},{8,4},{12,16},{16,12},{20,24},{24,20},{5,9},{9,5},{13,17},{1... | collective-permute-start | bytes 1474568 | tf_op jit(solution)/shard_map/ppermute | solution.py:28
  99.4 6.3 %collective-permute-done.8 = f32[30,32,128]{2,1,0:T(8,128)S(1)} collective-permute-done((f32[30,32,128]{2,1,0:T(8,128)S(1)}, f32[30,32,128]{2,1,0:T(8,128)S(1)}, u32[]{:S(2)}, u32[]{:S(2)}) %collective-permute-start.8) | collective-permute-done | bytes 491552 | tf_op jit(solution)/shard_map/ppermute | solution.py:28
  105.7 0.1 broadcast_select_fusion.19
  105.8 0.2 pad_add_fusion.1
  106.1 1.0 collective-permute-start.10
  107.1 4.8 %collective-permute-start.11 = (f32[48,16,128]{2,1,0:T(8,128)S(1)}, f32[48,16,128]{2,1,0:T(8,128)S(1)}, u32[]{:S(2)}, u32[]{:S(2)}) collective-permute-start(f32[48,16,128]{2,1,0:T(8,128)S(1)} %get-tuple-element.104), channel_id=1, source_target_pairs={{0,1},{1,0},{2,3},{3,2},{4,5},{5,4},{6,7},{7,6},{8,9},{9,8},{10,11... | collective-permute-start | bytes 1179656 | tf_op jit(solution)/shard_map/ppermute | solution.py:27
  111.9 4.3 %collective-permute-done.6 = f32[30,32,128]{2,1,0:T(8,128)S(1)} collective-permute-done((f32[30,32,128]{2,1,0:T(8,128)S(1)}, f32[30,32,128]{2,1,0:T(8,128)S(1)}, u32[]{:S(2)}, u32[]{:S(2)}) %collective-permute-start.6) | collective-permute-done | bytes 491552 | tf_op jit(solution)/shard_map/ppermute | solution.py:28
  116.2 0.1 broadcast_select_fusion.21
  116.3 2.9 %collective-permute-done.11 = f32[48,16,128]{2,1,0:T(8,128)S(1)} collective-permute-done((f32[48,16,128]{2,1,0:T(8,128)S(1)}, f32[48,16,128]{2,1,0:T(8,128)S(1)}, u32[]{:S(2)}, u32[]{:S(2)}) %collective-permute-start.11) | collective-permute-done | bytes 393248 | tf_op jit(solution)/shard_map/ppermute | solution.py:27
  119.3 0.3 add_multiply_fusion.1
  119.7 0.7 collective-permute-start.14
  120.4 2.5 %collective-permute-start.15 = (f32[48,16,128]{2,1,0:T(8,128)S(1)}, f32[48,16,128]{2,1,0:T(8,128)S(1)}, u32[]{:S(2)}, u32[]{:S(2)}) collective-permute-start(f32[48,16,128]{2,1,0:T(8,128)S(1)} %get-tuple-element.98), channel_id=1, source_target_pairs={{0,1},{1,0},{2,3},{3,2},{4,5},{5,4},{6,7},{7,6},{8,9},{9,8},{10,11... | collective-permute-start | bytes 1179656 | tf_op jit(solution)/shard_map/ppermute | solution.py:27
  122.9 0.1 slice_select_fusion
  123.0 0.1 collective-permute-start.13
  123.0 5.3 %collective-permute-start.12 = (f32[30,32,128]{2,1,0:T(8,128)S(1)}, f32[30,32,128]{2,1,0:T(8,128)S(1)}, u32[]{:S(2)}, u32[]{:S(2)}) collective-permute-start(f32[30,32,128]{2,1,0:T(8,128)S(1)} %get-tuple-element.100), channel_id=1, source_target_pairs={{4,8},{8,4},{12,16},{16,12},{20,24},{24,20},{5,9},{9,5},{13,17},{1... | collective-permute-start | bytes 1474568 | tf_op jit(solution)/shard_map/ppermute | solution.py:28
  128.5 0.1 broadcast_select_fusion.14
  128.7 8.2 %collective-permute-start.16 = (f32[30,32,128]{2,1,0:T(8,128)S(1)}, f32[30,32,128]{2,1,0:T(8,128)S(1)}, u32[]{:S(2)}, u32[]{:S(2)}) collective-permute-start(f32[30,32,128]{2,1,0:T(8,128)S(1)} %get-tuple-element.94), channel_id=1, source_target_pairs={{4,8},{8,4},{12,16},{16,12},{20,24},{24,20},{5,9},{9,5},{13,17},{1... | collective-permute-start | bytes 1474568 | tf_op jit(solution)/shard_map/ppermute | solution.py:28
  136.9 0.1 pad_maximum_fusion
  137.1 2.7 %collective-permute-done.12 = f32[30,32,128]{2,1,0:T(8,128)S(1)} collective-permute-done((f32[30,32,128]{2,1,0:T(8,128)S(1)}, f32[30,32,128]{2,1,0:T(8,128)S(1)}, u32[]{:S(2)}, u32[]{:S(2)}) %collective-permute-start.12) | collective-permute-done | bytes 491552 | tf_op jit(solution)/shard_map/ppermute | solution.py:28
  139.7 0.1 broadcast_select_fusion.16
  139.8 10.4 %collective-permute-done.16 = f32[30,32,128]{2,1,0:T(8,128)S(1)} collective-permute-done((f32[30,32,128]{2,1,0:T(8,128)S(1)}, f32[30,32,128]{2,1,0:T(8,128)S(1)}, u32[]{:S(2)}, u32[]{:S(2)}) %collective-permute-start.16) | collective-permute-done | bytes 491552 | tf_op jit(solution)/shard_map/ppermute | solution.py:28
  150.3 0.1 broadcast_select_fusion.12
  150.5 26.8 %both.1 = (f32[1536,128]{1,0:T(8,128)S(1)}, f32[960,128]{1,0:T(8,128)S(1)}, f32[960,128]{1,0:T(8,128)S(1)}, f32[1536,128]{1,0:T(8,128)S(1)}, f32[960,128]{1,0:T(8,128)S(1)}, /*index=5*/f32[960,128]{1,0:T(8,128)S(1)}) custom-call(f32[1536,128]{1,0:T(8,128)S(1)} %bitcast.28, f32[960,128]{1,0:T(8,128)S(1)} %bitcast.34, f32[960,128]{1,0:T(8,128)S(1)} %bitcast.33, ...), custom_call_target="tpu_custom_call" | custom-call | flops 10000000000 | bytes 12000000 | tf_op jit(solution)/shard_map/both/pallas_call | solution.py:318
  177.2 0.1 broadcast_select_fusion.1
  177.4 0.1 collective-permute-start.21
  177.4 3.2 %collective-permute-start.20 = (f32[30,32,128]{2,1,0:T(8,128)S(1)}, f32[30,32,128]{2,1,0:T(8,128)S(1)}, u32[]{:S(2)}, u32[]{:S(2)}) collective-permute-start(f32[30,32,128]{2,1,0:T(8,128)S(1)} %bitcast.50), channel_id=1, source_target_pairs={{4,8},{8,4},{12,16},{16,12},{20,24},{24,20},{5,9},{9,5},{13,17},{1... | collective-permute-start | bytes 1474568 | tf_op jit(solution)/shard_map/ppermute | solution.py:28
  180.7 0.1 collective-permute-start.19
  180.8 4.3 %collective-permute-start.18 = (f32[30,32,128]{2,1,0:T(8,128)S(1)}, f32[30,32,128]{2,1,0:T(8,128)S(1)}, u32[]{:S(2)}, u32[]{:S(2)}) collective-permute-start(f32[30,32,128]{2,1,0:T(8,128)S(1)} %bitcast.43), channel_id=1, source_target_pairs={{4,8},{8,4},{12,16},{16,12},{20,24},{24,20},{5,9},{9,5},{13,17},{1... | collective-permute-start | bytes 1474568 | tf_op jit(solution)/shard_map/ppermute | solution.py:28
  185.1 6.5 %collective-permute-done.20 = f32[30,32,128]{2,1,0:T(8,128)S(1)} collective-permute-done((f32[30,32,128]{2,1,0:T(8,128)S(1)}, f32[30,32,128]{2,1,0:T(8,128)S(1)}, u32[]{:S(2)}, u32[]{:S(2)}) %collective-permute-start.20) | collective-permute-done | bytes 491552 | tf_op jit(solution)/shard_map/ppermute | solution.py:28
  191.6 0.1 broadcast_select_fusion.9
  191.7 0.2 pad_add_fusion
  191.9 0.7 collective-permute-start.22
  192.6 2.9 %collective-permute-start.23 = (f32[48,16,128]{2,1,0:T(8,128)S(1)}, f32[48,16,128]{2,1,0:T(8,128)S(1)}, u32[]{:S(2)}, u32[]{:S(2)}) collective-permute-start(f32[48,16,128]{2,1,0:T(8,128)S(1)} %get-tuple-element.92), channel_id=1, source_target_pairs={{0,1},{1,0},{2,3},{3,2},{4,5},{5,4},{6,7},{7,6},{8,9},{9,8},{10,11... | collective-permute-start | bytes 1179656 | tf_op jit(solution)/shard_map/ppermute | solution.py:27
  195.5 6.6 %collective-permute-done.18 = f32[30,32,128]{2,1,0:T(8,128)S(1)} collective-permute-done((f32[30,32,128]{2,1,0:T(8,128)S(1)}, f32[30,32,128]{2,1,0:T(8,128)S(1)}, u32[]{:S(2)}, u32[]{:S(2)}) %collective-permute-start.18) | collective-permute-done | bytes 491552 | tf_op jit(solution)/shard_map/ppermute | solution.py:28
  202.1 0.1 broadcast_select_fusion.11
  202.2 1.2 add_multiply_fusion
  (57 shorter events, 0.6 us)
Async XLA Ops:
  1.2 11.0 %collective-permute-start.1 = (f32[48,16,128]{2,1,0:T(8,128)S(1)}, f32[48,16,128]{2,1,0:T(8,128)S(1)}, u32[]{:S(2)}, u32[]{:S(2)}) collective-permute-start(f32[48,16,128]{2,1,0:T(8,128)S(1)} %get-tuple-element.111), channel_id=1, source_target_pairs={{0,1},{1,0},{2,3},{3,2},{4,5},{5,4},{6,7},{7,6},{8,9},{9,8},{10,11... | collective-permute-start | bytes 1179656 | tf_op jit(solution)/shard_map/ppermute | solution.py:27
  3.4 8.8 %collective-permute-start = (f32[48,16,128]{2,1,0:T(8,128)S(1)}, f32[48,16,128]{2,1,0:T(8,128)S(1)}, u32[]{:S(2)}, u32[]{:S(2)}) collective-permute-start(f32[48,16,128]{2,1,0:T(8,128)S(1)} %get-tuple-element.112), channel_id=1, source_target_pairs={{1,2},{2,1},{5,6},{6,5},{9,10},{10,9},{13,14},{14,13},{17,18},{18,... | collective-permute-start | bytes 1179656 | tf_op jit(solution)/shard_map/ppermute | solution.py:28
  4.1 1.7 copy-start
  13.0 62.4 %all-to-all-start = ((f32[4,36,32,128]{3,2,1,0:T(8,128)}), f32[4,36,32,128]{3,2,1,0:T(8,128)S(1)}, u32[]{:S(2)}, u32[]{:S(2)}) async-start(f32[4,36,32,128]{3,2,1,0:T(8,128)} %pack.1), calls=%async_computation | async-start | bytes 4718592 | tf_op jit(solution)/shard_map/all_to_all | solution.py:549
  19.3 7.5 %copy-start.11 = (f32[48,32,128]{2,1,0:T(8,128)S(1)}, f32[48,32,128]{2,1,0:T(8,128)}, u32[]{:S(2)}) copy-start(f32[48,32,128]{2,1,0:T(8,128)} %param.8) | copy-start | bytes 2359300
  20.4 11.1 %copy-start.16 = (s32[32,3]{0,1:T(4,128)S(1)}, s32[32,3]{0,1:T(4,128)}, u32[]{:S(2)}) copy-start(s32[32,3]{0,1:T(4,128)} %param.15) | copy-start | bytes 1156
  20.5 7.5 %copy-start.13 = (f32[48,32,128]{2,1,0:T(8,128)}, f32[48,32,128]{2,1,0:T(8,128)S(1)}, u32[]{:S(2)}) copy-start(f32[48,32,128]{2,1,0:T(8,128)S(1)} %constant_dynamic-update-slice_fusion) | copy-start | bytes 2359300
  21.7 18.2 %collective-permute-start.5 = (f32[30,32,128]{2,1,0:T(8,128)}, f32[30,32,128]{2,1,0:T(8,128)}, u32[]{:S(2)}, u32[]{:S(2)}) collective-permute-start(f32[30,32,128]{2,1,0:T(8,128)} %get-tuple-element.105), channel_id=1, source_target_pairs={{0,4},{4,0},{8,12},{12,8},{16,20},{20,16},{24,28},{28,24},{1,5},{5... | collective-permute-start | bytes 1474568 | tf_op jit(solution)/shard_map/ppermute | solution.py:27
  23.8 16.0 %collective-permute-start.4 = (f32[30,32,128]{2,1,0:T(8,128)}, f32[30,32,128]{2,1,0:T(8,128)}, u32[]{:S(2)}, u32[]{:S(2)}) collective-permute-start(f32[30,32,128]{2,1,0:T(8,128)} %get-tuple-element.106), channel_id=1, source_target_pairs={{4,8},{8,4},{12,16},{16,12},{20,24},{24,20},{5,9},{9,5},{13,17},{1... | collective-permute-start | bytes 1474568 | tf_op jit(solution)/shard_map/ppermute | solution.py:28
  28.0 14.1 %collective-permute-start.3 = (f32[30,32,128]{2,1,0:T(8,128)}, f32[30,32,128]{2,1,0:T(8,128)S(1)}, u32[]{:S(2)}, u32[]{:S(2)}) collective-permute-start(f32[30,32,128]{2,1,0:T(8,128)} %get-tuple-element.107), channel_id=1, source_target_pairs={{0,4},{4,0},{8,12},{12,8},{16,20},{20,16},{24,28},{28,24},{1,5},{5... | collective-permute-start | bytes 1474568 | tf_op jit(solution)/shard_map/ppermute | solution.py:27
  28.0 21.7 %collective-permute-start.2 = (f32[30,32,128]{2,1,0:T(8,128)}, f32[30,32,128]{2,1,0:T(8,128)S(1)}, u32[]{:S(2)}, u32[]{:S(2)}) collective-permute-start(f32[30,32,128]{2,1,0:T(8,128)} %get-tuple-element.108), channel_id=1, source_target_pairs={{4,8},{8,4},{12,16},{16,12},{20,24},{24,20},{5,9},{9,5},{13,17},{1... | collective-permute-start | bytes 1474568 | tf_op jit(solution)/shard_map/ppermute | solution.py:28
  75.4 1.4 copy-start.1
  90.4 15.4 %copy-start.14 = (f32[1536,128]{1,0:T(8,128)S(1)}, f32[1536,128]{1,0:T(8,128)}, u32[]{:S(2)}) copy-start(f32[1536,128]{1,0:T(8,128)} %get-tuple-element.56) | copy-start | bytes 2359300
  90.4 9.0 %collective-permute-start.9 = (f32[30,32,128]{2,1,0:T(8,128)S(1)}, f32[30,32,128]{2,1,0:T(8,128)S(1)}, u32[]{:S(2)}, u32[]{:S(2)}) collective-permute-start(f32[30,32,128]{2,1,0:T(8,128)S(1)} %bitcast.51), channel_id=1, source_target_pairs={{0,4},{4,0},{8,12},{12,8},{16,20},{20,16},{24,28},{28,24},{1,5},{5... | collective-permute-start | bytes 1474568 | tf_op jit(solution)/shard_map/ppermute | solution.py:27
  90.5 15.2 %collective-permute-start.8 = (f32[30,32,128]{2,1,0:T(8,128)S(1)}, f32[30,32,128]{2,1,0:T(8,128)S(1)}, u32[]{:S(2)}, u32[]{:S(2)}) collective-permute-start(f32[30,32,128]{2,1,0:T(8,128)S(1)} %bitcast.47), channel_id=1, source_target_pairs={{4,8},{8,4},{12,16},{16,12},{20,24},{24,20},{5,9},{9,5},{13,17},{1... | collective-permute-start | bytes 1474568 | tf_op jit(solution)/shard_map/ppermute | solution.py:28
  95.8 16.1 %collective-permute-start.7 = (f32[30,32,128]{2,1,0:T(8,128)S(1)}, f32[30,32,128]{2,1,0:T(8,128)S(1)}, u32[]{:S(2)}, u32[]{:S(2)}) collective-permute-start(f32[30,32,128]{2,1,0:T(8,128)S(1)} %bitcast.46), channel_id=1, source_target_pairs={{0,4},{4,0},{8,12},{12,8},{16,20},{20,16},{24,28},{28,24},{1,5},{5... | collective-permute-start | bytes 1474568 | tf_op jit(solution)/shard_map/ppermute | solution.py:27
  95.8 20.4 %collective-permute-start.6 = (f32[30,32,128]{2,1,0:T(8,128)S(1)}, f32[30,32,128]{2,1,0:T(8,128)S(1)}, u32[]{:S(2)}, u32[]{:S(2)}) collective-permute-start(f32[30,32,128]{2,1,0:T(8,128)S(1)} %bitcast.45), channel_id=1, source_target_pairs={{4,8},{8,4},{12,16},{16,12},{20,24},{24,20},{5,9},{9,5},{13,17},{1... | collective-permute-start | bytes 1474568 | tf_op jit(solution)/shard_map/ppermute | solution.py:28
  106.0 13.3 %copy-start.12 = (f32[48,32,128]{2,1,0:T(8,128)S(1)}, f32[48,32,128]{2,1,0:T(8,128)}, u32[]{:S(2)}) copy-start(f32[48,32,128]{2,1,0:T(8,128)} %param.8) | copy-start | bytes 2359300
  106.0 13.3 %copy-start.15 = (f32[1536,128]{1,0:T(8,128)S(1)}, f32[1536,128]{1,0:T(8,128)}, u32[]{:S(2)}) copy-start(f32[1536,128]{1,0:T(8,128)} %get-tuple-element.53) | copy-start | bytes 2359300
  106.1 10.3 %collective-permute-start.10 = (f32[48,16,128]{2,1,0:T(8,128)S(1)}, f32[48,16,128]{2,1,0:T(8,128)S(1)}, u32[]{:S(2)}, u32[]{:S(2)}) collective-permute-start(f32[48,16,128]{2,1,0:T(8,128)S(1)} %get-tuple-element.103), channel_id=1, source_target_pairs={{1,2},{2,1},{5,6},{6,5},{9,10},{10,9},{13,14},{14,13},{17,18},{18,... | collective-permute-start | bytes 1179656 | tf_op jit(solution)/shard_map/ppermute | solution.py:28
  107.1 12.1 %collective-permute-start.11 = (f32[48,16,128]{2,1,0:T(8,128)S(1)}, f32[48,16,128]{2,1,0:T(8,128)S(1)}, u32[]{:S(2)}, u32[]{:S(2)}) collective-permute-start(f32[48,16,128]{2,1,0:T(8,128)S(1)} %get-tuple-element.104), channel_id=1, source_target_pairs={{0,1},{1,0},{2,3},{3,2},{4,5},{5,4},{6,7},{7,6},{8,9},{9,8},{10,11... | collective-permute-start | bytes 1179656 | tf_op jit(solution)/shard_map/ppermute | solution.py:27
  119.7 8.7 %collective-permute-start.14 = (f32[48,16,128]{2,1,0:T(8,128)S(1)}, f32[48,16,128]{2,1,0:T(8,128)S(1)}, u32[]{:S(2)}, u32[]{:S(2)}) collective-permute-start(f32[48,16,128]{2,1,0:T(8,128)S(1)} %get-tuple-element.97), channel_id=1, source_target_pairs={{1,2},{2,1},{5,6},{6,5},{9,10},{10,9},{13,14},{14,13},{17,18},{18,... | collective-permute-start | bytes 1179656 | tf_op jit(solution)/shard_map/ppermute | solution.py:28
  120.4 8.0 %collective-permute-start.15 = (f32[48,16,128]{2,1,0:T(8,128)S(1)}, f32[48,16,128]{2,1,0:T(8,128)S(1)}, u32[]{:S(2)}, u32[]{:S(2)}) collective-permute-start(f32[48,16,128]{2,1,0:T(8,128)S(1)} %get-tuple-element.98), channel_id=1, source_target_pairs={{0,1},{1,0},{2,3},{3,2},{4,5},{5,4},{6,7},{7,6},{8,9},{9,8},{10,11... | collective-permute-start | bytes 1179656 | tf_op jit(solution)/shard_map/ppermute | solution.py:27
  123.0 14.1 %collective-permute-start.13 = (f32[30,32,128]{2,1,0:T(8,128)S(1)}, f32[30,32,128]{2,1,0:T(8,128)S(1)}, u32[]{:S(2)}, u32[]{:S(2)}) collective-permute-start(f32[30,32,128]{2,1,0:T(8,128)S(1)} %get-tuple-element.99), channel_id=1, source_target_pairs={{0,4},{4,0},{8,12},{12,8},{16,20},{20,16},{24,28},{28,24},{1,5},{5... | collective-permute-start | bytes 1474568 | tf_op jit(solution)/shard_map/ppermute | solution.py:27
  123.0 16.7 %collective-permute-start.12 = (f32[30,32,128]{2,1,0:T(8,128)S(1)}, f32[30,32,128]{2,1,0:T(8,128)S(1)}, u32[]{:S(2)}, u32[]{:S(2)}) collective-permute-start(f32[30,32,128]{2,1,0:T(8,128)S(1)} %get-tuple-element.100), channel_id=1, source_target_pairs={{4,8},{8,4},{12,16},{16,12},{20,24},{24,20},{5,9},{9,5},{13,17},{1... | collective-permute-start | bytes 1474568 | tf_op jit(solution)/shard_map/ppermute | solution.py:28
  128.4 22.0 %copy-start.10 = (bf16[6,64,96]{2,1,0:T(8,128)(2,1)S(1)}, bf16[6,64,96]{2,1,0:T(8,128)(2,1)}, u32[]{:S(2)}) copy-start(bf16[6,64,96]{2,1,0:T(8,128)(2,1)} %get-tuple-element.45.refs_12_.refs_10_.refs_14_) | copy-start | bytes 221188
  128.5 21.9 %copy-start.5 = (bf16[6,256,256]{2,1,0:T(8,128)(2,1)S(1)}, bf16[6,256,256]{2,1,0:T(8,128)(2,1)}, u32[]{:S(2)}) copy-start(bf16[6,256,256]{2,1,0:T(8,128)(2,1)} %get-tuple-element.44.refs_11_.refs_9_.refs_13_) | copy-start | bytes 2359300
  128.5 21.9 %copy-start.6 = (bf16[3,112,432]{2,1,0:T(8,128)(2,1)S(1)}, bf16[3,112,432]{2,1,0:T(8,128)(2,1)}, u32[]{:S(2)}) copy-start(bf16[3,112,432]{2,1,0:T(8,128)(2,1)} %get-tuple-element.43.refs_10_) | copy-start | bytes 870916
  128.5 21.9 %copy-start.7 = (bf16[3,112,432]{2,1,0:T(8,128)(2,1)S(1)}, bf16[3,112,432]{2,1,0:T(8,128)(2,1)}, u32[]{:S(2)}) copy-start(bf16[3,112,432]{2,1,0:T(8,128)(2,1)} %get-tuple-element.36.refs_1_.refs_12_) | copy-start | bytes 870916
  128.5 21.9 %copy-start.8 = (bf16[288,336]{1,0:T(8,128)(2,1)S(1)}, bf16[288,336]{1,0:T(8,128)(2,1)}, u32[]{:S(2)}) copy-start(bf16[288,336]{1,0:T(8,128)(2,1)} %get-tuple-element.40.refs_6_) | copy-start | bytes 580612
  128.5 21.9 %copy-start.9 = (bf16[6,64,128]{2,1,0:T(8,128)(2,1)S(1)}, bf16[6,64,128]{2,1,0:T(8,128)(2,1)}, u32[]{:S(2)}) copy-start(bf16[6,64,128]{2,1,0:T(8,128)(2,1)} %get-tuple-element.41.refs_7_) | copy-start | bytes 294916
  128.6 11.2 %collective-permute-start.17 = (f32[30,32,128]{2,1,0:T(8,128)S(1)}, f32[30,32,128]{2,1,0:T(8,128)S(1)}, u32[]{:S(2)}, u32[]{:S(2)}) collective-permute-start(f32[30,32,128]{2,1,0:T(8,128)S(1)} %get-tuple-element.93), channel_id=1, source_target_pairs={{0,4},{4,0},{8,12},{12,8},{16,20},{20,16},{24,28},{28,24},{1,5},{5... | collective-permute-start | bytes 1474568 | tf_op jit(solution)/shard_map/ppermute | solution.py:27
  128.7 21.5 %collective-permute-start.16 = (f32[30,32,128]{2,1,0:T(8,128)S(1)}, f32[30,32,128]{2,1,0:T(8,128)S(1)}, u32[]{:S(2)}, u32[]{:S(2)}) collective-permute-start(f32[30,32,128]{2,1,0:T(8,128)S(1)} %get-tuple-element.94), channel_id=1, source_target_pairs={{4,8},{8,4},{12,16},{16,12},{20,24},{24,20},{5,9},{9,5},{13,17},{1... | collective-permute-start | bytes 1474568 | tf_op jit(solution)/shard_map/ppermute | solution.py:28
  136.9 13.5 %copy-start.3 = (f32[3,48,32,128]{3,2,1,0:T(8,128)S(1)}, f32[3,48,32,128]{3,2,1,0:T(8,128)}, u32[]{:S(2)}) copy-start(f32[3,48,32,128]{3,2,1,0:T(8,128)} %param.9) | copy-start | bytes 7077892
  137.0 13.4 %copy-start.2 = (f32[4,36,32,128]{3,2,1,0:T(8,128)S(1)}, f32[4,36,32,128]{3,2,1,0:T(8,128)}, u32[]{:S(2)}) copy-start(f32[4,36,32,128]{3,2,1,0:T(8,128)} %copy-done.1) | copy-start | bytes 7077892
  137.1 13.4 %copy-start.4 = (bf16[6,256,256]{2,1,0:T(8,128)(2,1)S(1)}, bf16[6,256,256]{2,1,0:T(8,128)(2,1)}, u32[]{:S(2)}) copy-start(bf16[6,256,256]{2,1,0:T(8,128)(2,1)} %get-tuple-element.42.refs_8_) | copy-start | bytes 2359300
  177.4 7.7 %collective-permute-start.21 = (f32[30,32,128]{2,1,0:T(8,128)S(1)}, f32[30,32,128]{2,1,0:T(8,128)S(1)}, u32[]{:S(2)}, u32[]{:S(2)}) collective-permute-start(f32[30,32,128]{2,1,0:T(8,128)S(1)} %bitcast.52), channel_id=1, source_target_pairs={{0,4},{4,0},{8,12},{12,8},{16,20},{20,16},{24,28},{28,24},{1,5},{5... | collective-permute-start | bytes 1474568 | tf_op jit(solution)/shard_map/ppermute | solution.py:27
  177.4 14.1 %collective-permute-start.20 = (f32[30,32,128]{2,1,0:T(8,128)S(1)}, f32[30,32,128]{2,1,0:T(8,128)S(1)}, u32[]{:S(2)}, u32[]{:S(2)}) collective-permute-start(f32[30,32,128]{2,1,0:T(8,128)S(1)} %bitcast.50), channel_id=1, source_target_pairs={{4,8},{8,4},{12,16},{16,12},{20,24},{24,20},{5,9},{9,5},{13,17},{1... | collective-permute-start | bytes 1474568 | tf_op jit(solution)/shard_map/ppermute | solution.py:28
  180.7 14.8 %collective-permute-start.19 = (f32[30,32,128]{2,1,0:T(8,128)S(1)}, f32[30,32,128]{2,1,0:T(8,128)S(1)}, u32[]{:S(2)}, u32[]{:S(2)}) collective-permute-start(f32[30,32,128]{2,1,0:T(8,128)S(1)} %bitcast.44), channel_id=1, source_target_pairs={{0,4},{4,0},{8,12},{12,8},{16,20},{20,16},{24,28},{28,24},{1,5},{5... | collective-permute-start | bytes 1474568 | tf_op jit(solution)/shard_map/ppermute | solution.py:27
  180.8 21.3 %collective-permute-start.18 = (f32[30,32,128]{2,1,0:T(8,128)S(1)}, f32[30,32,128]{2,1,0:T(8,128)S(1)}, u32[]{:S(2)}, u32[]{:S(2)}) collective-permute-start(f32[30,32,128]{2,1,0:T(8,128)S(1)} %bitcast.43), channel_id=1, source_target_pairs={{4,8},{8,4},{12,16},{16,12},{20,24},{24,20},{5,9},{9,5},{13,17},{1... | collective-permute-start | bytes 1474568 | tf_op jit(solution)/shard_map/ppermute | solution.py:28
  191.9 10.2 %collective-permute-start.22 = (f32[48,16,128]{2,1,0:T(8,128)S(1)}, f32[48,16,128]{2,1,0:T(8,128)S(1)}, u32[]{:S(2)}, u32[]{:S(2)}) collective-permute-start(f32[48,16,128]{2,1,0:T(8,128)S(1)} %get-tuple-element.91), channel_id=1, source_target_pairs={{1,2},{2,1},{5,6},{6,5},{9,10},{10,9},{13,14},{14,13},{17,18},{18,... | collective-permute-start | bytes 1179656 | tf_op jit(solution)/shard_map/ppermute | solution.py:28
  192.6 9.6 %collective-permute-start.23 = (f32[48,16,128]{2,1,0:T(8,128)S(1)}, f32[48,16,128]{2,1,0:T(8,128)S(1)}, u32[]{:S(2)}, u32[]{:S(2)}) collective-permute-start(f32[48,16,128]{2,1,0:T(8,128)S(1)} %get-tuple-element.92), channel_id=1, source_target_pairs={{0,1},{1,0},{2,3},{3,2},{4,5},{5,4},{6,7},{7,6},{8,9},{9,8},{10,11... | collective-permute-start | bytes 1179656 | tf_op jit(solution)/shard_map/ppermute | solution.py:27

commit v3 on v2

--- a/solution.py
+++ b/solution.py
@@ -11,6 +11,7 @@
 F32 = jnp.float32
 BF16 = jnp.bfloat16
 VMEM_LIMIT = 36 * 1024 * 1024
+SPLIT = (56, 56, 36)
 
 
 def round_up(value, unit):
@@ -46,28 +47,32 @@
     depth, rows, side, reach, zpad = plan.depth, plan.rows, plan.side, plan.reach, plan.zpad
     width = plan.width
     total = rows + side
-    pitch_y = total + 2
+    pitch_c = rows + 2
+    pitch_s = side + 2
+    pitch_r = depth + 2
     if plan.forward:
-        c, clo, chi, s, slo, shi, wzf, wyf, wxf = take(9)
+        ahead_c, s, slo, shi, wzf, wyf, wxf = take(7)
     if plan.upright_back:
         obs_u, wzb_u = take(2)
     if plan.turned_back:
         obs_t, wzb_t = take(2)
         if not plan.forward:
             (blur_in,) = take(1)
-            acc = take(6)
+            acc = take(3)
     wxb, wyb = take(2)
+    outs = take(3)
+    if plan.upright_back:
+        (lines_u,) = take(1)
     if plan.turned_back:
-        outs = take(6)
+        (lines_t,) = take(1)
     else:
-        outs = take(6)
         (blur_out,) = take(1)
     if plan.forward:
         (mid,) = take(1)
     (back,) = take(1)
     copies = []
     if plan.turned_back and not plan.forward:
-        held = take(6)
+        held = take(3)
         (arrived,) = take(1)
         copies = [
             pltpu.make_async_copy(x, y, arrived.at[i]) for i, (x, y) in enumerate(zip(acc, held))
@@ -91,44 +96,24 @@
 
         @pl.when(step == 0)
         def _():
-            fill = jnp.zeros((zpad - reach, width), F32)
-
-            def column(low, centre, high, y, n):
-                return jnp.concatenate(
-                    [
-                        low[pl.ds(y, reach, stride=n), :],
-                        fill,
-                        centre[pl.ds(y, depth, stride=n), :],
-                        high[pl.ds(y, reach, stride=n), :],
-                        fill,
-                    ],
-                    axis=0,
-                )
-
-            def run(low, centre, high, n, base):
-                def body(i, carry):
-                    both = jnp.concatenate(
-                        [column(low, centre, high, 2 * i + j, n) for j in range(2)], axis=1
-                    )
-                    result = jnp.dot(wzf[...], stack(both), preferred_element_type=F32)
-                    for j in range(2):
-                        mid[pl.ds(base + 2 * i + j, n_all * depth, stride=pitch_y), :] = result[
-                            :, j * width : (j + 1) * width
-                        ]
-                    return carry
-
-                lax.fori_loop(0, n // 2, body, 0, unroll=8)
-
-            run(clo, c, chi, rows, 0)
-            run(slo, s, shi, side, rows)
+            forward_z(plan, slo, s, shi, side, wzf, pitch_s, mid, n_all * depth)
 
     def blur_lines(view, i):
-        start = (view * depth + i * group) * pitch_y
         pieces = []
         for j in range(group // 2):
-            at = start + 2 * j * pitch_y
+            line = i * group + 2 * j
             both = jnp.concatenate(
-                [mid[pl.ds(at, total), :], mid[pl.ds(at + pitch_y, total), :]], axis=1
+                [
+                    jnp.concatenate(
+                        [
+                            ahead_c[0, pl.ds((line + k) * pitch_c, rows), :],
+                            mid[pl.ds((view * depth + line + k) * pitch_s, side), :],
+                        ],
+                        axis=0,
+                    )
+                    for k in range(2)
+                ],
+                axis=1,
             )
             top, rest = halves(both)
             result = jnp.dot(
@@ -142,7 +127,7 @@
         )
         return result[:, :width] + result[:, width:]
 
-    def spread_lines(slot, i, ratio):
+    def spread_lines(slot, i, ratio, lines_c):
         top, rest = halves(ratio)
         flat = jnp.dot(jnp.concatenate([top, rest], axis=1), wxb[0], preferred_element_type=F32)
         flat = flat[:, :width] + flat[:, width:]
@@ -152,10 +137,10 @@
             )
             result = jnp.dot(wyb[0], stack(both), preferred_element_type=F32)
             for k in range(2):
-                line = slot * depth + i * group + 2 * j + k
-                back[pl.ds(line, total, stride=pitch_z), :] = result[
-                    :, k * width : (k + 1) * width
-                ]
+                line = i * group + 2 * j + k
+                piece = result[:, k * width : (k + 1) * width]
+                lines_c[0, pl.ds(line, rows, stride=pitch_r), :] = piece[:rows]
+                back[pl.ds(slot * depth + line, side, stride=pitch_z), :] = piece[rows:]
 
     def turned_lines(i):
         per = plan.per
@@ -182,7 +167,7 @@
             view = step - first
 
             def body(i):
-                spread_lines(view, i, obs_u[0, window(i), :] / blur_lines(view, i))
+                spread_lines(view, i, obs_u[0, window(i), :] / blur_lines(view, i), lines_u)
 
             loop(body)
 
@@ -193,7 +178,7 @@
         def body(i):
             blurred = blur_lines(view, i) if plan.forward else blur_in[0, window(i), :]
             if plan.turned_back:
-                spread_lines(view, i, turned_lines(i) / blurred)
+                spread_lines(view, i, turned_lines(i) / blurred, lines_t)
             else:
                 blur_out[0, window(i), :] = blurred
 
@@ -209,35 +194,141 @@
         if plan.turned_back:
             banks.append((wzb_t, n_up * depth, plan.turned * depth))
 
-        def run(region, targets, adds, n, base, begin, end):
-            def body(i, carry):
-                at = (base + 2 * i) * pitch_z
-                result = None
-                for weights, offset, count in banks:
-                    both = jnp.concatenate(
-                        [back[pl.ds(at + j * pitch_z + offset, count), :] for j in range(2)],
-                        axis=1,
+        def sums(y, region):
+            result = None
+            for weights, offset, count in banks:
+                both = jnp.concatenate(
+                    [back[pl.ds((y + j) * pitch_z + offset, count), :] for j in range(2)], axis=1
+                )
+                term = jnp.dot(weights[region], stack(both), preferred_element_type=F32)
+                result = term if result is None else result + term
+            return result
+
+        adds = acc if (plan.turned_back and not plan.forward) else [None] * 3
+        backward_z(plan, lambda y: sums(y, 0), outs, adds, side, 0, side // 4)
+        backward_z(plan, lambda y: sums(y, 2), outs, adds, side, side // 4, side // 2)
+
+
+def forward_z(plan, low, centre, high, n, weights, pitch, target, count):
+    depth, reach = plan.depth, plan.reach
+    width = plan.width
+    fill = jnp.zeros((plan.zpad - reach, width), F32)
+
+    def column(y):
+        return jnp.concatenate(
+            [
+                low[pl.ds(y, reach, stride=n), :],
+                fill,
+                centre[pl.ds(y, depth, stride=n), :],
+                high[pl.ds(y, reach, stride=n), :],
+                fill,
+            ],
+            axis=0,
+        )
+
+    def body(i, carry):
+        both = jnp.concatenate([column(2 * i + j) for j in range(2)], axis=1)
+        result = jnp.dot(weights[...], stack(both), preferred_element_type=F32)
+        for j in range(2):
+            target[pl.ds(2 * i + j, count, stride=pitch), :] = result[
+                :, j * width : (j + 1) * width
+            ]
+        return carry
+
+    lax.fori_loop(0, n // 2, body, 0, unroll=8)
+
+
+def backward_z(plan, sums, targets, adds, n, begin, end, shift=0):
+    depth, reach, zpad, width = plan.depth, plan.reach, plan.zpad, plan.width
+
+    def body(i, carry):
+        result = sums(2 * i)
+        for j in range(2):
+            part = result[:, j * width : (j + 1) * width]
+            for target, add, low, count in zip(
+                targets, adds, (zpad, 0, zpad + depth), (depth, reach, reach)
+            ):
+                spot = (pl.ds(shift + 2 * i + j, count, stride=n), slice(None))
+                piece = part[low : low + count]
+                if add is not None:
+                    piece = piece + add[spot]
+                target[spot] = piece
+        return carry
+
+    lax.fori_loop(begin, end, body, 0, unroll=4)
+
+
+def ahead_kernel(plan, c, clo, chi, wzf, out):
+    forward_z(
+        plan, clo, c, chi, plan.rows, wzf, plan.rows + 2, out, wzf.shape[0]
+    )
+
+
+def ahead(plan, c, clo, chi, wzf):
+    cuts = 2
+    whole = lambda x: pl.BlockSpec(x.shape, lambda i: (0, 0), pipeline_mode=pl.Buffered(1))
+    lines = wzf.shape[0] * (plan.rows + 2)
+    return pl.pallas_call(
+        functools.partial(ahead_kernel, plan),
+        out_shape=jax.ShapeDtypeStruct((lines, plan.width), F32),
+        grid=(cuts,),
+        in_specs=[whole(x) for x in (c, clo, chi)]
+        + [pl.BlockSpec((wzf.shape[0] // cuts, wzf.shape[1]), lambda i: (i, 0))],
+        out_specs=pl.BlockSpec((lines // cuts, plan.width), lambda i: (i, 0)),
+        compiler_params=pltpu.CompilerParams(vmem_limit_bytes=plan.vmem),
+        cost_estimate=pl.CostEstimate(flops=3 * 10**9, bytes_accessed=8 * 10**6, transcendentals=0),
+        name=plan.name,
+    )(c, clo, chi, wzf)
+
+
+def behind_kernel(plan, span, ru, rt, wzu, wzt, cc, clo, chi):
+    depth = plan.depth
+    begin = pl.program_id(0) * span
+
+    def sums(y):
+        result = None
+        for lines, weights in ((ru, wzu), (rt, wzt)):
+            both = jnp.concatenate(
+                [
+                    jnp.concatenate(
+                        [
+                            lines[v, pl.ds((y + j) * (depth + 2), depth), :]
+                            for v in range(lines.shape[0])
+                        ],
+                        axis=0,
                     )
-                    term = jnp.dot(weights[region], stack(both), preferred_element_type=F32)
-                    result = term if result is None else result + term
-                for j in range(2):
-                    part = result[:, j * width : (j + 1) * width]
-                    for target, add, low, count in zip(
-                        targets, adds, (zpad, 0, zpad + depth), (depth, reach, reach)
-                    ):
-                        spot = (pl.ds(2 * i + j, count, stride=n), slice(None))
-                        piece = part[low : low + count]
-                        if add is not None:
-                            piece = piece + add[spot]
-                        target[spot] = piece
-                return carry
-
-            lax.fori_loop(begin, end, body, 0, unroll=4)
-
-        adds = acc if (plan.turned_back and not plan.forward) else [None] * 6
-        run(0, outs[3:], adds[3:], side, rows, 0, side // 4)
-        run(2, outs[3:], adds[3:], side, rows, side // 4, side // 2)
-        run(1, outs[:3], adds[:3], rows, 0, 0, rows // 2)
+                    for j in range(2)
+                ],
+                axis=1,
+            )
+            term = jnp.dot(weights[0], stack(both), preferred_element_type=F32)
+            result = term if result is None else result + term
+        return result
+
+    backward_z(plan, sums, (cc, clo, chi), [None] * 3, plan.rows, 0, span // 2, begin)
+
+
+def behind(plan, ru, rt, wzu, wzt):
+    span = 8
+    pitch = plan.depth + 2
+    block = lambda x: pl.BlockSpec((x.shape[0], span * pitch, plan.width), lambda i: (0, i, 0))
+    weights = lambda x: pl.BlockSpec((1,) + x.shape[1:], lambda i: (1, 0, 0))
+    shapes = [
+        jax.ShapeDtypeStruct((count * plan.rows, plan.width), F32)
+        for count in (plan.depth, plan.reach, plan.reach)
+    ]
+    return pl.pallas_call(
+        functools.partial(behind_kernel, plan, span),
+        out_shape=shapes,
+        grid=(plan.rows // span,),
+        in_specs=[block(ru), block(rt), weights(wzu), weights(wzt)],
+        out_specs=[
+            pl.BlockSpec(x.shape, lambda i: (0, 0), pipeline_mode=pl.Buffered(1)) for x in shapes
+        ],
+        compiler_params=pltpu.CompilerParams(vmem_limit_bytes=plan.vmem),
+        cost_estimate=pl.CostEstimate(flops=3 * 10**9, bytes_accessed=8 * 10**6, transcendentals=0),
+        name=plan.name,
+    )(ru, rt, wzu, wzt)
 
 
 class Plan:
@@ -251,7 +342,6 @@
     n_all = n_up + plan.turned
     used = (plan.upright if plan.upright_back else 0) + (plan.turned if plan.turned_back else 0)
     plan.lines = used * plan.depth
-    total = plan.rows + plan.side
     shift = plan.upright - n_up
     once = pl.Buffered(1)
 
@@ -271,6 +361,7 @@
         specs.append(spec)
 
     if plan.forward:
+        give(a["ahead_c"], per_view(a["ahead_c"], first, n_all))
         for x in a["volumes"]:
             give(x, whole(x))
         give(a["wzf"], whole(a["wzf"]))
@@ -300,18 +391,26 @@
 
     shapes = [
         jax.ShapeDtypeStruct((count * n, plan.width), F32)
-        for n in (plan.rows, plan.side)
+        for n in (plan.side,)
         for count in (plan.depth, plan.reach, plan.reach)
     ]
     out_specs = [whole(x) for x in shapes]
+    for used, begin, count in (
+        (plan.upright_back, first, plan.upright),
+        (plan.turned_back, first + n_up, plan.turned),
+    ):
+        if used:
+            x = jax.ShapeDtypeStruct((count, plan.rows * (plan.depth + 2), plan.width), F32)
+            shapes.append(x)
+            out_specs.append(per_view(x, begin, count))
     if not plan.turned_back:
         x = jax.ShapeDtypeStruct((plan.turned, plan.depth * plan.rows, plan.width), F32)
         shapes.append(x)
         out_specs.append(per_view(x, first + n_up, plan.turned))
     scratch = []
     if plan.forward:
-        scratch.append(pltpu.VMEM((n_all * plan.depth * (total + 2), plan.width), F32))
-    scratch.append(pltpu.VMEM((total * (plan.lines + 8), plan.width), F32))
+        scratch.append(pltpu.VMEM((n_all * plan.depth * (plan.side + 2), plan.width), F32))
+    scratch.append(pltpu.VMEM((plan.side * (plan.lines + 8), plan.width), F32))
     if plan.turned_back and not plan.forward:
         scratch += [pltpu.VMEM(x.shape, F32) for x in a["acc"]]
         scratch.append(pltpu.SemaphoreType.DMA((len(a["acc"]),)))
@@ -535,36 +634,52 @@
     head = ((0, depth - reach), (0, 0), (0, 0))
     tail = ((depth - reach, 0), (0, 0), (0, 0))
     back = dict(wxb=wx_b, wyb=wy_b)
-    ahead = dict(wzf=wz_f, wyf=wy_f, wxf=wx_f)
+    shared = dict(wzf=wz_f, wyf=wy_f, wxf=wx_f)
     estimate = prior_estimate
     for iteration in range(ITERS):
         from_left, from_right = exchange(
             estimate[:, :ypad], estimate[:, rows - ypad :], "xy"
         )
-        source = estimate
         if iteration == 0:
-            packed, source, from_left, from_right = lax.optimization_barrier(
-                (packed, estimate, from_left, from_right)
+            packed, from_left, from_right = lax.optimization_barrier(
+                (packed, from_left, from_right)
             )
             received = lax.all_to_all(packed, "xy", split_axis=0, concat_axis=0, tiled=True)
-        below, above = exchange(source[:reach], source[depth - reach :], "gz")
+        below, above = exchange(estimate[:reach], estimate[depth - reach :], "gz")
         sides = jnp.concatenate([from_left, from_right], axis=1)
         side_below, side_above = exchange(sides[:reach], sides[depth - reach :], "gz")
-        volumes = [flat(x) for x in (estimate, below, above, sides, side_below, side_above)]
+        early = ahead(
+            Plan(name="ahead", vmem=24 << 20, **common),
+            flat(estimate),
+            flat(below),
+            flat(above),
+            wz_f,
+        )
+        volumes = [flat(x) for x in (sides, side_below, side_above)]
+        forth = dict(ahead_c=early.reshape(views, -1, width), volumes=volumes, **shared)
         if iteration == 0:
-            *acc, blurred = update(
+            *acc, lines_u, blurred = update(
                 Plan(
-                    name="first", vmem=56 << 20, forward=True, upright_back=True, turned_back=False, **common
+                    name="first",
+                    vmem=SPLIT[0] << 20,
+                    forward=True,
+                    upright_back=True,
+                    turned_back=False,
+                    **common,
                 ),
-                volumes=volumes,
                 obs_u=upright,
                 wzb_u=wzb_u,
-                **ahead,
+                **forth,
                 **back,
             )
-            parts = update(
+            *parts, lines_t = update(
                 Plan(
-                    name="second", vmem=56 << 20, forward=False, upright_back=False, turned_back=True, **common
+                    name="second",
+                    vmem=SPLIT[1] << 20,
+                    forward=False,
+                    upright_back=False,
+                    turned_back=True,
+                    **common,
                 ),
                 obs_t=received,
                 wzb_t=wzb_t,
@@ -573,18 +688,29 @@
                 **back,
             )
         else:
-            parts = update(
-                Plan(name="both", vmem=36 << 20, forward=True, upright_back=True, turned_back=True, **common),
-                volumes=volumes,
+            *parts, lines_u, lines_t = update(
+                Plan(
+                    name="both",
+                    vmem=SPLIT[2] << 20,
+                    forward=True,
+                    upright_back=True,
+                    turned_back=True,
+                    **common,
+                ),
                 obs_u=upright,
                 obs_t=received,
                 wzb_u=wzb_u,
                 wzb_t=wzb_t,
-                **ahead,
+                **forth,
                 **back,
             )
-        cc, clo, chi = (cube(x, rows) for x in parts[:3])
-        sc, slo, shi = (cube(x, side) for x in parts[3:])
+        sc, slo, shi = (cube(x, side) for x in parts)
+        cc, clo, chi = (
+            cube(x, rows)
+            for x in behind(
+                Plan(name="behind", vmem=24 << 20, **common), lines_u, lines_t, wzb_u, wzb_t
+            )
+        )
         s_low, s_high = exchange(slo, shi, "gz")
         c_low, c_high = exchange(clo, chi, "gz")
         sc = sc + jnp.pad(s_low, head) + jnp.pad(s_high, tail)

time: 206 us -> 195 us (0.947)
  waiting for transfers between devices: 50.6 us -> 39.8 us
  local copies, waits for them, and re-layouts: 4.97 us -> 11.2 us
  starting transfers between devices: 59.3 us -> 55.3 us
  other arithmetic: 14 us -> 10.8 us
    pallas_call x0 -> x4, Pallas kernels: none -> 12.1 us  [the longest x2 6.85 us: ahead(): pl.pallas_call(functools.partial(ahead_kernel, plan), out_shape=jax.Shape...]
    pallas_call x3, Pallas kernels: 63.7 us -> 53.4 us  [update(): pl.pallas_call(functools.partial(update_kernel, plan), out_shape=shapes,...]
    ppermute x12, waiting for transfers between devices: 44.4 us -> 35.2 us  [exchange(): b = lax.ppermute(jnp.where(even, low, high), axis, rounds[1])]
    unnamed x36 -> x42, local copies, waits for them, and re-layouts: 4.93 us -> 10.1 us
    ppermute x12, starting transfers between devices: 15 us -> 10.9 us  [exchange(): a = lax.ppermute(jnp.where(even, high, low), axis, rounds[0])]
    ppermute x12, waiting for transfers between devices: 6.25 us -> 3.34 us  [exchange(): a = lax.ppermute(jnp.where(even, high, low), axis, rounds[0])]
  transfers between devices with their start and end apart: 25 -> 25, of which waited for: 9 -> 9; matrix products, arithmetic and copies ran while one was open for 5% -> 4% of each run, Pallas kernels for 17% -> 22%
where the time goes in v3:
time: 195 us; the launch traced here: 194 us
  Pallas kernels  75.8 us (39%)
  starting transfers between devices  55.3 us (28%)
  waiting for transfers between devices  39.8 us (20%)
  local copies, waits for them, and re-layouts  11.2 us (6%)
  other arithmetic  10.8 us (6%)
    pallas_call x3, Pallas kernels, update(): pl.pallas_call(functools.partial(update_kernel, plan), out_shape=shapes,...  53.4 us
    ppermute x12, starting transfers between devices, exchange(): b = lax.ppermute(jnp.where(even, low, high), axis, rounds[1])  38 us
    ppermute x12, waiting for transfers between devices, exchange(): b = lax.ppermute(jnp.where(even, low, high), axis, rounds[1])  35.2 us
    ppermute x12, starting transfers between devices, exchange(): a = lax.ppermute(jnp.where(even, high, low), axis, rounds[0])  10.9 us
    unnamed x42, local copies, waits for them, and re-layouts  10.1 us
    pallas_call x1, Pallas kernels, bands(): pl.pallas_call(functools.partial(bands_kernel, plan), out_shape=[jax.Shap...  7.04 us
    pallas_call x2, Pallas kernels, ahead(): pl.pallas_call(functools.partial(ahead_kernel, plan), out_shape=jax.Shape...  6.85 us
    all_to_all x1, starting transfers between devices, local(): lax.all_to_all(packed, 'xy', split_axis=0, concat_axis=0, tiled=True)  6.41 us
  transfers between devices with their start and end apart: 25, of which 9 were waited for; matrix products, arithmetic and copies ran while one was open for 4% of the time, Pallas kernels for 22%

profile of v3, /device:TPU:1, one launch (start us, length us, event | category | flops | bytes accessed | tf_op | source)
XLA Modules:
  0.0 193.7 jit_solution(17096517057013068642)
XLA Ops:
  0.0 1.2 slice_select_fusion.12
  1.2 2.2 %collective-permute-start.3 = (f32[48,16,128]{2,1,0:T(8,128)S(1)}, f32[48,16,128]{2,1,0:T(8,128)S(1)}, u32[]{:S(2)}, u32[]{:S(2)}) collective-permute-start(f32[48,16,128]{2,1,0:T(8,128)S(1)} %get-tuple-element.111), channel_id=1, source_target_pairs={{0,1},{1,0},{2,3},{3,2},{4,5},{5,4},{6,7},{7,6},{8,9},{9,8},{10,11... | collective-permute-start | bytes 1179656 | tf_op jit(solution)/shard_map/ppermute | solution.py:28
  3.4 0.7 collective-permute-start.2
  4.1 1.7 copy-done.1
  5.7 3.2 %pack.1 = f32[4,36,32,128]{3,2,1,0:T(8,128)} custom-call(f32[144,32,128]{2,1,0:T(8,128)S(1)} %bitcast.32), custom_call_target="tpu_custom_call" | custom-call | tf_op jit(solution)/shard_map/pack/pallas_call | solution.py:444
  8.9 3.3 %collective-permute-done.3 = f32[48,16,128]{2,1,0:T(8,128)S(1)} collective-permute-done((f32[48,16,128]{2,1,0:T(8,128)S(1)}, f32[48,16,128]{2,1,0:T(8,128)S(1)}, u32[]{:S(2)}, u32[]{:S(2)}) %collective-permute-start.3) | collective-permute-done | bytes 393248 | tf_op jit(solution)/shard_map/ppermute | solution.py:28
  12.2 0.8 broadcast_select_fusion.32
  13.0 6.4 %all-to-all-start = ((f32[4,36,32,128]{3,2,1,0:T(8,128)}), f32[4,36,32,128]{3,2,1,0:T(8,128)S(1)}, u32[]{:S(2)}, u32[]{:S(2)}) async-start(f32[4,36,32,128]{3,2,1,0:T(8,128)} %pack.1), calls=%async_computation | async-start | bytes 4718592 | tf_op jit(solution)/shard_map/all_to_all | solution.py:647
  19.5 1.1 slice_select_fusion.4
  20.6 2.1 %collective-permute-start.1 = (f32[30,32,128]{2,1,0:T(8,128)}, f32[30,32,128]{2,1,0:T(8,128)}, u32[]{:S(2)}, u32[]{:S(2)}) collective-permute-start(f32[30,32,128]{2,1,0:T(8,128)} %get-tuple-element.107), channel_id=1, source_target_pairs={{0,4},{4,0},{8,12},{12,8},{16,20},{20,16},{24,28},{28,24},{1,5},{5... | collective-permute-start | bytes 1474568 | tf_op jit(solution)/shard_map/ppermute | solution.py:28
  22.7 3.0 %collective-permute-start = (f32[30,32,128]{2,1,0:T(8,128)}, f32[30,32,128]{2,1,0:T(8,128)}, u32[]{:S(2)}, u32[]{:S(2)}) collective-permute-start(f32[30,32,128]{2,1,0:T(8,128)} %get-tuple-element.108), channel_id=1, source_target_pairs={{4,8},{8,4},{12,16},{16,12},{20,24},{24,20},{5,9},{9,5},{13,17},{1... | collective-permute-start | bytes 1474568 | tf_op jit(solution)/shard_map/ppermute | solution.py:29
  25.7 0.7 copy.9.views_of
  26.4 0.6 pad_add_fusion.2.place
  27.0 7.0 %bands.1 = (bf16[288,336]{1,0:T(8,128)(2,1)}, bf16[6,64,128]{2,1,0:T(8,128)(2,1)}, bf16[6,256,256]{2,1,0:T(8,128)(2,1)}, bf16[6,256,256]{2,1,0:T(8,128)(2,1)}, b...) custom-call(s32[2]{0:T(128)} %pad_add_fusion.2.place, ...), custom_call_target="tpu_custom_call" | custom-call | tf_op jit(solution)/shard_map/bands/pallas_call | solution.py:572
  34.1 1.1 constant_dynamic-update-slice_fusion
  35.2 0.1 slice_select_fusion.2
  35.4 3.5 %collective-permute-start.4 = (f32[30,32,128]{2,1,0:T(8,128)S(1)}, f32[30,32,128]{2,1,0:T(8,128)S(1)}, u32[]{:S(2)}, u32[]{:S(2)}) collective-permute-start(f32[30,32,128]{2,1,0:T(8,128)S(1)} %get-tuple-element.106), channel_id=1, source_target_pairs={{4,8},{8,4},{12,16},{16,12},{20,24},{24,20},{5,9},{9,5},{13,17},{1... | collective-permute-start | bytes 1474568 | tf_op jit(solution)/shard_map/ppermute | solution.py:29
  38.9 1.3 broadcast_select_fusion.24
  40.2 3.4 %ahead.2 = f32[9792,128]{1,0:T(8,128)S(1)} custom-call(f32[1536,128]{1,0:T(8,128)S(1)} %bitcast.31, f32[960,128]{1,0:T(8,128)S(1)} %bitcast.40, f32[960,128]{1,0:T(8,128)S(1)} %bitcast.39, bf16[288,336]{1,0:T(8,128)(2,1)S(1)} %copy-done.9), custom_call_target="tpu_custom_call" | custom-call | flops 3000000000 | bytes 8000000 | tf_op jit(solution)/shard_map/ahead/pallas_call | solution.py:271
  43.7 2.3 %copy-done.14 = f32[9792,128]{1,0:T(8,128)} copy-done((f32[9792,128]{1,0:T(8,128)}, f32[9792,128]{1,0:T(8,128)S(1)}, u32[]{:S(2)}) %copy-start.14) | copy-done | bytes 5013528
  45.9 4.2 %collective-permute-done.4 = f32[30,32,128]{2,1,0:T(8,128)S(1)} collective-permute-done((f32[30,32,128]{2,1,0:T(8,128)S(1)}, f32[30,32,128]{2,1,0:T(8,128)S(1)}, u32[]{:S(2)}, u32[]{:S(2)}) %collective-permute-start.4) | collective-permute-done | bytes 491552 | tf_op jit(solution)/shard_map/ppermute | solution.py:29
  50.1 1.1 broadcast_select_fusion.22
  51.2 20.4 %first.1 = (f32[1536,128]{1,0:T(8,128)}, f32[960,128]{1,0:T(8,128)}, f32[960,128]{1,0:T(8,128)}, f32[3,1600,128]{2,1,0:T(8,128)}, f32[3,1536,128]{2,1,0:T(8,128)}) custom-call(f32[6,1632,128]{2,1,0:T(8,128)} %bitcast.46, f32[1536,128]{1,0:T(8,128)} %bitcast.47, f32[960,128]{1,0:T(8,128)} %bitcast.58, f32[960,128]{1,0:T(8,128)} %bitcast.57, ...), custom_call_target="tpu_custom_call" | custom-call | flops 10000000000 | bytes 12000000 | tf_op jit(solution)/shard_map/first/pallas_call | solution.py:417
  71.6 1.2 all-to-all-done.refs_0_.refs_9_
  72.8 1.5 copy-done.2
  74.2 9.5 %second.1 = (f32[1536,128]{1,0:T(8,128)}, f32[960,128]{1,0:T(8,128)}, f32[960,128]{1,0:T(8,128)}, f32[3,1600,128]{2,1,0:T(8,128)}) custom-call(f32[4,36,32,128]{3,2,1,0:T(8,128)} %copy-done.2, bf16[3,112,432]{2,1,0:T(8,128)(2,1)} %get-tuple-element.45.refs_1_.wzt.refs_10_, f32[3,1536,128]{2,1,0:T(8,128)} %get-tuple-element.46.refs_2_, ...), custom_call_target="tpu_custom_call" | custom-call | flops 10000000000 | bytes 12000000 | tf_op jit(solution)/shard_map/second/pallas_call | solution.py:417
  83.8 1.2 broadcast_select_fusion.5
  85.0 1.5 collective-permute-start.9
  86.5 3.2 %collective-permute-start.8 = (f32[30,32,128]{2,1,0:T(8,128)S(1)}, f32[30,32,128]{2,1,0:T(8,128)S(1)}, u32[]{:S(2)}, u32[]{:S(2)}) collective-permute-start(f32[30,32,128]{2,1,0:T(8,128)S(1)} %bitcast.54), channel_id=1, source_target_pairs={{4,8},{8,4},{12,16},{16,12},{20,24},{24,20},{5,9},{9,5},{13,17},{1... | collective-permute-start | bytes 1474568 | tf_op jit(solution)/shard_map/ppermute | solution.py:29
  89.8 1.7 copy-done.16
  91.5 2.6 %behind.2 = (f32[1536,128]{1,0:T(8,128)S(1)}, f32[960,128]{1,0:T(8,128)S(1)}, f32[960,128]{1,0:T(8,128)S(1)}) custom-call(f32[3,1600,128]{2,1,0:T(8,128)S(1)} %copy-done.15, f32[3,1600,128]{2,1,0:T(8,128)S(1)} %copy-done.16, bf16[3,112,432]{2,1,0:T(8,128)(2,1)S(1)} %copy-done.7, bf16[3,112,432]{2,1,0:T(8,128)(2,1)S(1)} %copy-done.8), custom_call_target="tpu_custom_call" | custom-call | flops 3000000000 | bytes 8000000 | tf_op jit(solution)/shard_map/behind/pallas_call | solution.py:320
  94.3 3.5 %collective-permute-start.6 = (f32[30,32,128]{2,1,0:T(8,128)S(1)}, f32[30,32,128]{2,1,0:T(8,128)S(1)}, u32[]{:S(2)}, u32[]{:S(2)}) collective-permute-start(f32[30,32,128]{2,1,0:T(8,128)S(1)} %bitcast.49), channel_id=1, source_target_pairs={{4,8},{8,4},{12,16},{16,12},{20,24},{24,20},{5,9},{9,5},{13,17},{1... | collective-permute-start | bytes 1474568 | tf_op jit(solution)/shard_map/ppermute | solution.py:29
  97.8 4.1 %collective-permute-done.8 = f32[30,32,128]{2,1,0:T(8,128)S(1)} collective-permute-done((f32[30,32,128]{2,1,0:T(8,128)S(1)}, f32[30,32,128]{2,1,0:T(8,128)S(1)}, u32[]{:S(2)}, u32[]{:S(2)}) %collective-permute-start.8) | collective-permute-done | bytes 491552 | tf_op jit(solution)/shard_map/ppermute | solution.py:29
  101.9 0.1 broadcast_select_fusion.19
  102.1 0.2 pad_add_fusion.1
  102.3 0.7 collective-permute-start.10
  103.0 1.4 collective-permute-start.11
  104.4 8.1 %collective-permute-done.6 = f32[30,32,128]{2,1,0:T(8,128)S(1)} collective-permute-done((f32[30,32,128]{2,1,0:T(8,128)S(1)}, f32[30,32,128]{2,1,0:T(8,128)S(1)}, u32[]{:S(2)}, u32[]{:S(2)}) %collective-permute-start.6) | collective-permute-done | bytes 491552 | tf_op jit(solution)/shard_map/ppermute | solution.py:29
  112.7 0.3 add_multiply_fusion.1
  113.1 0.7 collective-permute-start.14
  113.8 1.4 collective-permute-start.15
  115.1 0.1 slice_select_fusion
  115.3 5.8 %collective-permute-start.12 = (f32[30,32,128]{2,1,0:T(8,128)S(1)}, f32[30,32,128]{2,1,0:T(8,128)S(1)}, u32[]{:S(2)}, u32[]{:S(2)}) collective-permute-start(f32[30,32,128]{2,1,0:T(8,128)S(1)} %get-tuple-element.100), channel_id=1, source_target_pairs={{4,8},{8,4},{12,16},{16,12},{20,24},{24,20},{5,9},{9,5},{13,17},{1... | collective-permute-start | bytes 1474568 | tf_op jit(solution)/shard_map/ppermute | solution.py:29
  121.2 0.1 broadcast_select_fusion.14
  121.4 8.0 %collective-permute-start.16 = (f32[30,32,128]{2,1,0:T(8,128)S(1)}, f32[30,32,128]{2,1,0:T(8,128)S(1)}, u32[]{:S(2)}, u32[]{:S(2)}) collective-permute-start(f32[30,32,128]{2,1,0:T(8,128)S(1)} %get-tuple-element.94), channel_id=1, source_target_pairs={{4,8},{8,4},{12,16},{16,12},{20,24},{24,20},{5,9},{9,5},{13,17},{1... | collective-permute-start | bytes 1474568 | tf_op jit(solution)/shard_map/ppermute | solution.py:29
  129.4 0.1 pad_maximum_fusion
  129.5 2.1 %collective-permute-done.12 = f32[30,32,128]{2,1,0:T(8,128)S(1)} collective-permute-done((f32[30,32,128]{2,1,0:T(8,128)S(1)}, f32[30,32,128]{2,1,0:T(8,128)S(1)}, u32[]{:S(2)}, u32[]{:S(2)}) %collective-permute-start.12) | collective-permute-done | bytes 491552 | tf_op jit(solution)/shard_map/ppermute | solution.py:29
  131.6 0.1 broadcast_select_fusion.16
  131.8 3.4 %ahead.3 = f32[9792,128]{1,0:T(8,128)S(1)} custom-call(f32[1536,128]{1,0:T(8,128)S(1)} %bitcast.30, f32[960,128]{1,0:T(8,128)S(1)} %bitcast.42, f32[960,128]{1,0:T(8,128)S(1)} %bitcast.41, bf16[288,336]{1,0:T(8,128)(2,1)S(1)} %copy-done.10), custom_call_target="tpu_custom_call" | custom-call | flops 3000000000 | bytes 8000000 | tf_op jit(solution)/shard_map/ahead/pallas_call | solution.py:271
  135.3 2.3 %copy-done.13 = f32[9792,128]{1,0:T(8,128)} copy-done((f32[9792,128]{1,0:T(8,128)}, f32[9792,128]{1,0:T(8,128)S(1)}, u32[]{:S(2)}) %copy-start.13) | copy-done | bytes 5013528
  137.5 4.6 %collective-permute-done.16 = f32[30,32,128]{2,1,0:T(8,128)S(1)} collective-permute-done((f32[30,32,128]{2,1,0:T(8,128)S(1)}, f32[30,32,128]{2,1,0:T(8,128)S(1)}, u32[]{:S(2)}, u32[]{:S(2)}) %collective-permute-start.16) | collective-permute-done | bytes 491552 | tf_op jit(solution)/shard_map/ppermute | solution.py:29
  142.2 0.1 broadcast_select_fusion.12
  142.4 23.5 %both.1 = (f32[1536,128]{1,0:T(8,128)S(1)}, f32[960,128]{1,0:T(8,128)S(1)}, f32[960,128]{1,0:T(8,128)S(1)}, f32[3,1600,128]{2,1,0:T(8,128)S(1)}, f32[3,1600,128]{2,1,0:T(8,128)S(1)}) custom-call(f32[6,1632,128]{2,1,0:T(8,128)} %bitcast.45, f32[1536,128]{1,0:T(8,128)S(1)} %bitcast.33, f32[960,128]{1,0:T(8,128)S(1)} %bitcast.38, f32[960,128]{1,0:T(8,128)S(1)} %bitcast.37, ...), custom_call_target="tpu_custom_call" | custom-call | flops 10000000000 | bytes 12000000 | tf_op jit(solution)/shard_map/both/pallas_call | solution.py:417
  166.1 4.8 %collective-permute-start.20 = (f32[30,32,128]{2,1,0:T(8,128)S(1)}, f32[30,32,128]{2,1,0:T(8,128)S(1)}, u32[]{:S(2)}, u32[]{:S(2)}) collective-permute-start(f32[30,32,128]{2,1,0:T(8,128)S(1)} %bitcast.53), channel_id=1, source_target_pairs={{4,8},{8,4},{12,16},{16,12},{20,24},{24,20},{5,9},{9,5},{13,17},{1... | collective-permute-start | bytes 1474568 | tf_op jit(solution)/shard_map/ppermute | solution.py:29
  170.9 2.7 %behind.3 = (f32[1536,128]{1,0:T(8,128)S(1)}, f32[960,128]{1,0:T(8,128)S(1)}, f32[960,128]{1,0:T(8,128)S(1)}) custom-call(f32[3,1600,128]{2,1,0:T(8,128)S(1)} %get-tuple-element.57.ru, f32[3,1600,128]{2,1,0:T(8,128)S(1)} %get-tuple-element.58.rt, bf16[3,112,432]{2,1,0:T(8,128)(2,1)S(1)} %copy-done.7, bf16[3,112,432]{2,1,0:T(8,128)(2,1)S(1)} %copy-done.8), custom_call_target="tpu_custom_call" | custom-call | flops 3000000000 | bytes 8000000 | tf_op jit(solution)/shard_map/behind/pallas_call | solution.py:320
  173.7 3.5 %collective-permute-start.18 = (f32[30,32,128]{2,1,0:T(8,128)S(1)}, f32[30,32,128]{2,1,0:T(8,128)S(1)}, u32[]{:S(2)}, u32[]{:S(2)}) collective-permute-start(f32[30,32,128]{2,1,0:T(8,128)S(1)} %bitcast.50), channel_id=1, source_target_pairs={{4,8},{8,4},{12,16},{16,12},{20,24},{24,20},{5,9},{9,5},{13,17},{1... | collective-permute-start | bytes 1474568 | tf_op jit(solution)/shard_map/ppermute | solution.py:29
  177.3 4.7 %collective-permute-done.20 = f32[30,32,128]{2,1,0:T(8,128)S(1)} collective-permute-done((f32[30,32,128]{2,1,0:T(8,128)S(1)}, f32[30,32,128]{2,1,0:T(8,128)S(1)}, u32[]{:S(2)}, u32[]{:S(2)}) %collective-permute-start.20) | collective-permute-done | bytes 491552 | tf_op jit(solution)/shard_map/ppermute | solution.py:29
  182.0 0.1 broadcast_select_fusion.9
  182.1 0.2 pad_add_fusion
  182.3 0.7 collective-permute-start.22
  183.0 1.9 collective-permute-start.23
  184.9 7.3 %collective-permute-done.18 = f32[30,32,128]{2,1,0:T(8,128)S(1)} collective-permute-done((f32[30,32,128]{2,1,0:T(8,128)S(1)}, f32[30,32,128]{2,1,0:T(8,128)S(1)}, u32[]{:S(2)}, u32[]{:S(2)}) %collective-permute-start.18) | collective-permute-done | bytes 491552 | tf_op jit(solution)/shard_map/ppermute | solution.py:29
  192.2 0.1 broadcast_select_fusion.11
  192.4 1.2 add_multiply_fusion
  (68 shorter events, 1.2 us)
Async XLA Ops:
  1.2 11.0 %collective-permute-start.3 = (f32[48,16,128]{2,1,0:T(8,128)S(1)}, f32[48,16,128]{2,1,0:T(8,128)S(1)}, u32[]{:S(2)}, u32[]{:S(2)}) collective-permute-start(f32[48,16,128]{2,1,0:T(8,128)S(1)} %get-tuple-element.111), channel_id=1, source_target_pairs={{0,1},{1,0},{2,3},{3,2},{4,5},{5,4},{6,7},{7,6},{8,9},{9,8},{10,11... | collective-permute-start | bytes 1179656 | tf_op jit(solution)/shard_map/ppermute | solution.py:28
  3.4 8.8 %collective-permute-start.2 = (f32[48,16,128]{2,1,0:T(8,128)S(1)}, f32[48,16,128]{2,1,0:T(8,128)S(1)}, u32[]{:S(2)}, u32[]{:S(2)}) collective-permute-start(f32[48,16,128]{2,1,0:T(8,128)S(1)} %get-tuple-element.112), channel_id=1, source_target_pairs={{1,2},{2,1},{5,6},{6,5},{9,10},{10,9},{13,14},{14,13},{17,18},{18,... | collective-permute-start | bytes 1179656 | tf_op jit(solution)/shard_map/ppermute | solution.py:29
  4.1 1.7 copy-start.1
  13.0 6.4 %copy-start = (f32[48,32,128]{2,1,0:T(8,128)S(1)}, f32[48,32,128]{2,1,0:T(8,128)}, u32[]{:S(2)}) copy-start(f32[48,32,128]{2,1,0:T(8,128)} %param.8) | copy-start | bytes 2359300
  13.0 12.7 %copy-start.19 = (s32[32,3]{0,1:T(4,128)S(1)}, s32[32,3]{0,1:T(4,128)}, u32[]{:S(2)}) copy-start(s32[32,3]{0,1:T(4,128)} %param.15) | copy-start | bytes 1156
  13.0 59.7 %all-to-all-start = ((f32[4,36,32,128]{3,2,1,0:T(8,128)}), f32[4,36,32,128]{3,2,1,0:T(8,128)S(1)}, u32[]{:S(2)}, u32[]{:S(2)}) async-start(f32[4,36,32,128]{3,2,1,0:T(8,128)} %pack.1), calls=%async_computation | async-start | bytes 4718592 | tf_op jit(solution)/shard_map/all_to_all | solution.py:647
  20.6 18.4 %collective-permute-start.1 = (f32[30,32,128]{2,1,0:T(8,128)}, f32[30,32,128]{2,1,0:T(8,128)}, u32[]{:S(2)}, u32[]{:S(2)}) collective-permute-start(f32[30,32,128]{2,1,0:T(8,128)} %get-tuple-element.107), channel_id=1, source_target_pairs={{0,4},{4,0},{8,12},{12,8},{16,20},{20,16},{24,28},{28,24},{1,5},{5... | collective-permute-start | bytes 1474568 | tf_op jit(solution)/shard_map/ppermute | solution.py:28
  22.7 16.2 %collective-permute-start = (f32[30,32,128]{2,1,0:T(8,128)}, f32[30,32,128]{2,1,0:T(8,128)}, u32[]{:S(2)}, u32[]{:S(2)}) collective-permute-start(f32[30,32,128]{2,1,0:T(8,128)} %get-tuple-element.108), channel_id=1, source_target_pairs={{4,8},{8,4},{12,16},{16,12},{20,24},{24,20},{5,9},{9,5},{13,17},{1... | collective-permute-start | bytes 1474568 | tf_op jit(solution)/shard_map/ppermute | solution.py:29
  34.1 6.1 %copy-start.9 = (bf16[288,336]{1,0:T(8,128)(2,1)S(1)}, bf16[288,336]{1,0:T(8,128)(2,1)}, u32[]{:S(2)}) copy-start(bf16[288,336]{1,0:T(8,128)(2,1)} %get-tuple-element.35.wzf.refs_4_) | copy-start | bytes 580612
  35.2 8.5 %copy-start.17 = (f32[48,32,128]{2,1,0:T(8,128)}, f32[48,32,128]{2,1,0:T(8,128)S(1)}, u32[]{:S(2)}) copy-start(f32[48,32,128]{2,1,0:T(8,128)S(1)} %constant_dynamic-update-slice_fusion) | copy-start | bytes 2359300
  35.4 10.6 %collective-permute-start.5 = (f32[30,32,128]{2,1,0:T(8,128)S(1)}, f32[30,32,128]{2,1,0:T(8,128)S(1)}, u32[]{:S(2)}, u32[]{:S(2)}) collective-permute-start(f32[30,32,128]{2,1,0:T(8,128)S(1)} %get-tuple-element.105), channel_id=1, source_target_pairs={{0,4},{4,0},{8,12},{12,8},{16,20},{20,16},{24,28},{28,24},{1,5},{5... | collective-permute-start | bytes 1474568 | tf_op jit(solution)/shard_map/ppermute | solution.py:28
  35.4 14.7 %collective-permute-start.4 = (f32[30,32,128]{2,1,0:T(8,128)S(1)}, f32[30,32,128]{2,1,0:T(8,128)S(1)}, u32[]{:S(2)}, u32[]{:S(2)}) collective-permute-start(f32[30,32,128]{2,1,0:T(8,128)S(1)} %get-tuple-element.106), channel_id=1, source_target_pairs={{4,8},{8,4},{12,16},{16,12},{20,24},{24,20},{5,9},{9,5},{13,17},{1... | collective-permute-start | bytes 1474568 | tf_op jit(solution)/shard_map/ppermute | solution.py:29
  43.7 2.3 %copy-start.14 = (f32[9792,128]{1,0:T(8,128)}, f32[9792,128]{1,0:T(8,128)S(1)}, u32[]{:S(2)}) copy-start(f32[9792,128]{1,0:T(8,128)S(1)} %ahead.2) | copy-start | bytes 15040516
  72.8 1.5 copy-start.2
  74.2 15.5 %copy-start.7 = (bf16[3,112,432]{2,1,0:T(8,128)(2,1)S(1)}, bf16[3,112,432]{2,1,0:T(8,128)(2,1)}, u32[]{:S(2)}) copy-start(bf16[3,112,432]{2,1,0:T(8,128)(2,1)} %get-tuple-element.40.refs_8_.wzu) | copy-start | bytes 870916
  74.2 15.5 %copy-start.8 = (bf16[3,112,432]{2,1,0:T(8,128)(2,1)S(1)}, bf16[3,112,432]{2,1,0:T(8,128)(2,1)}, u32[]{:S(2)}) copy-start(bf16[3,112,432]{2,1,0:T(8,128)(2,1)} %get-tuple-element.45.refs_1_.wzt.refs_10_) | copy-start | bytes 870916
  74.2 15.5 %copy-start.15 = (f32[3,1600,128]{2,1,0:T(8,128)S(1)}, f32[3,1600,128]{2,1,0:T(8,128)}, u32[]{:S(2)}) copy-start(f32[3,1600,128]{2,1,0:T(8,128)} %get-tuple-element.43.ru) | copy-start | bytes 7372804
  85.0 12.8 %collective-permute-start.9 = (f32[30,32,128]{2,1,0:T(8,128)S(1)}, f32[30,32,128]{2,1,0:T(8,128)S(1)}, u32[]{:S(2)}, u32[]{:S(2)}) collective-permute-start(f32[30,32,128]{2,1,0:T(8,128)S(1)} %bitcast.56), channel_id=1, source_target_pairs={{0,4},{4,0},{8,12},{12,8},{16,20},{20,16},{24,28},{28,24},{1,5},{5... | collective-permute-start | bytes 1474568 | tf_op jit(solution)/shard_map/ppermute | solution.py:28
  86.5 15.4 %collective-permute-start.8 = (f32[30,32,128]{2,1,0:T(8,128)S(1)}, f32[30,32,128]{2,1,0:T(8,128)S(1)}, u32[]{:S(2)}, u32[]{:S(2)}) collective-permute-start(f32[30,32,128]{2,1,0:T(8,128)S(1)} %bitcast.54), channel_id=1, source_target_pairs={{4,8},{8,4},{12,16},{16,12},{20,24},{24,20},{5,9},{9,5},{13,17},{1... | collective-permute-start | bytes 1474568 | tf_op jit(solution)/shard_map/ppermute | solution.py:29
  89.8 1.7 copy-start.16
  94.1 7.9 %copy-start.18 = (f32[1536,128]{1,0:T(8,128)S(1)}, f32[1536,128]{1,0:T(8,128)}, u32[]{:S(2)}) copy-start(f32[1536,128]{1,0:T(8,128)} %get-tuple-element.54) | copy-start | bytes 2359300
  94.2 10.2 %collective-permute-start.7 = (f32[30,32,128]{2,1,0:T(8,128)S(1)}, f32[30,32,128]{2,1,0:T(8,128)S(1)}, u32[]{:S(2)}, u32[]{:S(2)}) collective-permute-start(f32[30,32,128]{2,1,0:T(8,128)S(1)} %bitcast.51), channel_id=1, source_target_pairs={{0,4},{4,0},{8,12},{12,8},{16,20},{20,16},{24,28},{28,24},{1,5},{5... | collective-permute-start | bytes 1474568 | tf_op jit(solution)/shard_map/ppermute | solution.py:28
  94.3 18.2 %collective-permute-start.6 = (f32[30,32,128]{2,1,0:T(8,128)S(1)}, f32[30,32,128]{2,1,0:T(8,128)S(1)}, u32[]{:S(2)}, u32[]{:S(2)}) collective-permute-start(f32[30,32,128]{2,1,0:T(8,128)S(1)} %bitcast.49), channel_id=1, source_target_pairs={{4,8},{8,4},{12,16},{16,12},{20,24},{24,20},{5,9},{9,5},{13,17},{1... | collective-permute-start | bytes 1474568 | tf_op jit(solution)/shard_map/ppermute | solution.py:29
  102.3 10.3 %collective-permute-start.10 = (f32[48,16,128]{2,1,0:T(8,128)S(1)}, f32[48,16,128]{2,1,0:T(8,128)S(1)}, u32[]{:S(2)}, u32[]{:S(2)}) collective-permute-start(f32[48,16,128]{2,1,0:T(8,128)S(1)} %get-tuple-element.103), channel_id=1, source_target_pairs={{1,2},{2,1},{5,6},{6,5},{9,10},{10,9},{13,14},{14,13},{17,18},{18,... | collective-permute-start | bytes 1179656 | tf_op jit(solution)/shard_map/ppermute | solution.py:29
  103.0 9.6 %collective-permute-start.11 = (f32[48,16,128]{2,1,0:T(8,128)S(1)}, f32[48,16,128]{2,1,0:T(8,128)S(1)}, u32[]{:S(2)}, u32[]{:S(2)}) collective-permute-start(f32[48,16,128]{2,1,0:T(8,128)S(1)} %get-tuple-element.104), channel_id=1, source_target_pairs={{0,1},{1,0},{2,3},{3,2},{4,5},{5,4},{6,7},{7,6},{8,9},{9,8},{10,11... | collective-permute-start | bytes 1179656 | tf_op jit(solution)/shard_map/ppermute | solution.py:28
  113.1 8.1 %collective-permute-start.14 = (f32[48,16,128]{2,1,0:T(8,128)S(1)}, f32[48,16,128]{2,1,0:T(8,128)S(1)}, u32[]{:S(2)}, u32[]{:S(2)}) collective-permute-start(f32[48,16,128]{2,1,0:T(8,128)S(1)} %get-tuple-element.97), channel_id=1, source_target_pairs={{1,2},{2,1},{5,6},{6,5},{9,10},{10,9},{13,14},{14,13},{17,18},{18,... | collective-permute-start | bytes 1179656 | tf_op jit(solution)/shard_map/ppermute | solution.py:29
  113.8 7.4 %collective-permute-start.15 = (f32[48,16,128]{2,1,0:T(8,128)S(1)}, f32[48,16,128]{2,1,0:T(8,128)S(1)}, u32[]{:S(2)}, u32[]{:S(2)}) collective-permute-start(f32[48,16,128]{2,1,0:T(8,128)S(1)} %get-tuple-element.98), channel_id=1, source_target_pairs={{0,1},{1,0},{2,3},{3,2},{4,5},{5,4},{6,7},{7,6},{8,9},{9,8},{10,11... | collective-permute-start | bytes 1179656 | tf_op jit(solution)/shard_map/ppermute | solution.py:28
  115.3 14.3 %collective-permute-start.13 = (f32[30,32,128]{2,1,0:T(8,128)S(1)}, f32[30,32,128]{2,1,0:T(8,128)S(1)}, u32[]{:S(2)}, u32[]{:S(2)}) collective-permute-start(f32[30,32,128]{2,1,0:T(8,128)S(1)} %get-tuple-element.99), channel_id=1, source_target_pairs={{0,4},{4,0},{8,12},{12,8},{16,20},{20,16},{24,28},{28,24},{1,5},{5... | collective-permute-start | bytes 1474568 | tf_op jit(solution)/shard_map/ppermute | solution.py:28
  115.3 16.3 %collective-permute-start.12 = (f32[30,32,128]{2,1,0:T(8,128)S(1)}, f32[30,32,128]{2,1,0:T(8,128)S(1)}, u32[]{:S(2)}, u32[]{:S(2)}) collective-permute-start(f32[30,32,128]{2,1,0:T(8,128)S(1)} %get-tuple-element.100), channel_id=1, source_target_pairs={{4,8},{8,4},{12,16},{16,12},{20,24},{24,20},{5,9},{9,5},{13,17},{1... | collective-permute-start | bytes 1474568 | tf_op jit(solution)/shard_map/ppermute | solution.py:29
  121.2 10.6 %copy-start.10 = (bf16[288,336]{1,0:T(8,128)(2,1)S(1)}, bf16[288,336]{1,0:T(8,128)(2,1)}, u32[]{:S(2)}) copy-start(bf16[288,336]{1,0:T(8,128)(2,1)} %get-tuple-element.35.wzf.refs_4_) | copy-start | bytes 580612
  121.3 16.2 %collective-permute-start.17 = (f32[30,32,128]{2,1,0:T(8,128)S(1)}, f32[30,32,128]{2,1,0:T(8,128)S(1)}, u32[]{:S(2)}, u32[]{:S(2)}) collective-permute-start(f32[30,32,128]{2,1,0:T(8,128)S(1)} %get-tuple-element.93), channel_id=1, source_target_pairs={{0,4},{4,0},{8,12},{12,8},{16,20},{20,16},{24,28},{28,24},{1,5},{5... | collective-permute-start | bytes 1474568 | tf_op jit(solution)/shard_map/ppermute | solution.py:28
  121.4 20.8 %collective-permute-start.16 = (f32[30,32,128]{2,1,0:T(8,128)S(1)}, f32[30,32,128]{2,1,0:T(8,128)S(1)}, u32[]{:S(2)}, u32[]{:S(2)}) collective-permute-start(f32[30,32,128]{2,1,0:T(8,128)S(1)} %get-tuple-element.94), channel_id=1, source_target_pairs={{4,8},{8,4},{12,16},{16,12},{20,24},{24,20},{5,9},{9,5},{13,17},{1... | collective-permute-start | bytes 1474568 | tf_op jit(solution)/shard_map/ppermute | solution.py:29
  131.8 10.5 %copy-start.3 = (f32[4,36,32,128]{3,2,1,0:T(8,128)S(1)}, f32[4,36,32,128]{3,2,1,0:T(8,128)}, u32[]{:S(2)}) copy-start(f32[4,36,32,128]{3,2,1,0:T(8,128)} %copy-done.2) | copy-start | bytes 7077892
  131.8 10.5 %copy-start.4 = (f32[3,48,32,128]{3,2,1,0:T(8,128)S(1)}, f32[3,48,32,128]{3,2,1,0:T(8,128)}, u32[]{:S(2)}) copy-start(f32[3,48,32,128]{3,2,1,0:T(8,128)} %param.9) | copy-start | bytes 7077892
  131.8 10.5 %copy-start.5 = (bf16[6,256,256]{2,1,0:T(8,128)(2,1)S(1)}, bf16[6,256,256]{2,1,0:T(8,128)(2,1)}, u32[]{:S(2)}) copy-start(bf16[6,256,256]{2,1,0:T(8,128)(2,1)} %get-tuple-element.39.refs_6_) | copy-start | bytes 2359300
  131.8 10.5 %copy-start.6 = (bf16[6,256,256]{2,1,0:T(8,128)(2,1)S(1)}, bf16[6,256,256]{2,1,0:T(8,128)(2,1)}, u32[]{:S(2)}) copy-start(bf16[6,256,256]{2,1,0:T(8,128)(2,1)} %get-tuple-element.41.refs_9_.refs_6_.refs_11_) | copy-start | bytes 2359300
  131.8 10.5 %copy-start.11 = (bf16[6,64,128]{2,1,0:T(8,128)(2,1)S(1)}, bf16[6,64,128]{2,1,0:T(8,128)(2,1)}, u32[]{:S(2)}) copy-start(bf16[6,64,128]{2,1,0:T(8,128)(2,1)} %get-tuple-element.38.refs_5_) | copy-start | bytes 294916
  131.8 10.5 %copy-start.12 = (bf16[6,64,96]{2,1,0:T(8,128)(2,1)S(1)}, bf16[6,64,96]{2,1,0:T(8,128)(2,1)}, u32[]{:S(2)}) copy-start(bf16[6,64,96]{2,1,0:T(8,128)(2,1)} %get-tuple-element.42.refs_10_.refs_7_.refs_12_) | copy-start | bytes 221188
  135.3 2.3 %copy-start.13 = (f32[9792,128]{1,0:T(8,128)}, f32[9792,128]{1,0:T(8,128)S(1)}, u32[]{:S(2)}) copy-start(f32[9792,128]{1,0:T(8,128)S(1)} %ahead.3) | copy-start | bytes 15040516
  166.0 11.3 %collective-permute-start.21 = (f32[30,32,128]{2,1,0:T(8,128)S(1)}, f32[30,32,128]{2,1,0:T(8,128)S(1)}, u32[]{:S(2)}, u32[]{:S(2)}) collective-permute-start(f32[30,32,128]{2,1,0:T(8,128)S(1)} %bitcast.55), channel_id=1, source_target_pairs={{0,4},{4,0},{8,12},{12,8},{16,20},{20,16},{24,28},{28,24},{1,5},{5... | collective-permute-start | bytes 1474568 | tf_op jit(solution)/shard_map/ppermute | solution.py:28
  166.1 15.9 %collective-permute-start.20 = (f32[30,32,128]{2,1,0:T(8,128)S(1)}, f32[30,32,128]{2,1,0:T(8,128)S(1)}, u32[]{:S(2)}, u32[]{:S(2)}) collective-permute-start(f32[30,32,128]{2,1,0:T(8,128)S(1)} %bitcast.53), channel_id=1, source_target_pairs={{4,8},{8,4},{12,16},{16,12},{20,24},{24,20},{5,9},{9,5},{13,17},{1... | collective-permute-start | bytes 1474568 | tf_op jit(solution)/shard_map/ppermute | solution.py:29
  173.6 11.3 %collective-permute-start.19 = (f32[30,32,128]{2,1,0:T(8,128)S(1)}, f32[30,32,128]{2,1,0:T(8,128)S(1)}, u32[]{:S(2)}, u32[]{:S(2)}) collective-permute-start(f32[30,32,128]{2,1,0:T(8,128)S(1)} %bitcast.52), channel_id=1, source_target_pairs={{0,4},{4,0},{8,12},{12,8},{16,20},{20,16},{24,28},{28,24},{1,5},{5... | collective-permute-start | bytes 1474568 | tf_op jit(solution)/shard_map/ppermute | solution.py:28
  173.7 18.5 %collective-permute-start.18 = (f32[30,32,128]{2,1,0:T(8,128)S(1)}, f32[30,32,128]{2,1,0:T(8,128)S(1)}, u32[]{:S(2)}, u32[]{:S(2)}) collective-permute-start(f32[30,32,128]{2,1,0:T(8,128)S(1)} %bitcast.50), channel_id=1, source_target_pairs={{4,8},{8,4},{12,16},{16,12},{20,24},{24,20},{5,9},{9,5},{13,17},{1... | collective-permute-start | bytes 1474568 | tf_op jit(solution)/shard_map/ppermute | solution.py:29
  182.3 10.0 %collective-permute-start.22 = (f32[48,16,128]{2,1,0:T(8,128)S(1)}, f32[48,16,128]{2,1,0:T(8,128)S(1)}, u32[]{:S(2)}, u32[]{:S(2)}) collective-permute-start(f32[48,16,128]{2,1,0:T(8,128)S(1)} %get-tuple-element.91), channel_id=1, source_target_pairs={{1,2},{2,1},{5,6},{6,5},{9,10},{10,9},{13,14},{14,13},{17,18},{18,... | collective-permute-start | bytes 1179656 | tf_op jit(solution)/shard_map/ppermute | solution.py:29
  183.0 9.3 %collective-permute-start.23 = (f32[48,16,128]{2,1,0:T(8,128)S(1)}, f32[48,16,128]{2,1,0:T(8,128)S(1)}, u32[]{:S(2)}, u32[]{:S(2)}) collective-permute-start(f32[48,16,128]{2,1,0:T(8,128)S(1)} %get-tuple-element.92), channel_id=1, source_target_pairs={{0,1},{1,0},{2,3},{3,2},{4,5},{5,4},{6,7},{7,6},{8,9},{9,8},{10,11... | collective-permute-start | bytes 1179656 | tf_op jit(solution)/shard_map/ppermute | solution.py:28

commit v4 on v3

--- a/solution.py
+++ b/solution.py
@@ -619,8 +619,8 @@
         turned=half,
         per=per,
         count=n_xy,
-        group=8,
-        unroll=depth // 8,
+        group=16,
+        unroll=depth // 16,
     )
     plan = Plan(
         name="bands", vmem=56 << 20, n_gz=n_gz, reach_y=reach_y, reach_x=reach_x, **common

time: 195 us -> 188 us (0.964)
  Pallas kernels: 75.8 us -> 65.3 us
  waiting for transfers between devices: 39.8 us -> 42 us
    pallas_call x3, Pallas kernels: 53.4 us -> 42.9 us  [update(): pl.pallas_call(functools.partial(update_kernel, plan), out_shape=shapes,...]
    all_to_all x1, waiting for transfers between devices: 1.18 us -> 4.7 us  [local(): lax.all_to_all(packed, 'xy', split_axis=0, concat_axis=0, tiled=True)]
  transfers between devices with their start and end apart: 25 -> 25, of which waited for: 9 -> 9; matrix products, arithmetic and copies ran while one was open for 4% -> 4% of each run, Pallas kernels for 22% -> 21%
where the time goes in v4:
time: 188 us; the launch traced here: 186 us
  Pallas kernels  65.3 us (35%)
  starting transfers between devices  55.8 us (30%)
  waiting for transfers between devices  42 us (22%)
  local copies, waits for them, and re-layouts  11.2 us (6%)
  other arithmetic  10.8 us (6%)
    pallas_call x3, Pallas kernels, update(): pl.pallas_call(functools.partial(update_kernel, plan), out_shape=shapes,...  42.9 us
    ppermute x12, starting transfers between devices, exchange(): b = lax.ppermute(jnp.where(even, low, high), axis, rounds[1])  37.9 us
    ppermute x12, waiting for transfers between devices, exchange(): b = lax.ppermute(jnp.where(even, low, high), axis, rounds[1])  34 us
    ppermute x12, starting transfers between devices, exchange(): a = lax.ppermute(jnp.where(even, high, low), axis, rounds[0])  11.4 us
    unnamed x42, local copies, waits for them, and re-layouts  10.1 us
    pallas_call x1, Pallas kernels, bands(): pl.pallas_call(functools.partial(bands_kernel, plan), out_shape=[jax.Shap...  7.04 us
    pallas_call x2, Pallas kernels, ahead(): pl.pallas_call(functools.partial(ahead_kernel, plan), out_shape=jax.Shape...  6.85 us
    all_to_all x1, starting transfers between devices, local(): lax.all_to_all(packed, 'xy', split_axis=0, concat_axis=0, tiled=True)  6.41 us
  transfers between devices with their start and end apart: 25, of which 9 were waited for; matrix products, arithmetic and copies ran while one was open for 4% of the time, Pallas kernels for 21%

profile of v4, /device:TPU:1, one launch (start us, length us, event | category | flops | bytes accessed | tf_op | source)
XLA Modules:
  0.0 185.8 jit_solution(10531278149725620239)
XLA Ops:
  0.0 1.2 slice_select_fusion.12
  1.2 2.2 %collective-permute-start.3 = (f32[48,16,128]{2,1,0:T(8,128)S(1)}, f32[48,16,128]{2,1,0:T(8,128)S(1)}, u32[]{:S(2)}, u32[]{:S(2)}) collective-permute-start(f32[48,16,128]{2,1,0:T(8,128)S(1)} %get-tuple-element.111), channel_id=1, source_target_pairs={{0,1},{1,0},{2,3},{3,2},{4,5},{5,4},{6,7},{7,6},{8,9},{9,8},{10,11... | collective-permute-start | bytes 1179656 | tf_op jit(solution)/shard_map/ppermute | solution.py:28
  3.4 0.7 collective-permute-start.2
  4.1 1.7 copy-done.1
  5.7 3.2 %pack.1 = f32[4,36,32,128]{3,2,1,0:T(8,128)} custom-call(f32[144,32,128]{2,1,0:T(8,128)S(1)} %bitcast.32), custom_call_target="tpu_custom_call" | custom-call | tf_op jit(solution)/shard_map/pack/pallas_call | solution.py:444
  8.9 3.3 %collective-permute-done.3 = f32[48,16,128]{2,1,0:T(8,128)S(1)} collective-permute-done((f32[48,16,128]{2,1,0:T(8,128)S(1)}, f32[48,16,128]{2,1,0:T(8,128)S(1)}, u32[]{:S(2)}, u32[]{:S(2)}) %collective-permute-start.3) | collective-permute-done | bytes 393248 | tf_op jit(solution)/shard_map/ppermute | solution.py:28
  12.2 0.8 broadcast_select_fusion.32
  13.0 6.4 %all-to-all-start = ((f32[4,36,32,128]{3,2,1,0:T(8,128)}), f32[4,36,32,128]{3,2,1,0:T(8,128)S(1)}, u32[]{:S(2)}, u32[]{:S(2)}) async-start(f32[4,36,32,128]{3,2,1,0:T(8,128)} %pack.1), calls=%async_computation | async-start | bytes 4718592 | tf_op jit(solution)/shard_map/all_to_all | solution.py:647
  19.5 1.1 slice_select_fusion.4
  20.6 2.1 %collective-permute-start.1 = (f32[30,32,128]{2,1,0:T(8,128)}, f32[30,32,128]{2,1,0:T(8,128)}, u32[]{:S(2)}, u32[]{:S(2)}) collective-permute-start(f32[30,32,128]{2,1,0:T(8,128)} %get-tuple-element.107), channel_id=1, source_target_pairs={{0,4},{4,0},{8,12},{12,8},{16,20},{20,16},{24,28},{28,24},{1,5},{5... | collective-permute-start | bytes 1474568 | tf_op jit(solution)/shard_map/ppermute | solution.py:28
  22.7 3.0 %collective-permute-start = (f32[30,32,128]{2,1,0:T(8,128)}, f32[30,32,128]{2,1,0:T(8,128)}, u32[]{:S(2)}, u32[]{:S(2)}) collective-permute-start(f32[30,32,128]{2,1,0:T(8,128)} %get-tuple-element.108), channel_id=1, source_target_pairs={{4,8},{8,4},{12,16},{16,12},{20,24},{24,20},{5,9},{9,5},{13,17},{1... | collective-permute-start | bytes 1474568 | tf_op jit(solution)/shard_map/ppermute | solution.py:29
  25.7 0.7 copy.9.views_of
  26.4 0.6 pad_add_fusion.2.place
  27.0 7.0 %bands.1 = (bf16[288,336]{1,0:T(8,128)(2,1)}, bf16[6,64,128]{2,1,0:T(8,128)(2,1)}, bf16[6,256,256]{2,1,0:T(8,128)(2,1)}, bf16[6,256,256]{2,1,0:T(8,128)(2,1)}, b...) custom-call(s32[2]{0:T(128)} %pad_add_fusion.2.place, ...), custom_call_target="tpu_custom_call" | custom-call | tf_op jit(solution)/shard_map/bands/pallas_call | solution.py:572
  34.1 1.1 constant_dynamic-update-slice_fusion
  35.2 0.1 slice_select_fusion.2
  35.4 3.5 %collective-permute-start.4 = (f32[30,32,128]{2,1,0:T(8,128)S(1)}, f32[30,32,128]{2,1,0:T(8,128)S(1)}, u32[]{:S(2)}, u32[]{:S(2)}) collective-permute-start(f32[30,32,128]{2,1,0:T(8,128)S(1)} %get-tuple-element.106), channel_id=1, source_target_pairs={{4,8},{8,4},{12,16},{16,12},{20,24},{24,20},{5,9},{9,5},{13,17},{1... | collective-permute-start | bytes 1474568 | tf_op jit(solution)/shard_map/ppermute | solution.py:29
  38.9 1.3 broadcast_select_fusion.24
  40.2 3.4 %ahead.2 = f32[9792,128]{1,0:T(8,128)S(1)} custom-call(f32[1536,128]{1,0:T(8,128)S(1)} %bitcast.31, f32[960,128]{1,0:T(8,128)S(1)} %bitcast.40, f32[960,128]{1,0:T(8,128)S(1)} %bitcast.39, bf16[288,336]{1,0:T(8,128)(2,1)S(1)} %copy-done.9), custom_call_target="tpu_custom_call" | custom-call | flops 3000000000 | bytes 8000000 | tf_op jit(solution)/shard_map/ahead/pallas_call | solution.py:271
  43.7 2.3 %copy-done.14 = f32[9792,128]{1,0:T(8,128)} copy-done((f32[9792,128]{1,0:T(8,128)}, f32[9792,128]{1,0:T(8,128)S(1)}, u32[]{:S(2)}) %copy-start.14) | copy-done | bytes 5013528
  45.9 4.2 %collective-permute-done.4 = f32[30,32,128]{2,1,0:T(8,128)S(1)} collective-permute-done((f32[30,32,128]{2,1,0:T(8,128)S(1)}, f32[30,32,128]{2,1,0:T(8,128)S(1)}, u32[]{:S(2)}, u32[]{:S(2)}) %collective-permute-start.4) | collective-permute-done | bytes 491552 | tf_op jit(solution)/shard_map/ppermute | solution.py:29
  50.1 1.1 broadcast_select_fusion.22
  51.2 16.9 %first.1 = (f32[1536,128]{1,0:T(8,128)}, f32[960,128]{1,0:T(8,128)}, f32[960,128]{1,0:T(8,128)}, f32[3,1600,128]{2,1,0:T(8,128)}, f32[3,1536,128]{2,1,0:T(8,128)}) custom-call(f32[6,1632,128]{2,1,0:T(8,128)} %bitcast.46, f32[1536,128]{1,0:T(8,128)} %bitcast.47, f32[960,128]{1,0:T(8,128)} %bitcast.58, f32[960,128]{1,0:T(8,128)} %bitcast.57, ...), custom_call_target="tpu_custom_call" | custom-call | flops 10000000000 | bytes 12000000 | tf_op jit(solution)/shard_map/first/pallas_call | solution.py:417
  68.1 4.7 %all-to-all-done.refs_0_.refs_9_ = f32[4,36,32,128]{3,2,1,0:T(8,128)S(1)} async-done(((f32[4,36,32,128]{3,2,1,0:T(8,128)}), f32[4,36,32,128]{3,2,1,0:T(8,128)S(1)}, u32[]{:S(2)}, u32[]{:S(2)}) %all-to-all-start) | async-done | bytes 2359328 | tf_op jit(solution)/shard_map/all_to_all | solution.py:647
  72.8 1.5 copy-done.2
  74.2 9.5 %second.1 = (f32[1536,128]{1,0:T(8,128)}, f32[960,128]{1,0:T(8,128)}, f32[960,128]{1,0:T(8,128)}, f32[3,1600,128]{2,1,0:T(8,128)}) custom-call(f32[4,36,32,128]{3,2,1,0:T(8,128)} %copy-done.2, bf16[3,112,432]{2,1,0:T(8,128)(2,1)} %get-tuple-element.45.refs_1_.wzt.refs_10_, f32[3,1536,128]{2,1,0:T(8,128)} %get-tuple-element.46.refs_2_, ...), custom_call_target="tpu_custom_call" | custom-call | flops 10000000000 | bytes 12000000 | tf_op jit(solution)/shard_map/second/pallas_call | solution.py:417
  83.8 1.2 broadcast_select_fusion.5
  85.0 1.5 collective-permute-start.9
  86.5 3.2 %collective-permute-start.8 = (f32[30,32,128]{2,1,0:T(8,128)S(1)}, f32[30,32,128]{2,1,0:T(8,128)S(1)}, u32[]{:S(2)}, u32[]{:S(2)}) collective-permute-start(f32[30,32,128]{2,1,0:T(8,128)S(1)} %bitcast.54), channel_id=1, source_target_pairs={{4,8},{8,4},{12,16},{16,12},{20,24},{24,20},{5,9},{9,5},{13,17},{1... | collective-permute-start | bytes 1474568 | tf_op jit(solution)/shard_map/ppermute | solution.py:29
  89.8 1.7 copy-done.16
  91.5 2.6 %behind.2 = (f32[1536,128]{1,0:T(8,128)S(1)}, f32[960,128]{1,0:T(8,128)S(1)}, f32[960,128]{1,0:T(8,128)S(1)}) custom-call(f32[3,1600,128]{2,1,0:T(8,128)S(1)} %copy-done.15, f32[3,1600,128]{2,1,0:T(8,128)S(1)} %copy-done.16, bf16[3,112,432]{2,1,0:T(8,128)(2,1)S(1)} %copy-done.7, bf16[3,112,432]{2,1,0:T(8,128)(2,1)S(1)} %copy-done.8), custom_call_target="tpu_custom_call" | custom-call | flops 3000000000 | bytes 8000000 | tf_op jit(solution)/shard_map/behind/pallas_call | solution.py:320
  94.3 3.5 %collective-permute-start.6 = (f32[30,32,128]{2,1,0:T(8,128)S(1)}, f32[30,32,128]{2,1,0:T(8,128)S(1)}, u32[]{:S(2)}, u32[]{:S(2)}) collective-permute-start(f32[30,32,128]{2,1,0:T(8,128)S(1)} %bitcast.49), channel_id=1, source_target_pairs={{4,8},{8,4},{12,16},{16,12},{20,24},{24,20},{5,9},{9,5},{13,17},{1... | collective-permute-start | bytes 1474568 | tf_op jit(solution)/shard_map/ppermute | solution.py:29
  97.8 4.1 %collective-permute-done.8 = f32[30,32,128]{2,1,0:T(8,128)S(1)} collective-permute-done((f32[30,32,128]{2,1,0:T(8,128)S(1)}, f32[30,32,128]{2,1,0:T(8,128)S(1)}, u32[]{:S(2)}, u32[]{:S(2)}) %collective-permute-start.8) | collective-permute-done | bytes 491552 | tf_op jit(solution)/shard_map/ppermute | solution.py:29
  101.9 0.1 broadcast_select_fusion.19
  102.1 0.2 pad_add_fusion.1
  102.3 0.7 collective-permute-start.10
  103.0 0.9 collective-permute-start.11
  103.9 8.5 %collective-permute-done.6 = f32[30,32,128]{2,1,0:T(8,128)S(1)} collective-permute-done((f32[30,32,128]{2,1,0:T(8,128)S(1)}, f32[30,32,128]{2,1,0:T(8,128)S(1)}, u32[]{:S(2)}, u32[]{:S(2)}) %collective-permute-start.6) | collective-permute-done | bytes 491552 | tf_op jit(solution)/shard_map/ppermute | solution.py:29
  112.7 0.3 add_multiply_fusion.1
  113.1 0.7 collective-permute-start.14
  113.8 0.9 collective-permute-start.15
  114.7 0.1 slice_select_fusion
  114.9 5.5 %collective-permute-start.12 = (f32[30,32,128]{2,1,0:T(8,128)S(1)}, f32[30,32,128]{2,1,0:T(8,128)S(1)}, u32[]{:S(2)}, u32[]{:S(2)}) collective-permute-start(f32[30,32,128]{2,1,0:T(8,128)S(1)} %get-tuple-element.100), channel_id=1, source_target_pairs={{4,8},{8,4},{12,16},{16,12},{20,24},{24,20},{5,9},{9,5},{13,17},{1... | collective-permute-start | bytes 1474568 | tf_op jit(solution)/shard_map/ppermute | solution.py:29
  120.5 0.1 broadcast_select_fusion.14
  120.7 8.9 %collective-permute-start.16 = (f32[30,32,128]{2,1,0:T(8,128)S(1)}, f32[30,32,128]{2,1,0:T(8,128)S(1)}, u32[]{:S(2)}, u32[]{:S(2)}) collective-permute-start(f32[30,32,128]{2,1,0:T(8,128)S(1)} %get-tuple-element.94), channel_id=1, source_target_pairs={{4,8},{8,4},{12,16},{16,12},{20,24},{24,20},{5,9},{9,5},{13,17},{1... | collective-permute-start | bytes 1474568 | tf_op jit(solution)/shard_map/ppermute | solution.py:29
  129.6 0.1 pad_maximum_fusion
  129.7 2.0 %collective-permute-done.12 = f32[30,32,128]{2,1,0:T(8,128)S(1)} collective-permute-done((f32[30,32,128]{2,1,0:T(8,128)S(1)}, f32[30,32,128]{2,1,0:T(8,128)S(1)}, u32[]{:S(2)}, u32[]{:S(2)}) %collective-permute-start.12) | collective-permute-done | bytes 491552 | tf_op jit(solution)/shard_map/ppermute | solution.py:29
  131.7 0.1 broadcast_select_fusion.16
  131.9 3.4 %ahead.3 = f32[9792,128]{1,0:T(8,128)S(1)} custom-call(f32[1536,128]{1,0:T(8,128)S(1)} %bitcast.30, f32[960,128]{1,0:T(8,128)S(1)} %bitcast.42, f32[960,128]{1,0:T(8,128)S(1)} %bitcast.41, bf16[288,336]{1,0:T(8,128)(2,1)S(1)} %copy-done.10), custom_call_target="tpu_custom_call" | custom-call | flops 3000000000 | bytes 8000000 | tf_op jit(solution)/shard_map/ahead/pallas_call | solution.py:271
  135.3 2.3 %copy-done.13 = f32[9792,128]{1,0:T(8,128)} copy-done((f32[9792,128]{1,0:T(8,128)}, f32[9792,128]{1,0:T(8,128)S(1)}, u32[]{:S(2)}) %copy-start.13) | copy-done | bytes 5013528
  137.6 4.6 %collective-permute-done.16 = f32[30,32,128]{2,1,0:T(8,128)S(1)} collective-permute-done((f32[30,32,128]{2,1,0:T(8,128)S(1)}, f32[30,32,128]{2,1,0:T(8,128)S(1)}, u32[]{:S(2)}, u32[]{:S(2)}) %collective-permute-start.16) | collective-permute-done | bytes 491552 | tf_op jit(solution)/shard_map/ppermute | solution.py:29
  142.2 0.1 broadcast_select_fusion.12
  142.4 16.5 %both.1 = (f32[1536,128]{1,0:T(8,128)S(1)}, f32[960,128]{1,0:T(8,128)S(1)}, f32[960,128]{1,0:T(8,128)S(1)}, f32[3,1600,128]{2,1,0:T(8,128)S(1)}, f32[3,1600,128]{2,1,0:T(8,128)S(1)}) custom-call(f32[6,1632,128]{2,1,0:T(8,128)} %bitcast.45, f32[1536,128]{1,0:T(8,128)S(1)} %bitcast.33, f32[960,128]{1,0:T(8,128)S(1)} %bitcast.38, f32[960,128]{1,0:T(8,128)S(1)} %bitcast.37, ...), custom_call_target="tpu_custom_call" | custom-call | flops 10000000000 | bytes 12000000 | tf_op jit(solution)/shard_map/both/pallas_call | solution.py:417
  159.1 4.0 %collective-permute-start.20 = (f32[30,32,128]{2,1,0:T(8,128)S(1)}, f32[30,32,128]{2,1,0:T(8,128)S(1)}, u32[]{:S(2)}, u32[]{:S(2)}) collective-permute-start(f32[30,32,128]{2,1,0:T(8,128)S(1)} %bitcast.53), channel_id=1, source_target_pairs={{4,8},{8,4},{12,16},{16,12},{20,24},{24,20},{5,9},{9,5},{13,17},{1... | collective-permute-start | bytes 1474568 | tf_op jit(solution)/shard_map/ppermute | solution.py:29
  163.1 2.7 %behind.3 = (f32[1536,128]{1,0:T(8,128)S(1)}, f32[960,128]{1,0:T(8,128)S(1)}, f32[960,128]{1,0:T(8,128)S(1)}) custom-call(f32[3,1600,128]{2,1,0:T(8,128)S(1)} %get-tuple-element.57.ru, f32[3,1600,128]{2,1,0:T(8,128)S(1)} %get-tuple-element.58.rt, bf16[3,112,432]{2,1,0:T(8,128)(2,1)S(1)} %copy-done.7, bf16[3,112,432]{2,1,0:T(8,128)(2,1)S(1)} %copy-done.8), custom_call_target="tpu_custom_call" | custom-call | flops 3000000000 | bytes 8000000 | tf_op jit(solution)/shard_map/behind/pallas_call | solution.py:320
  165.9 3.6 %collective-permute-start.18 = (f32[30,32,128]{2,1,0:T(8,128)S(1)}, f32[30,32,128]{2,1,0:T(8,128)S(1)}, u32[]{:S(2)}, u32[]{:S(2)}) collective-permute-start(f32[30,32,128]{2,1,0:T(8,128)S(1)} %bitcast.50), channel_id=1, source_target_pairs={{4,8},{8,4},{12,16},{16,12},{20,24},{24,20},{5,9},{9,5},{13,17},{1... | collective-permute-start | bytes 1474568 | tf_op jit(solution)/shard_map/ppermute | solution.py:29
  169.6 4.6 %collective-permute-done.20 = f32[30,32,128]{2,1,0:T(8,128)S(1)} collective-permute-done((f32[30,32,128]{2,1,0:T(8,128)S(1)}, f32[30,32,128]{2,1,0:T(8,128)S(1)}, u32[]{:S(2)}, u32[]{:S(2)}) %collective-permute-start.20) | collective-permute-done | bytes 491552 | tf_op jit(solution)/shard_map/ppermute | solution.py:29
  174.1 0.1 broadcast_select_fusion.9
  174.2 0.2 pad_add_fusion
  174.5 0.7 collective-permute-start.22
  175.2 3.3 %collective-permute-start.23 = (f32[48,16,128]{2,1,0:T(8,128)S(1)}, f32[48,16,128]{2,1,0:T(8,128)S(1)}, u32[]{:S(2)}, u32[]{:S(2)}) collective-permute-start(f32[48,16,128]{2,1,0:T(8,128)S(1)} %get-tuple-element.92), channel_id=1, source_target_pairs={{0,1},{1,0},{2,3},{3,2},{4,5},{5,4},{6,7},{7,6},{8,9},{9,8},{10,11... | collective-permute-start | bytes 1179656 | tf_op jit(solution)/shard_map/ppermute | solution.py:28
  178.4 5.9 %collective-permute-done.18 = f32[30,32,128]{2,1,0:T(8,128)S(1)} collective-permute-done((f32[30,32,128]{2,1,0:T(8,128)S(1)}, f32[30,32,128]{2,1,0:T(8,128)S(1)}, u32[]{:S(2)}, u32[]{:S(2)}) %collective-permute-start.18) | collective-permute-done | bytes 491552 | tf_op jit(solution)/shard_map/ppermute | solution.py:29
  184.4 0.1 broadcast_select_fusion.11
  184.5 1.2 add_multiply_fusion
  (68 shorter events, 1.2 us)
Async XLA Ops:
  1.2 11.0 %collective-permute-start.3 = (f32[48,16,128]{2,1,0:T(8,128)S(1)}, f32[48,16,128]{2,1,0:T(8,128)S(1)}, u32[]{:S(2)}, u32[]{:S(2)}) collective-permute-start(f32[48,16,128]{2,1,0:T(8,128)S(1)} %get-tuple-element.111), channel_id=1, source_target_pairs={{0,1},{1,0},{2,3},{3,2},{4,5},{5,4},{6,7},{7,6},{8,9},{9,8},{10,11... | collective-permute-start | bytes 1179656 | tf_op jit(solution)/shard_map/ppermute | solution.py:28
  3.4 8.8 %collective-permute-start.2 = (f32[48,16,128]{2,1,0:T(8,128)S(1)}, f32[48,16,128]{2,1,0:T(8,128)S(1)}, u32[]{:S(2)}, u32[]{:S(2)}) collective-permute-start(f32[48,16,128]{2,1,0:T(8,128)S(1)} %get-tuple-element.112), channel_id=1, source_target_pairs={{1,2},{2,1},{5,6},{6,5},{9,10},{10,9},{13,14},{14,13},{17,18},{18,... | collective-permute-start | bytes 1179656 | tf_op jit(solution)/shard_map/ppermute | solution.py:29
  4.1 1.7 copy-start.1
  13.0 6.4 %copy-start = (f32[48,32,128]{2,1,0:T(8,128)S(1)}, f32[48,32,128]{2,1,0:T(8,128)}, u32[]{:S(2)}) copy-start(f32[48,32,128]{2,1,0:T(8,128)} %param.8) | copy-start | bytes 2359300
  13.0 12.7 %copy-start.19 = (s32[32,3]{0,1:T(4,128)S(1)}, s32[32,3]{0,1:T(4,128)}, u32[]{:S(2)}) copy-start(s32[32,3]{0,1:T(4,128)} %param.15) | copy-start | bytes 1156
  13.0 59.7 %all-to-all-start = ((f32[4,36,32,128]{3,2,1,0:T(8,128)}), f32[4,36,32,128]{3,2,1,0:T(8,128)S(1)}, u32[]{:S(2)}, u32[]{:S(2)}) async-start(f32[4,36,32,128]{3,2,1,0:T(8,128)} %pack.1), calls=%async_computation | async-start | bytes 4718592 | tf_op jit(solution)/shard_map/all_to_all | solution.py:647
  20.6 18.4 %collective-permute-start.1 = (f32[30,32,128]{2,1,0:T(8,128)}, f32[30,32,128]{2,1,0:T(8,128)}, u32[]{:S(2)}, u32[]{:S(2)}) collective-permute-start(f32[30,32,128]{2,1,0:T(8,128)} %get-tuple-element.107), channel_id=1, source_target_pairs={{0,4},{4,0},{8,12},{12,8},{16,20},{20,16},{24,28},{28,24},{1,5},{5... | collective-permute-start | bytes 1474568 | tf_op jit(solution)/shard_map/ppermute | solution.py:28
  22.7 16.2 %collective-permute-start = (f32[30,32,128]{2,1,0:T(8,128)}, f32[30,32,128]{2,1,0:T(8,128)}, u32[]{:S(2)}, u32[]{:S(2)}) collective-permute-start(f32[30,32,128]{2,1,0:T(8,128)} %get-tuple-element.108), channel_id=1, source_target_pairs={{4,8},{8,4},{12,16},{16,12},{20,24},{24,20},{5,9},{9,5},{13,17},{1... | collective-permute-start | bytes 1474568 | tf_op jit(solution)/shard_map/ppermute | solution.py:29
  34.1 6.1 %copy-start.9 = (bf16[288,336]{1,0:T(8,128)(2,1)S(1)}, bf16[288,336]{1,0:T(8,128)(2,1)}, u32[]{:S(2)}) copy-start(bf16[288,336]{1,0:T(8,128)(2,1)} %get-tuple-element.35.wzf.refs_4_) | copy-start | bytes 580612
  35.2 8.5 %copy-start.17 = (f32[48,32,128]{2,1,0:T(8,128)}, f32[48,32,128]{2,1,0:T(8,128)S(1)}, u32[]{:S(2)}) copy-start(f32[48,32,128]{2,1,0:T(8,128)S(1)} %constant_dynamic-update-slice_fusion) | copy-start | bytes 2359300
  35.4 10.6 %collective-permute-start.5 = (f32[30,32,128]{2,1,0:T(8,128)S(1)}, f32[30,32,128]{2,1,0:T(8,128)S(1)}, u32[]{:S(2)}, u32[]{:S(2)}) collective-permute-start(f32[30,32,128]{2,1,0:T(8,128)S(1)} %get-tuple-element.105), channel_id=1, source_target_pairs={{0,4},{4,0},{8,12},{12,8},{16,20},{20,16},{24,28},{28,24},{1,5},{5... | collective-permute-start | bytes 1474568 | tf_op jit(solution)/shard_map/ppermute | solution.py:28
  35.4 14.7 %collective-permute-start.4 = (f32[30,32,128]{2,1,0:T(8,128)S(1)}, f32[30,32,128]{2,1,0:T(8,128)S(1)}, u32[]{:S(2)}, u32[]{:S(2)}) collective-permute-start(f32[30,32,128]{2,1,0:T(8,128)S(1)} %get-tuple-element.106), channel_id=1, source_target_pairs={{4,8},{8,4},{12,16},{16,12},{20,24},{24,20},{5,9},{9,5},{13,17},{1... | collective-permute-start | bytes 1474568 | tf_op jit(solution)/shard_map/ppermute | solution.py:29
  43.7 2.3 %copy-start.14 = (f32[9792,128]{1,0:T(8,128)}, f32[9792,128]{1,0:T(8,128)S(1)}, u32[]{:S(2)}) copy-start(f32[9792,128]{1,0:T(8,128)S(1)} %ahead.2) | copy-start | bytes 15040516
  72.8 1.5 copy-start.2
  74.2 15.5 %copy-start.7 = (bf16[3,112,432]{2,1,0:T(8,128)(2,1)S(1)}, bf16[3,112,432]{2,1,0:T(8,128)(2,1)}, u32[]{:S(2)}) copy-start(bf16[3,112,432]{2,1,0:T(8,128)(2,1)} %get-tuple-element.40.refs_8_.wzu) | copy-start | bytes 870916
  74.2 15.5 %copy-start.8 = (bf16[3,112,432]{2,1,0:T(8,128)(2,1)S(1)}, bf16[3,112,432]{2,1,0:T(8,128)(2,1)}, u32[]{:S(2)}) copy-start(bf16[3,112,432]{2,1,0:T(8,128)(2,1)} %get-tuple-element.45.refs_1_.wzt.refs_10_) | copy-start | bytes 870916
  74.2 15.5 %copy-start.15 = (f32[3,1600,128]{2,1,0:T(8,128)S(1)}, f32[3,1600,128]{2,1,0:T(8,128)}, u32[]{:S(2)}) copy-start(f32[3,1600,128]{2,1,0:T(8,128)} %get-tuple-element.43.ru) | copy-start | bytes 7372804
  85.0 12.8 %collective-permute-start.9 = (f32[30,32,128]{2,1,0:T(8,128)S(1)}, f32[30,32,128]{2,1,0:T(8,128)S(1)}, u32[]{:S(2)}, u32[]{:S(2)}) collective-permute-start(f32[30,32,128]{2,1,0:T(8,128)S(1)} %bitcast.56), channel_id=1, source_target_pairs={{0,4},{4,0},{8,12},{12,8},{16,20},{20,16},{24,28},{28,24},{1,5},{5... | collective-permute-start | bytes 1474568 | tf_op jit(solution)/shard_map/ppermute | solution.py:28
  86.5 15.4 %collective-permute-start.8 = (f32[30,32,128]{2,1,0:T(8,128)S(1)}, f32[30,32,128]{2,1,0:T(8,128)S(1)}, u32[]{:S(2)}, u32[]{:S(2)}) collective-permute-start(f32[30,32,128]{2,1,0:T(8,128)S(1)} %bitcast.54), channel_id=1, source_target_pairs={{4,8},{8,4},{12,16},{16,12},{20,24},{24,20},{5,9},{9,5},{13,17},{1... | collective-permute-start | bytes 1474568 | tf_op jit(solution)/shard_map/ppermute | solution.py:29
  89.8 1.7 copy-start.16
  94.1 7.9 %copy-start.18 = (f32[1536,128]{1,0:T(8,128)S(1)}, f32[1536,128]{1,0:T(8,128)}, u32[]{:S(2)}) copy-start(f32[1536,128]{1,0:T(8,128)} %get-tuple-element.54) | copy-start | bytes 2359300
  94.2 9.7 %collective-permute-start.7 = (f32[30,32,128]{2,1,0:T(8,128)S(1)}, f32[30,32,128]{2,1,0:T(8,128)S(1)}, u32[]{:S(2)}, u32[]{:S(2)}) collective-permute-start(f32[30,32,128]{2,1,0:T(8,128)S(1)} %bitcast.51), channel_id=1, source_target_pairs={{0,4},{4,0},{8,12},{12,8},{16,20},{20,16},{24,28},{28,24},{1,5},{5... | collective-permute-start | bytes 1474568 | tf_op jit(solution)/shard_map/ppermute | solution.py:28
  94.3 18.2 %collective-permute-start.6 = (f32[30,32,128]{2,1,0:T(8,128)S(1)}, f32[30,32,128]{2,1,0:T(8,128)S(1)}, u32[]{:S(2)}, u32[]{:S(2)}) collective-permute-start(f32[30,32,128]{2,1,0:T(8,128)S(1)} %bitcast.49), channel_id=1, source_target_pairs={{4,8},{8,4},{12,16},{16,12},{20,24},{24,20},{5,9},{9,5},{13,17},{1... | collective-permute-start | bytes 1474568 | tf_op jit(solution)/shard_map/ppermute | solution.py:29
  102.3 10.3 %collective-permute-start.10 = (f32[48,16,128]{2,1,0:T(8,128)S(1)}, f32[48,16,128]{2,1,0:T(8,128)S(1)}, u32[]{:S(2)}, u32[]{:S(2)}) collective-permute-start(f32[48,16,128]{2,1,0:T(8,128)S(1)} %get-tuple-element.103), channel_id=1, source_target_pairs={{1,2},{2,1},{5,6},{6,5},{9,10},{10,9},{13,14},{14,13},{17,18},{18,... | collective-permute-start | bytes 1179656 | tf_op jit(solution)/shard_map/ppermute | solution.py:29
  103.0 9.6 %collective-permute-start.11 = (f32[48,16,128]{2,1,0:T(8,128)S(1)}, f32[48,16,128]{2,1,0:T(8,128)S(1)}, u32[]{:S(2)}, u32[]{:S(2)}) collective-permute-start(f32[48,16,128]{2,1,0:T(8,128)S(1)} %get-tuple-element.104), channel_id=1, source_target_pairs={{0,1},{1,0},{2,3},{3,2},{4,5},{5,4},{6,7},{7,6},{8,9},{9,8},{10,11... | collective-permute-start | bytes 1179656 | tf_op jit(solution)/shard_map/ppermute | solution.py:28
  113.1 7.4 %collective-permute-start.14 = (f32[48,16,128]{2,1,0:T(8,128)S(1)}, f32[48,16,128]{2,1,0:T(8,128)S(1)}, u32[]{:S(2)}, u32[]{:S(2)}) collective-permute-start(f32[48,16,128]{2,1,0:T(8,128)S(1)} %get-tuple-element.97), channel_id=1, source_target_pairs={{1,2},{2,1},{5,6},{6,5},{9,10},{10,9},{13,14},{14,13},{17,18},{18,... | collective-permute-start | bytes 1179656 | tf_op jit(solution)/shard_map/ppermute | solution.py:29
  113.8 6.7 %collective-permute-start.15 = (f32[48,16,128]{2,1,0:T(8,128)S(1)}, f32[48,16,128]{2,1,0:T(8,128)S(1)}, u32[]{:S(2)}, u32[]{:S(2)}) collective-permute-start(f32[48,16,128]{2,1,0:T(8,128)S(1)} %get-tuple-element.98), channel_id=1, source_target_pairs={{0,1},{1,0},{2,3},{3,2},{4,5},{5,4},{6,7},{7,6},{8,9},{9,8},{10,11... | collective-permute-start | bytes 1179656 | tf_op jit(solution)/shard_map/ppermute | solution.py:28
  114.8 14.9 %collective-permute-start.13 = (f32[30,32,128]{2,1,0:T(8,128)S(1)}, f32[30,32,128]{2,1,0:T(8,128)S(1)}, u32[]{:S(2)}, u32[]{:S(2)}) collective-permute-start(f32[30,32,128]{2,1,0:T(8,128)S(1)} %get-tuple-element.99), channel_id=1, source_target_pairs={{0,4},{4,0},{8,12},{12,8},{16,20},{20,16},{24,28},{28,24},{1,5},{5... | collective-permute-start | bytes 1474568 | tf_op jit(solution)/shard_map/ppermute | solution.py:28
  114.9 16.8 %collective-permute-start.12 = (f32[30,32,128]{2,1,0:T(8,128)S(1)}, f32[30,32,128]{2,1,0:T(8,128)S(1)}, u32[]{:S(2)}, u32[]{:S(2)}) collective-permute-start(f32[30,32,128]{2,1,0:T(8,128)S(1)} %get-tuple-element.100), channel_id=1, source_target_pairs={{4,8},{8,4},{12,16},{16,12},{20,24},{24,20},{5,9},{9,5},{13,17},{1... | collective-permute-start | bytes 1474568 | tf_op jit(solution)/shard_map/ppermute | solution.py:29
  120.5 11.3 %copy-start.10 = (bf16[288,336]{1,0:T(8,128)(2,1)S(1)}, bf16[288,336]{1,0:T(8,128)(2,1)}, u32[]{:S(2)}) copy-start(bf16[288,336]{1,0:T(8,128)(2,1)} %get-tuple-element.35.wzf.refs_4_) | copy-start | bytes 580612
  120.6 16.9 %collective-permute-start.17 = (f32[30,32,128]{2,1,0:T(8,128)S(1)}, f32[30,32,128]{2,1,0:T(8,128)S(1)}, u32[]{:S(2)}, u32[]{:S(2)}) collective-permute-start(f32[30,32,128]{2,1,0:T(8,128)S(1)} %get-tuple-element.93), channel_id=1, source_target_pairs={{0,4},{4,0},{8,12},{12,8},{16,20},{20,16},{24,28},{28,24},{1,5},{5... | collective-permute-start | bytes 1474568 | tf_op jit(solution)/shard_map/ppermute | solution.py:28
  120.7 21.5 %collective-permute-start.16 = (f32[30,32,128]{2,1,0:T(8,128)S(1)}, f32[30,32,128]{2,1,0:T(8,128)S(1)}, u32[]{:S(2)}, u32[]{:S(2)}) collective-permute-start(f32[30,32,128]{2,1,0:T(8,128)S(1)} %get-tuple-element.94), channel_id=1, source_target_pairs={{4,8},{8,4},{12,16},{16,12},{20,24},{24,20},{5,9},{9,5},{13,17},{1... | collective-permute-start | bytes 1474568 | tf_op jit(solution)/shard_map/ppermute | solution.py:29
  131.8 10.5 %copy-start.3 = (f32[4,36,32,128]{3,2,1,0:T(8,128)S(1)}, f32[4,36,32,128]{3,2,1,0:T(8,128)}, u32[]{:S(2)}) copy-start(f32[4,36,32,128]{3,2,1,0:T(8,128)} %copy-done.2) | copy-start | bytes 7077892
  131.8 10.5 %copy-start.4 = (f32[3,48,32,128]{3,2,1,0:T(8,128)S(1)}, f32[3,48,32,128]{3,2,1,0:T(8,128)}, u32[]{:S(2)}) copy-start(f32[3,48,32,128]{3,2,1,0:T(8,128)} %param.9) | copy-start | bytes 7077892
  131.8 10.5 %copy-start.5 = (bf16[6,256,256]{2,1,0:T(8,128)(2,1)S(1)}, bf16[6,256,256]{2,1,0:T(8,128)(2,1)}, u32[]{:S(2)}) copy-start(bf16[6,256,256]{2,1,0:T(8,128)(2,1)} %get-tuple-element.39.refs_6_) | copy-start | bytes 2359300
  131.8 10.5 %copy-start.6 = (bf16[6,256,256]{2,1,0:T(8,128)(2,1)S(1)}, bf16[6,256,256]{2,1,0:T(8,128)(2,1)}, u32[]{:S(2)}) copy-start(bf16[6,256,256]{2,1,0:T(8,128)(2,1)} %get-tuple-element.41.refs_9_.refs_6_.refs_11_) | copy-start | bytes 2359300
  131.8 10.5 %copy-start.11 = (bf16[6,64,128]{2,1,0:T(8,128)(2,1)S(1)}, bf16[6,64,128]{2,1,0:T(8,128)(2,1)}, u32[]{:S(2)}) copy-start(bf16[6,64,128]{2,1,0:T(8,128)(2,1)} %get-tuple-element.38.refs_5_) | copy-start | bytes 294916
  131.9 10.5 %copy-start.12 = (bf16[6,64,96]{2,1,0:T(8,128)(2,1)S(1)}, bf16[6,64,96]{2,1,0:T(8,128)(2,1)}, u32[]{:S(2)}) copy-start(bf16[6,64,96]{2,1,0:T(8,128)(2,1)} %get-tuple-element.42.refs_10_.refs_7_.refs_12_) | copy-start | bytes 221188
  135.3 2.3 %copy-start.13 = (f32[9792,128]{1,0:T(8,128)}, f32[9792,128]{1,0:T(8,128)S(1)}, u32[]{:S(2)}) copy-start(f32[9792,128]{1,0:T(8,128)S(1)} %ahead.3) | copy-start | bytes 15040516
  159.0 10.6 %collective-permute-start.21 = (f32[30,32,128]{2,1,0:T(8,128)S(1)}, f32[30,32,128]{2,1,0:T(8,128)S(1)}, u32[]{:S(2)}, u32[]{:S(2)}) collective-permute-start(f32[30,32,128]{2,1,0:T(8,128)S(1)} %bitcast.55), channel_id=1, source_target_pairs={{0,4},{4,0},{8,12},{12,8},{16,20},{20,16},{24,28},{28,24},{1,5},{5... | collective-permute-start | bytes 1474568 | tf_op jit(solution)/shard_map/ppermute | solution.py:28
  159.1 15.0 %collective-permute-start.20 = (f32[30,32,128]{2,1,0:T(8,128)S(1)}, f32[30,32,128]{2,1,0:T(8,128)S(1)}, u32[]{:S(2)}, u32[]{:S(2)}) collective-permute-start(f32[30,32,128]{2,1,0:T(8,128)S(1)} %bitcast.53), channel_id=1, source_target_pairs={{4,8},{8,4},{12,16},{16,12},{20,24},{24,20},{5,9},{9,5},{13,17},{1... | collective-permute-start | bytes 1474568 | tf_op jit(solution)/shard_map/ppermute | solution.py:29
  165.8 12.6 %collective-permute-start.19 = (f32[30,32,128]{2,1,0:T(8,128)S(1)}, f32[30,32,128]{2,1,0:T(8,128)S(1)}, u32[]{:S(2)}, u32[]{:S(2)}) collective-permute-start(f32[30,32,128]{2,1,0:T(8,128)S(1)} %bitcast.52), channel_id=1, source_target_pairs={{0,4},{4,0},{8,12},{12,8},{16,20},{20,16},{24,28},{28,24},{1,5},{5... | collective-permute-start | bytes 1474568 | tf_op jit(solution)/shard_map/ppermute | solution.py:28
  165.9 18.4 %collective-permute-start.18 = (f32[30,32,128]{2,1,0:T(8,128)S(1)}, f32[30,32,128]{2,1,0:T(8,128)S(1)}, u32[]{:S(2)}, u32[]{:S(2)}) collective-permute-start(f32[30,32,128]{2,1,0:T(8,128)S(1)} %bitcast.50), channel_id=1, source_target_pairs={{4,8},{8,4},{12,16},{16,12},{20,24},{24,20},{5,9},{9,5},{13,17},{1... | collective-permute-start | bytes 1474568 | tf_op jit(solution)/shard_map/ppermute | solution.py:29
  174.5 10.0 %collective-permute-start.22 = (f32[48,16,128]{2,1,0:T(8,128)S(1)}, f32[48,16,128]{2,1,0:T(8,128)S(1)}, u32[]{:S(2)}, u32[]{:S(2)}) collective-permute-start(f32[48,16,128]{2,1,0:T(8,128)S(1)} %get-tuple-element.91), channel_id=1, source_target_pairs={{1,2},{2,1},{5,6},{6,5},{9,10},{10,9},{13,14},{14,13},{17,18},{18,... | collective-permute-start | bytes 1179656 | tf_op jit(solution)/shard_map/ppermute | solution.py:29
  175.2 9.3 %collective-permute-start.23 = (f32[48,16,128]{2,1,0:T(8,128)S(1)}, f32[48,16,128]{2,1,0:T(8,128)S(1)}, u32[]{:S(2)}, u32[]{:S(2)}) collective-permute-start(f32[48,16,128]{2,1,0:T(8,128)S(1)} %get-tuple-element.92), channel_id=1, source_target_pairs={{0,1},{1,0},{2,3},{3,2},{4,5},{5,4},{6,7},{7,6},{8,9},{9,8},{10,11... | collective-permute-start | bytes 1179656 | tf_op jit(solution)/shard_map/ppermute | solution.py:28

commit v5 on v4

--- a/solution.py
+++ b/solution.py
@@ -11,7 +11,7 @@
 F32 = jnp.float32
 BF16 = jnp.bfloat16
 VMEM_LIMIT = 36 * 1024 * 1024
-SPLIT = (56, 56, 36)
+SPLIT = (56, 56, 28)
 
 
 def round_up(value, unit):

time: 188 us -> 187 us (level)
  waiting for transfers between devices: 42 us -> 44.4 us
  local copies, waits for them, and re-layouts: 11.2 us -> 8.9 us
    ppermute x12, waiting for transfers between devices: 34 us -> 36.3 us  [exchange(): b = lax.ppermute(jnp.where(even, low, high), axis, rounds[1])]
    unnamed x42 -> x40, local copies, waits for them, and re-layouts: 10.1 us -> 7.82 us
where the time goes in v5:
time: 187 us; the launch traced here: 185 us
  Pallas kernels  64.3 us (34%)
  starting transfers between devices  55.7 us (30%)
  waiting for transfers between devices  44.4 us (24%)
  other arithmetic  10.8 us (6%)
  local copies, waits for them, and re-layouts  8.9 us (5%)
    pallas_call x3, Pallas kernels, update(): pl.pallas_call(functools.partial(update_kernel, plan), out_shape=shapes,...  41.9 us
    ppermute x12, starting transfers between devices, exchange(): b = lax.ppermute(jnp.where(even, low, high), axis, rounds[1])  37.9 us
    ppermute x12, waiting for transfers between devices, exchange(): b = lax.ppermute(jnp.where(even, low, high), axis, rounds[1])  36.3 us
    ppermute x12, starting transfers between devices, exchange(): a = lax.ppermute(jnp.where(even, high, low), axis, rounds[0])  11.4 us
    unnamed x40, local copies, waits for them, and re-layouts  7.82 us
    pallas_call x1, Pallas kernels, bands(): pl.pallas_call(functools.partial(bands_kernel, plan), out_shape=[jax.Shap...  7.04 us
    pallas_call x2, Pallas kernels, ahead(): pl.pallas_call(functools.partial(ahead_kernel, plan), out_shape=jax.Shape...  6.85 us
    all_to_all x1, starting transfers between devices, local(): lax.all_to_all(packed, 'xy', split_axis=0, concat_axis=0, tiled=True)  6.41 us
  transfers between devices with their start and end apart: 25, of which 9 were waited for; matrix products, arithmetic and copies ran while one was open for 4% of the time, Pallas kernels for 21%

profile of v5, /device:TPU:1, one launch (start us, length us, event | category | flops | bytes accessed | tf_op | source)
XLA Modules:
  0.0 184.8 jit_solution(7393226506732437880)
XLA Ops:
  0.0 1.2 slice_select_fusion.12
  1.2 2.2 %collective-permute-start.3 = (f32[48,16,128]{2,1,0:T(8,128)S(1)}, f32[48,16,128]{2,1,0:T(8,128)S(1)}, u32[]{:S(2)}, u32[]{:S(2)}) collective-permute-start(f32[48,16,128]{2,1,0:T(8,128)S(1)} %get-tuple-element.111), channel_id=1, source_target_pairs={{0,1},{1,0},{2,3},{3,2},{4,5},{5,4},{6,7},{7,6},{8,9},{9,8},{10,11... | collective-permute-start | bytes 1179656 | tf_op jit(solution)/shard_map/ppermute | solution.py:28
  3.4 0.7 collective-permute-start.2
  4.1 1.7 copy-done.1
  5.7 3.2 %pack.1 = f32[4,36,32,128]{3,2,1,0:T(8,128)} custom-call(f32[144,32,128]{2,1,0:T(8,128)S(1)} %bitcast.32), custom_call_target="tpu_custom_call" | custom-call | tf_op jit(solution)/shard_map/pack/pallas_call | solution.py:444
  8.9 3.3 %collective-permute-done.3 = f32[48,16,128]{2,1,0:T(8,128)S(1)} collective-permute-done((f32[48,16,128]{2,1,0:T(8,128)S(1)}, f32[48,16,128]{2,1,0:T(8,128)S(1)}, u32[]{:S(2)}, u32[]{:S(2)}) %collective-permute-start.3) | collective-permute-done | bytes 393248 | tf_op jit(solution)/shard_map/ppermute | solution.py:28
  12.2 0.8 broadcast_select_fusion.32
  13.0 6.4 %all-to-all-start = ((f32[4,36,32,128]{3,2,1,0:T(8,128)}), f32[4,36,32,128]{3,2,1,0:T(8,128)S(1)}, u32[]{:S(2)}, u32[]{:S(2)}) async-start(f32[4,36,32,128]{3,2,1,0:T(8,128)} %pack.1), calls=%async_computation | async-start | bytes 4718592 | tf_op jit(solution)/shard_map/all_to_all | solution.py:647
  19.5 1.1 slice_select_fusion.4
  20.6 2.1 %collective-permute-start.1 = (f32[30,32,128]{2,1,0:T(8,128)}, f32[30,32,128]{2,1,0:T(8,128)}, u32[]{:S(2)}, u32[]{:S(2)}) collective-permute-start(f32[30,32,128]{2,1,0:T(8,128)} %get-tuple-element.107), channel_id=1, source_target_pairs={{0,4},{4,0},{8,12},{12,8},{16,20},{20,16},{24,28},{28,24},{1,5},{5... | collective-permute-start | bytes 1474568 | tf_op jit(solution)/shard_map/ppermute | solution.py:28
  22.7 3.0 %collective-permute-start = (f32[30,32,128]{2,1,0:T(8,128)}, f32[30,32,128]{2,1,0:T(8,128)}, u32[]{:S(2)}, u32[]{:S(2)}) collective-permute-start(f32[30,32,128]{2,1,0:T(8,128)} %get-tuple-element.108), channel_id=1, source_target_pairs={{4,8},{8,4},{12,16},{16,12},{20,24},{24,20},{5,9},{9,5},{13,17},{1... | collective-permute-start | bytes 1474568 | tf_op jit(solution)/shard_map/ppermute | solution.py:29
  25.7 0.7 copy.9.views_of
  26.4 0.6 pad_add_fusion.2.place
  27.0 7.0 %bands.1 = (bf16[288,336]{1,0:T(8,128)(2,1)}, bf16[6,64,128]{2,1,0:T(8,128)(2,1)}, bf16[6,256,256]{2,1,0:T(8,128)(2,1)}, bf16[6,256,256]{2,1,0:T(8,128)(2,1)}, b...) custom-call(s32[2]{0:T(128)} %pad_add_fusion.2.place, ...), custom_call_target="tpu_custom_call" | custom-call | tf_op jit(solution)/shard_map/bands/pallas_call | solution.py:572
  34.1 1.1 constant_dynamic-update-slice_fusion
  35.2 0.1 slice_select_fusion.2
  35.4 3.5 %collective-permute-start.4 = (f32[30,32,128]{2,1,0:T(8,128)S(1)}, f32[30,32,128]{2,1,0:T(8,128)S(1)}, u32[]{:S(2)}, u32[]{:S(2)}) collective-permute-start(f32[30,32,128]{2,1,0:T(8,128)S(1)} %get-tuple-element.106), channel_id=1, source_target_pairs={{4,8},{8,4},{12,16},{16,12},{20,24},{24,20},{5,9},{9,5},{13,17},{1... | collective-permute-start | bytes 1474568 | tf_op jit(solution)/shard_map/ppermute | solution.py:29
  39.0 1.3 broadcast_select_fusion.24
  40.2 3.4 %ahead.2 = f32[9792,128]{1,0:T(8,128)S(1)} custom-call(f32[1536,128]{1,0:T(8,128)S(1)} %bitcast.31, f32[960,128]{1,0:T(8,128)S(1)} %bitcast.40, f32[960,128]{1,0:T(8,128)S(1)} %bitcast.39, bf16[288,336]{1,0:T(8,128)(2,1)S(1)} %copy-done.9), custom_call_target="tpu_custom_call" | custom-call | flops 3000000000 | bytes 8000000 | tf_op jit(solution)/shard_map/ahead/pallas_call | solution.py:271
  43.7 2.3 %copy-done.13 = f32[9792,128]{1,0:T(8,128)} copy-done((f32[9792,128]{1,0:T(8,128)}, f32[9792,128]{1,0:T(8,128)S(1)}, u32[]{:S(2)}) %copy-start.13) | copy-done | bytes 5013528
  46.0 4.2 %collective-permute-done.4 = f32[30,32,128]{2,1,0:T(8,128)S(1)} collective-permute-done((f32[30,32,128]{2,1,0:T(8,128)S(1)}, f32[30,32,128]{2,1,0:T(8,128)S(1)}, u32[]{:S(2)}, u32[]{:S(2)}) %collective-permute-start.4) | collective-permute-done | bytes 491552 | tf_op jit(solution)/shard_map/ppermute | solution.py:29
  50.1 1.0 broadcast_select_fusion.22
  51.2 16.9 %first.1 = (f32[1536,128]{1,0:T(8,128)}, f32[960,128]{1,0:T(8,128)}, f32[960,128]{1,0:T(8,128)}, f32[3,1600,128]{2,1,0:T(8,128)}, f32[3,1536,128]{2,1,0:T(8,128)}) custom-call(f32[6,1632,128]{2,1,0:T(8,128)} %bitcast.46, f32[1536,128]{1,0:T(8,128)} %bitcast.47, f32[960,128]{1,0:T(8,128)} %bitcast.58, f32[960,128]{1,0:T(8,128)} %bitcast.57, ...), custom_call_target="tpu_custom_call" | custom-call | flops 10000000000 | bytes 12000000 | tf_op jit(solution)/shard_map/first/pallas_call | solution.py:417
  68.1 4.7 %all-to-all-done.refs_0_.refs_9_ = f32[4,36,32,128]{3,2,1,0:T(8,128)S(1)} async-done(((f32[4,36,32,128]{3,2,1,0:T(8,128)}), f32[4,36,32,128]{3,2,1,0:T(8,128)S(1)}, u32[]{:S(2)}, u32[]{:S(2)}) %all-to-all-start) | async-done | bytes 2359328 | tf_op jit(solution)/shard_map/all_to_all | solution.py:647
  72.8 1.4 copy-done.2
  74.2 9.6 %second.1 = (f32[1536,128]{1,0:T(8,128)}, f32[960,128]{1,0:T(8,128)}, f32[960,128]{1,0:T(8,128)}, f32[3,1600,128]{2,1,0:T(8,128)}) custom-call(f32[4,36,32,128]{3,2,1,0:T(8,128)} %copy-done.2, bf16[3,112,432]{2,1,0:T(8,128)(2,1)} %get-tuple-element.45.refs_1_.wzt.refs_10_, f32[3,1536,128]{2,1,0:T(8,128)} %get-tuple-element.46.refs_2_, ...), custom_call_target="tpu_custom_call" | custom-call | flops 10000000000 | bytes 12000000 | tf_op jit(solution)/shard_map/second/pallas_call | solution.py:417
  83.8 1.2 broadcast_select_fusion.5
  85.0 1.5 collective-permute-start.9
  86.6 3.2 %collective-permute-start.8 = (f32[30,32,128]{2,1,0:T(8,128)S(1)}, f32[30,32,128]{2,1,0:T(8,128)S(1)}, u32[]{:S(2)}, u32[]{:S(2)}) collective-permute-start(f32[30,32,128]{2,1,0:T(8,128)S(1)} %bitcast.54), channel_id=1, source_target_pairs={{4,8},{8,4},{12,16},{16,12},{20,24},{24,20},{5,9},{9,5},{13,17},{1... | collective-permute-start | bytes 1474568 | tf_op jit(solution)/shard_map/ppermute | solution.py:29
  89.8 1.7 copy-done.15
  91.5 2.6 %behind.2 = (f32[1536,128]{1,0:T(8,128)S(1)}, f32[960,128]{1,0:T(8,128)S(1)}, f32[960,128]{1,0:T(8,128)S(1)}) custom-call(f32[3,1600,128]{2,1,0:T(8,128)S(1)} %copy-done.14, f32[3,1600,128]{2,1,0:T(8,128)S(1)} %copy-done.15, bf16[3,112,432]{2,1,0:T(8,128)(2,1)S(1)} %copy-done.7, bf16[3,112,432]{2,1,0:T(8,128)(2,1)S(1)} %copy-done.8), custom_call_target="tpu_custom_call" | custom-call | flops 3000000000 | bytes 8000000 | tf_op jit(solution)/shard_map/behind/pallas_call | solution.py:320
  94.3 3.5 %collective-permute-start.6 = (f32[30,32,128]{2,1,0:T(8,128)S(1)}, f32[30,32,128]{2,1,0:T(8,128)S(1)}, u32[]{:S(2)}, u32[]{:S(2)}) collective-permute-start(f32[30,32,128]{2,1,0:T(8,128)S(1)} %bitcast.49), channel_id=1, source_target_pairs={{4,8},{8,4},{12,16},{16,12},{20,24},{24,20},{5,9},{9,5},{13,17},{1... | collective-permute-start | bytes 1474568 | tf_op jit(solution)/shard_map/ppermute | solution.py:29
  97.8 4.1 %collective-permute-done.8 = f32[30,32,128]{2,1,0:T(8,128)S(1)} collective-permute-done((f32[30,32,128]{2,1,0:T(8,128)S(1)}, f32[30,32,128]{2,1,0:T(8,128)S(1)}, u32[]{:S(2)}, u32[]{:S(2)}) %collective-permute-start.8) | collective-permute-done | bytes 491552 | tf_op jit(solution)/shard_map/ppermute | solution.py:29
  102.0 0.1 broadcast_select_fusion.19
  102.1 0.2 pad_add_fusion.1
  102.3 0.7 collective-permute-start.10
  103.0 0.9 collective-permute-start.11
  104.0 8.5 %collective-permute-done.6 = f32[30,32,128]{2,1,0:T(8,128)S(1)} collective-permute-done((f32[30,32,128]{2,1,0:T(8,128)S(1)}, f32[30,32,128]{2,1,0:T(8,128)S(1)}, u32[]{:S(2)}, u32[]{:S(2)}) %collective-permute-start.6) | collective-permute-done | bytes 491552 | tf_op jit(solution)/shard_map/ppermute | solution.py:29
  112.5 0.1 broadcast_select_fusion.21
  112.7 0.3 add_multiply_fusion.1
  113.1 0.7 collective-permute-start.14
  113.8 0.9 collective-permute-start.15
  114.7 0.1 slice_select_fusion
  114.9 5.5 %collective-permute-start.12 = (f32[30,32,128]{2,1,0:T(8,128)S(1)}, f32[30,32,128]{2,1,0:T(8,128)S(1)}, u32[]{:S(2)}, u32[]{:S(2)}) collective-permute-start(f32[30,32,128]{2,1,0:T(8,128)S(1)} %get-tuple-element.100), channel_id=1, source_target_pairs={{4,8},{8,4},{12,16},{16,12},{20,24},{24,20},{5,9},{9,5},{13,17},{1... | collective-permute-start | bytes 1474568 | tf_op jit(solution)/shard_map/ppermute | solution.py:29
  120.5 0.1 broadcast_select_fusion.14
  120.7 8.8 %collective-permute-start.16 = (f32[30,32,128]{2,1,0:T(8,128)S(1)}, f32[30,32,128]{2,1,0:T(8,128)S(1)}, u32[]{:S(2)}, u32[]{:S(2)}) collective-permute-start(f32[30,32,128]{2,1,0:T(8,128)S(1)} %get-tuple-element.94), channel_id=1, source_target_pairs={{4,8},{8,4},{12,16},{16,12},{20,24},{24,20},{5,9},{9,5},{13,17},{1... | collective-permute-start | bytes 1474568 | tf_op jit(solution)/shard_map/ppermute | solution.py:29
  129.6 0.1 pad_maximum_fusion
  129.7 2.0 %collective-permute-done.12 = f32[30,32,128]{2,1,0:T(8,128)S(1)} collective-permute-done((f32[30,32,128]{2,1,0:T(8,128)S(1)}, f32[30,32,128]{2,1,0:T(8,128)S(1)}, u32[]{:S(2)}, u32[]{:S(2)}) %collective-permute-start.12) | collective-permute-done | bytes 491552 | tf_op jit(solution)/shard_map/ppermute | solution.py:29
  131.7 0.1 broadcast_select_fusion.16
  131.9 3.4 %ahead.3 = f32[9792,128]{1,0:T(8,128)S(1)} custom-call(f32[1536,128]{1,0:T(8,128)S(1)} %bitcast.30, f32[960,128]{1,0:T(8,128)S(1)} %bitcast.42, f32[960,128]{1,0:T(8,128)S(1)} %bitcast.41, bf16[288,336]{1,0:T(8,128)(2,1)S(1)} %copy-done.10), custom_call_target="tpu_custom_call" | custom-call | flops 3000000000 | bytes 8000000 | tf_op jit(solution)/shard_map/ahead/pallas_call | solution.py:271
  135.3 6.9 %collective-permute-done.16 = f32[30,32,128]{2,1,0:T(8,128)S(1)} collective-permute-done((f32[30,32,128]{2,1,0:T(8,128)S(1)}, f32[30,32,128]{2,1,0:T(8,128)S(1)}, u32[]{:S(2)}, u32[]{:S(2)}) %collective-permute-start.16) | collective-permute-done | bytes 491552 | tf_op jit(solution)/shard_map/ppermute | solution.py:29
  142.2 0.1 broadcast_select_fusion.12
  142.4 15.5 %both.1 = (f32[1536,128]{1,0:T(8,128)S(1)}, f32[960,128]{1,0:T(8,128)S(1)}, f32[960,128]{1,0:T(8,128)S(1)}, f32[3,1600,128]{2,1,0:T(8,128)S(1)}, f32[3,1600,128]{2,1,0:T(8,128)S(1)}) custom-call(f32[6,1632,128]{2,1,0:T(8,128)S(1)} %bitcast.45, f32[1536,128]{1,0:T(8,128)S(1)} %bitcast.33, f32[960,128]{1,0:T(8,128)S(1)} %bitcast.38, f32[960,128]{1,0:T(8,128)S(1)} %bitcast.37, ...), custom_call_target="tpu_custom_call" | custom-call | flops 10000000000 | bytes 12000000 | tf_op jit(solution)/shard_map/both/pallas_call | solution.py:417
  158.0 4.0 %collective-permute-start.20 = (f32[30,32,128]{2,1,0:T(8,128)S(1)}, f32[30,32,128]{2,1,0:T(8,128)S(1)}, u32[]{:S(2)}, u32[]{:S(2)}) collective-permute-start(f32[30,32,128]{2,1,0:T(8,128)S(1)} %bitcast.53), channel_id=1, source_target_pairs={{4,8},{8,4},{12,16},{16,12},{20,24},{24,20},{5,9},{9,5},{13,17},{1... | collective-permute-start | bytes 1474568 | tf_op jit(solution)/shard_map/ppermute | solution.py:29
  162.1 2.7 %behind.3 = (f32[1536,128]{1,0:T(8,128)S(1)}, f32[960,128]{1,0:T(8,128)S(1)}, f32[960,128]{1,0:T(8,128)S(1)}) custom-call(f32[3,1600,128]{2,1,0:T(8,128)S(1)} %get-tuple-element.57.ru, f32[3,1600,128]{2,1,0:T(8,128)S(1)} %get-tuple-element.58.rt, bf16[3,112,432]{2,1,0:T(8,128)(2,1)S(1)} %copy-done.7, bf16[3,112,432]{2,1,0:T(8,128)(2,1)S(1)} %copy-done.8), custom_call_target="tpu_custom_call" | custom-call | flops 3000000000 | bytes 8000000 | tf_op jit(solution)/shard_map/behind/pallas_call | solution.py:320
  164.9 3.6 %collective-permute-start.18 = (f32[30,32,128]{2,1,0:T(8,128)S(1)}, f32[30,32,128]{2,1,0:T(8,128)S(1)}, u32[]{:S(2)}, u32[]{:S(2)}) collective-permute-start(f32[30,32,128]{2,1,0:T(8,128)S(1)} %bitcast.50), channel_id=1, source_target_pairs={{4,8},{8,4},{12,16},{16,12},{20,24},{24,20},{5,9},{9,5},{13,17},{1... | collective-permute-start | bytes 1474568 | tf_op jit(solution)/shard_map/ppermute | solution.py:29
  168.5 4.6 %collective-permute-done.20 = f32[30,32,128]{2,1,0:T(8,128)S(1)} collective-permute-done((f32[30,32,128]{2,1,0:T(8,128)S(1)}, f32[30,32,128]{2,1,0:T(8,128)S(1)}, u32[]{:S(2)}, u32[]{:S(2)}) %collective-permute-start.20) | collective-permute-done | bytes 491552 | tf_op jit(solution)/shard_map/ppermute | solution.py:29
  173.1 0.1 broadcast_select_fusion.9
  173.2 0.2 pad_add_fusion
  173.4 0.7 collective-permute-start.22
  174.1 3.2 %collective-permute-start.23 = (f32[48,16,128]{2,1,0:T(8,128)S(1)}, f32[48,16,128]{2,1,0:T(8,128)S(1)}, u32[]{:S(2)}, u32[]{:S(2)}) collective-permute-start(f32[48,16,128]{2,1,0:T(8,128)S(1)} %get-tuple-element.92), channel_id=1, source_target_pairs={{0,1},{1,0},{2,3},{3,2},{4,5},{5,4},{6,7},{7,6},{8,9},{9,8},{10,11... | collective-permute-start | bytes 1179656 | tf_op jit(solution)/shard_map/ppermute | solution.py:28
  177.3 6.0 %collective-permute-done.18 = f32[30,32,128]{2,1,0:T(8,128)S(1)} collective-permute-done((f32[30,32,128]{2,1,0:T(8,128)S(1)}, f32[30,32,128]{2,1,0:T(8,128)S(1)}, u32[]{:S(2)}, u32[]{:S(2)}) %collective-permute-start.18) | collective-permute-done | bytes 491552 | tf_op jit(solution)/shard_map/ppermute | solution.py:29
  183.3 0.1 broadcast_select_fusion.11
  183.5 1.2 add_multiply_fusion
  (66 shorter events, 1.1 us)
Async XLA Ops:
  1.2 11.0 %collective-permute-start.3 = (f32[48,16,128]{2,1,0:T(8,128)S(1)}, f32[48,16,128]{2,1,0:T(8,128)S(1)}, u32[]{:S(2)}, u32[]{:S(2)}) collective-permute-start(f32[48,16,128]{2,1,0:T(8,128)S(1)} %get-tuple-element.111), channel_id=1, source_target_pairs={{0,1},{1,0},{2,3},{3,2},{4,5},{5,4},{6,7},{7,6},{8,9},{9,8},{10,11... | collective-permute-start | bytes 1179656 | tf_op jit(solution)/shard_map/ppermute | solution.py:28
  3.4 8.8 %collective-permute-start.2 = (f32[48,16,128]{2,1,0:T(8,128)S(1)}, f32[48,16,128]{2,1,0:T(8,128)S(1)}, u32[]{:S(2)}, u32[]{:S(2)}) collective-permute-start(f32[48,16,128]{2,1,0:T(8,128)S(1)} %get-tuple-element.112), channel_id=1, source_target_pairs={{1,2},{2,1},{5,6},{6,5},{9,10},{10,9},{13,14},{14,13},{17,18},{18,... | collective-permute-start | bytes 1179656 | tf_op jit(solution)/shard_map/ppermute | solution.py:29
  4.1 1.7 copy-start.1
  13.0 6.4 %copy-start = (f32[48,32,128]{2,1,0:T(8,128)S(1)}, f32[48,32,128]{2,1,0:T(8,128)}, u32[]{:S(2)}) copy-start(f32[48,32,128]{2,1,0:T(8,128)} %param.8) | copy-start | bytes 2359300
  13.0 12.7 %copy-start.18 = (s32[32,3]{0,1:T(4,128)S(1)}, s32[32,3]{0,1:T(4,128)}, u32[]{:S(2)}) copy-start(s32[32,3]{0,1:T(4,128)} %param.15) | copy-start | bytes 1156
  13.0 59.7 %all-to-all-start = ((f32[4,36,32,128]{3,2,1,0:T(8,128)}), f32[4,36,32,128]{3,2,1,0:T(8,128)S(1)}, u32[]{:S(2)}, u32[]{:S(2)}) async-start(f32[4,36,32,128]{3,2,1,0:T(8,128)} %pack.1), calls=%async_computation | async-start | bytes 4718592 | tf_op jit(solution)/shard_map/all_to_all | solution.py:647
  20.6 18.4 %collective-permute-start.1 = (f32[30,32,128]{2,1,0:T(8,128)}, f32[30,32,128]{2,1,0:T(8,128)}, u32[]{:S(2)}, u32[]{:S(2)}) collective-permute-start(f32[30,32,128]{2,1,0:T(8,128)} %get-tuple-element.107), channel_id=1, source_target_pairs={{0,4},{4,0},{8,12},{12,8},{16,20},{20,16},{24,28},{28,24},{1,5},{5... | collective-permute-start | bytes 1474568 | tf_op jit(solution)/shard_map/ppermute | solution.py:28
  22.7 16.2 %collective-permute-start = (f32[30,32,128]{2,1,0:T(8,128)}, f32[30,32,128]{2,1,0:T(8,128)}, u32[]{:S(2)}, u32[]{:S(2)}) collective-permute-start(f32[30,32,128]{2,1,0:T(8,128)} %get-tuple-element.108), channel_id=1, source_target_pairs={{4,8},{8,4},{12,16},{16,12},{20,24},{24,20},{5,9},{9,5},{13,17},{1... | collective-permute-start | bytes 1474568 | tf_op jit(solution)/shard_map/ppermute | solution.py:29
  34.1 6.1 %copy-start.9 = (bf16[288,336]{1,0:T(8,128)(2,1)S(1)}, bf16[288,336]{1,0:T(8,128)(2,1)}, u32[]{:S(2)}) copy-start(bf16[288,336]{1,0:T(8,128)(2,1)} %get-tuple-element.35.wzf.refs_4_) | copy-start | bytes 580612
  35.2 8.5 %copy-start.16 = (f32[48,32,128]{2,1,0:T(8,128)}, f32[48,32,128]{2,1,0:T(8,128)S(1)}, u32[]{:S(2)}) copy-start(f32[48,32,128]{2,1,0:T(8,128)S(1)} %constant_dynamic-update-slice_fusion) | copy-start | bytes 2359300
  35.4 10.6 %collective-permute-start.5 = (f32[30,32,128]{2,1,0:T(8,128)S(1)}, f32[30,32,128]{2,1,0:T(8,128)S(1)}, u32[]{:S(2)}, u32[]{:S(2)}) collective-permute-start(f32[30,32,128]{2,1,0:T(8,128)S(1)} %get-tuple-element.105), channel_id=1, source_target_pairs={{0,4},{4,0},{8,12},{12,8},{16,20},{20,16},{24,28},{28,24},{1,5},{5... | collective-permute-start | bytes 1474568 | tf_op jit(solution)/shard_map/ppermute | solution.py:28
  35.4 14.7 %collective-permute-start.4 = (f32[30,32,128]{2,1,0:T(8,128)S(1)}, f32[30,32,128]{2,1,0:T(8,128)S(1)}, u32[]{:S(2)}, u32[]{:S(2)}) collective-permute-start(f32[30,32,128]{2,1,0:T(8,128)S(1)} %get-tuple-element.106), channel_id=1, source_target_pairs={{4,8},{8,4},{12,16},{16,12},{20,24},{24,20},{5,9},{9,5},{13,17},{1... | collective-permute-start | bytes 1474568 | tf_op jit(solution)/shard_map/ppermute | solution.py:29
  43.7 2.3 %copy-start.13 = (f32[9792,128]{1,0:T(8,128)}, f32[9792,128]{1,0:T(8,128)S(1)}, u32[]{:S(2)}) copy-start(f32[9792,128]{1,0:T(8,128)S(1)} %ahead.2) | copy-start | bytes 15040516
  72.8 1.4 copy-start.2
  74.2 15.6 %copy-start.7 = (bf16[3,112,432]{2,1,0:T(8,128)(2,1)S(1)}, bf16[3,112,432]{2,1,0:T(8,128)(2,1)}, u32[]{:S(2)}) copy-start(bf16[3,112,432]{2,1,0:T(8,128)(2,1)} %get-tuple-element.40.refs_8_.wzu) | copy-start | bytes 870916
  74.2 15.6 %copy-start.8 = (bf16[3,112,432]{2,1,0:T(8,128)(2,1)S(1)}, bf16[3,112,432]{2,1,0:T(8,128)(2,1)}, u32[]{:S(2)}) copy-start(bf16[3,112,432]{2,1,0:T(8,128)(2,1)} %get-tuple-element.45.refs_1_.wzt.refs_10_) | copy-start | bytes 870916
  74.2 15.6 %copy-start.14 = (f32[3,1600,128]{2,1,0:T(8,128)S(1)}, f32[3,1600,128]{2,1,0:T(8,128)}, u32[]{:S(2)}) copy-start(f32[3,1600,128]{2,1,0:T(8,128)} %get-tuple-element.43.ru) | copy-start | bytes 7372804
  85.0 12.8 %collective-permute-start.9 = (f32[30,32,128]{2,1,0:T(8,128)S(1)}, f32[30,32,128]{2,1,0:T(8,128)S(1)}, u32[]{:S(2)}, u32[]{:S(2)}) collective-permute-start(f32[30,32,128]{2,1,0:T(8,128)S(1)} %bitcast.56), channel_id=1, source_target_pairs={{0,4},{4,0},{8,12},{12,8},{16,20},{20,16},{24,28},{28,24},{1,5},{5... | collective-permute-start | bytes 1474568 | tf_op jit(solution)/shard_map/ppermute | solution.py:28
  86.6 15.4 %collective-permute-start.8 = (f32[30,32,128]{2,1,0:T(8,128)S(1)}, f32[30,32,128]{2,1,0:T(8,128)S(1)}, u32[]{:S(2)}, u32[]{:S(2)}) collective-permute-start(f32[30,32,128]{2,1,0:T(8,128)S(1)} %bitcast.54), channel_id=1, source_target_pairs={{4,8},{8,4},{12,16},{16,12},{20,24},{24,20},{5,9},{9,5},{13,17},{1... | collective-permute-start | bytes 1474568 | tf_op jit(solution)/shard_map/ppermute | solution.py:29
  89.8 1.7 copy-start.15
  94.1 7.9 %copy-start.17 = (f32[1536,128]{1,0:T(8,128)S(1)}, f32[1536,128]{1,0:T(8,128)}, u32[]{:S(2)}) copy-start(f32[1536,128]{1,0:T(8,128)} %get-tuple-element.54) | copy-start | bytes 2359300
  94.2 9.7 %collective-permute-start.7 = (f32[30,32,128]{2,1,0:T(8,128)S(1)}, f32[30,32,128]{2,1,0:T(8,128)S(1)}, u32[]{:S(2)}, u32[]{:S(2)}) collective-permute-start(f32[30,32,128]{2,1,0:T(8,128)S(1)} %bitcast.51), channel_id=1, source_target_pairs={{0,4},{4,0},{8,12},{12,8},{16,20},{20,16},{24,28},{28,24},{1,5},{5... | collective-permute-start | bytes 1474568 | tf_op jit(solution)/shard_map/ppermute | solution.py:28
  94.3 18.2 %collective-permute-start.6 = (f32[30,32,128]{2,1,0:T(8,128)S(1)}, f32[30,32,128]{2,1,0:T(8,128)S(1)}, u32[]{:S(2)}, u32[]{:S(2)}) collective-permute-start(f32[30,32,128]{2,1,0:T(8,128)S(1)} %bitcast.49), channel_id=1, source_target_pairs={{4,8},{8,4},{12,16},{16,12},{20,24},{24,20},{5,9},{9,5},{13,17},{1... | collective-permute-start | bytes 1474568 | tf_op jit(solution)/shard_map/ppermute | solution.py:29
  102.3 10.3 %collective-permute-start.10 = (f32[48,16,128]{2,1,0:T(8,128)S(1)}, f32[48,16,128]{2,1,0:T(8,128)S(1)}, u32[]{:S(2)}, u32[]{:S(2)}) collective-permute-start(f32[48,16,128]{2,1,0:T(8,128)S(1)} %get-tuple-element.103), channel_id=1, source_target_pairs={{1,2},{2,1},{5,6},{6,5},{9,10},{10,9},{13,14},{14,13},{17,18},{18,... | collective-permute-start | bytes 1179656 | tf_op jit(solution)/shard_map/ppermute | solution.py:29
  103.0 9.6 %collective-permute-start.11 = (f32[48,16,128]{2,1,0:T(8,128)S(1)}, f32[48,16,128]{2,1,0:T(8,128)S(1)}, u32[]{:S(2)}, u32[]{:S(2)}) collective-permute-start(f32[48,16,128]{2,1,0:T(8,128)S(1)} %get-tuple-element.104), channel_id=1, source_target_pairs={{0,1},{1,0},{2,3},{3,2},{4,5},{5,4},{6,7},{7,6},{8,9},{9,8},{10,11... | collective-permute-start | bytes 1179656 | tf_op jit(solution)/shard_map/ppermute | solution.py:28
  113.1 7.4 %collective-permute-start.14 = (f32[48,16,128]{2,1,0:T(8,128)S(1)}, f32[48,16,128]{2,1,0:T(8,128)S(1)}, u32[]{:S(2)}, u32[]{:S(2)}) collective-permute-start(f32[48,16,128]{2,1,0:T(8,128)S(1)} %get-tuple-element.97), channel_id=1, source_target_pairs={{1,2},{2,1},{5,6},{6,5},{9,10},{10,9},{13,14},{14,13},{17,18},{18,... | collective-permute-start | bytes 1179656 | tf_op jit(solution)/shard_map/ppermute | solution.py:29
  113.8 6.7 %collective-permute-start.15 = (f32[48,16,128]{2,1,0:T(8,128)S(1)}, f32[48,16,128]{2,1,0:T(8,128)S(1)}, u32[]{:S(2)}, u32[]{:S(2)}) collective-permute-start(f32[48,16,128]{2,1,0:T(8,128)S(1)} %get-tuple-element.98), channel_id=1, source_target_pairs={{0,1},{1,0},{2,3},{3,2},{4,5},{5,4},{6,7},{7,6},{8,9},{9,8},{10,11... | collective-permute-start | bytes 1179656 | tf_op jit(solution)/shard_map/ppermute | solution.py:28
  114.8 14.9 %collective-permute-start.13 = (f32[30,32,128]{2,1,0:T(8,128)S(1)}, f32[30,32,128]{2,1,0:T(8,128)S(1)}, u32[]{:S(2)}, u32[]{:S(2)}) collective-permute-start(f32[30,32,128]{2,1,0:T(8,128)S(1)} %get-tuple-element.99), channel_id=1, source_target_pairs={{0,4},{4,0},{8,12},{12,8},{16,20},{20,16},{24,28},{28,24},{1,5},{5... | collective-permute-start | bytes 1474568 | tf_op jit(solution)/shard_map/ppermute | solution.py:28
  114.9 16.8 %collective-permute-start.12 = (f32[30,32,128]{2,1,0:T(8,128)S(1)}, f32[30,32,128]{2,1,0:T(8,128)S(1)}, u32[]{:S(2)}, u32[]{:S(2)}) collective-permute-start(f32[30,32,128]{2,1,0:T(8,128)S(1)} %get-tuple-element.100), channel_id=1, source_target_pairs={{4,8},{8,4},{12,16},{16,12},{20,24},{24,20},{5,9},{9,5},{13,17},{1... | collective-permute-start | bytes 1474568 | tf_op jit(solution)/shard_map/ppermute | solution.py:29
  120.5 11.3 %copy-start.10 = (bf16[288,336]{1,0:T(8,128)(2,1)S(1)}, bf16[288,336]{1,0:T(8,128)(2,1)}, u32[]{:S(2)}) copy-start(bf16[288,336]{1,0:T(8,128)(2,1)} %get-tuple-element.35.wzf.refs_4_) | copy-start | bytes 580612
  120.7 14.6 %collective-permute-start.17 = (f32[30,32,128]{2,1,0:T(8,128)S(1)}, f32[30,32,128]{2,1,0:T(8,128)S(1)}, u32[]{:S(2)}, u32[]{:S(2)}) collective-permute-start(f32[30,32,128]{2,1,0:T(8,128)S(1)} %get-tuple-element.93), channel_id=1, source_target_pairs={{0,4},{4,0},{8,12},{12,8},{16,20},{20,16},{24,28},{28,24},{1,5},{5... | collective-permute-start | bytes 1474568 | tf_op jit(solution)/shard_map/ppermute | solution.py:28
  120.7 21.5 %collective-permute-start.16 = (f32[30,32,128]{2,1,0:T(8,128)S(1)}, f32[30,32,128]{2,1,0:T(8,128)S(1)}, u32[]{:S(2)}, u32[]{:S(2)}) collective-permute-start(f32[30,32,128]{2,1,0:T(8,128)S(1)} %get-tuple-element.94), channel_id=1, source_target_pairs={{4,8},{8,4},{12,16},{16,12},{20,24},{24,20},{5,9},{9,5},{13,17},{1... | collective-permute-start | bytes 1474568 | tf_op jit(solution)/shard_map/ppermute | solution.py:29
  131.8 10.5 %copy-start.3 = (f32[4,36,32,128]{3,2,1,0:T(8,128)S(1)}, f32[4,36,32,128]{3,2,1,0:T(8,128)}, u32[]{:S(2)}) copy-start(f32[4,36,32,128]{3,2,1,0:T(8,128)} %copy-done.2) | copy-start | bytes 7077892
  131.8 10.5 %copy-start.4 = (f32[3,48,32,128]{3,2,1,0:T(8,128)S(1)}, f32[3,48,32,128]{3,2,1,0:T(8,128)}, u32[]{:S(2)}) copy-start(f32[3,48,32,128]{3,2,1,0:T(8,128)} %param.9) | copy-start | bytes 7077892
  131.8 10.5 %copy-start.5 = (bf16[6,256,256]{2,1,0:T(8,128)(2,1)S(1)}, bf16[6,256,256]{2,1,0:T(8,128)(2,1)}, u32[]{:S(2)}) copy-start(bf16[6,256,256]{2,1,0:T(8,128)(2,1)} %get-tuple-element.39.refs_6_) | copy-start | bytes 2359300
  131.8 10.5 %copy-start.6 = (bf16[6,256,256]{2,1,0:T(8,128)(2,1)S(1)}, bf16[6,256,256]{2,1,0:T(8,128)(2,1)}, u32[]{:S(2)}) copy-start(bf16[6,256,256]{2,1,0:T(8,128)(2,1)} %get-tuple-element.41.refs_9_.refs_6_.refs_11_) | copy-start | bytes 2359300
  131.9 10.5 %copy-start.11 = (bf16[6,64,128]{2,1,0:T(8,128)(2,1)S(1)}, bf16[6,64,128]{2,1,0:T(8,128)(2,1)}, u32[]{:S(2)}) copy-start(bf16[6,64,128]{2,1,0:T(8,128)(2,1)} %get-tuple-element.38.refs_5_) | copy-start | bytes 294916
  131.9 10.5 %copy-start.12 = (bf16[6,64,96]{2,1,0:T(8,128)(2,1)S(1)}, bf16[6,64,96]{2,1,0:T(8,128)(2,1)}, u32[]{:S(2)}) copy-start(bf16[6,64,96]{2,1,0:T(8,128)(2,1)} %get-tuple-element.42.refs_10_.refs_7_.refs_12_) | copy-start | bytes 221188
  157.9 10.6 %collective-permute-start.21 = (f32[30,32,128]{2,1,0:T(8,128)S(1)}, f32[30,32,128]{2,1,0:T(8,128)S(1)}, u32[]{:S(2)}, u32[]{:S(2)}) collective-permute-start(f32[30,32,128]{2,1,0:T(8,128)S(1)} %bitcast.55), channel_id=1, source_target_pairs={{0,4},{4,0},{8,12},{12,8},{16,20},{20,16},{24,28},{28,24},{1,5},{5... | collective-permute-start | bytes 1474568 | tf_op jit(solution)/shard_map/ppermute | solution.py:28
  158.0 15.1 %collective-permute-start.20 = (f32[30,32,128]{2,1,0:T(8,128)S(1)}, f32[30,32,128]{2,1,0:T(8,128)S(1)}, u32[]{:S(2)}, u32[]{:S(2)}) collective-permute-start(f32[30,32,128]{2,1,0:T(8,128)S(1)} %bitcast.53), channel_id=1, source_target_pairs={{4,8},{8,4},{12,16},{16,12},{20,24},{24,20},{5,9},{9,5},{13,17},{1... | collective-permute-start | bytes 1474568 | tf_op jit(solution)/shard_map/ppermute | solution.py:29
  164.8 12.5 %collective-permute-start.19 = (f32[30,32,128]{2,1,0:T(8,128)S(1)}, f32[30,32,128]{2,1,0:T(8,128)S(1)}, u32[]{:S(2)}, u32[]{:S(2)}) collective-permute-start(f32[30,32,128]{2,1,0:T(8,128)S(1)} %bitcast.52), channel_id=1, source_target_pairs={{0,4},{4,0},{8,12},{12,8},{16,20},{20,16},{24,28},{28,24},{1,5},{5... | collective-permute-start | bytes 1474568 | tf_op jit(solution)/shard_map/ppermute | solution.py:28
  164.9 18.4 %collective-permute-start.18 = (f32[30,32,128]{2,1,0:T(8,128)S(1)}, f32[30,32,128]{2,1,0:T(8,128)S(1)}, u32[]{:S(2)}, u32[]{:S(2)}) collective-permute-start(f32[30,32,128]{2,1,0:T(8,128)S(1)} %bitcast.50), channel_id=1, source_target_pairs={{4,8},{8,4},{12,16},{16,12},{20,24},{24,20},{5,9},{9,5},{13,17},{1... | collective-permute-start | bytes 1474568 | tf_op jit(solution)/shard_map/ppermute | solution.py:29
  173.4 10.0 %collective-permute-start.22 = (f32[48,16,128]{2,1,0:T(8,128)S(1)}, f32[48,16,128]{2,1,0:T(8,128)S(1)}, u32[]{:S(2)}, u32[]{:S(2)}) collective-permute-start(f32[48,16,128]{2,1,0:T(8,128)S(1)} %get-tuple-element.91), channel_id=1, source_target_pairs={{1,2},{2,1},{5,6},{6,5},{9,10},{10,9},{13,14},{14,13},{17,18},{18,... | collective-permute-start | bytes 1179656 | tf_op jit(solution)/shard_map/ppermute | solution.py:29
  174.1 9.3 %collective-permute-start.23 = (f32[48,16,128]{2,1,0:T(8,128)S(1)}, f32[48,16,128]{2,1,0:T(8,128)S(1)}, u32[]{:S(2)}, u32[]{:S(2)}) collective-permute-start(f32[48,16,128]{2,1,0:T(8,128)S(1)} %get-tuple-element.92), channel_id=1, source_target_pairs={{0,1},{1,0},{2,3},{3,2},{4,5},{5,4},{6,7},{7,6},{8,9},{9,8},{10,11... | collective-permute-start | bytes 1179656 | tf_op jit(solution)/shard_map/ppermute | solution.py:28
